TPU v7x, 32 devices: a whole 2x2x4 slice. The times are simulated.
32 devices in a mesh: lat: 8 (over y, x, core), lon: 4 (over z).
Axes of the slice: x: 2, y: 2, z: 4, core: 2. Of those that a mesh axis runs over, the one named last changes fastest.
Arguments:
- latent: bfloat16 [16, 5760, 256], P('lon', 'lat'), may hold values from -6 to 6
- psi_one: bfloat16 [16, 9, 5, 5], P('lon'), may hold values from -4 to 4
- psi_two: bfloat16 [16, 9, 5, 5], P('lon'), may hold values from -4 to 4
- cycle_one: float32 [16, 9, 2, 4], P('lon'), may hold values from -4 to 4
- cycle_two: float32 [16, 9, 2, 4], P('lon'), may hold values from -4 to 4
- w_one: bfloat16 [2304, 256], replicated, may hold values from -0.125 to 0.125
- w_two: bfloat16 [2304, 256], replicated, may hold values from -0.125 to 0.125
- b_one: float32 [256], replicated, may hold values from -3 to 3
- b_two: float32 [256], replicated, may hold values from -3 to 3
- lon_start: int32 [16], replicated, may hold values from -2 to 0, as said below
- lon_width: int32 [16], replicated, may hold values from 1 to 5
- polar_counts: int32 [2], replicated, may hold values from 1 to 4, as said below
Outputs:
- result: bfloat16 [16, 5760, 256], P('lon', 'lat')
Inputs may be any that keep to these rules, and one draw needn't show every extreme that they name: lon_start[i] + lon_width[i] - 1 <= 2 in every row. `polar_counts`: at least one of the two counts is exactly 4.
All inputs are finite; a program needn't handle non-finite values.
Results may differ from a plain program's by a relative error of at most 0.005.
Values may be sent and summed in bfloat16 or wider, within the bound.
No kernel may reach another device: no remote copies, remote signals or barrier semaphores. Data moves between devices by JAX's collectives and lax.ppermute only.
A program may use at most 256 MiB of HBM per device.

v0:
```python
import math

import jax
import jax.numpy as jnp
from jax import lax
from jax.sharding import PartitionSpec as P


def with_halo(block, sides, width, periodic):
    for axis, dim in sides:
        count = lax.axis_size(axis)
        forward = [(i, i + 1) for i in range(count - 1)]
        if periodic:
            forward.append((count - 1, 0))
        backward = [(target, source) for source, target in forward]
        low = lax.ppermute(
            lax.slice_in_dim(block, block.shape[dim] - width, None, axis=dim), axis, forward
        )
        high = lax.ppermute(lax.slice_in_dim(block, 0, width, axis=dim), axis, backward)
        block = jnp.concatenate([low, block, high], axis=dim)
    return block


def cycle_tables(columns, cycle_length, count):
    orders = jnp.arange(count, dtype=jnp.int32)
    phase_index = columns[:, None] % cycle_length * orders[None, :] % cycle_length
    angles = phase_index.astype(jnp.float32) * jnp.float32(2.0 * math.pi / cycle_length)
    return (jnp.cos(angles), jnp.sin(angles))


def tap_weights(psi, lon_start, lon_width):
    offsets = jnp.arange(5, dtype=jnp.int32)
    shifted = lon_start[:, None, None] + offsets[None, :, None]
    target = offsets[None, None, :] - 2
    select = ((shifted == target) & (offsets[None, :, None] < lon_width[:, None, None])).astype(
        jnp.float32
    )
    mixed_taps = jnp.einsum(
        "ikrq,iqd->ikrd", psi.astype(jnp.float32), select, precision=lax.Precision.HIGHEST
    )
    return mixed_taps.astype(jnp.bfloat16).reshape(psi.shape[0], psi.shape[1], 25)


def partial_harmonics(source, first_col, cycle_length, count):
    columns = first_col + jnp.arange(source.shape[1], dtype=jnp.int32)
    cos_full, sin_full = cycle_tables(columns, cycle_length, count)
    cos_part = jnp.einsum(
        "jm,ijc->imc", cos_full.astype(jnp.bfloat16), source, preferred_element_type=jnp.float32
    )
    sin_part = jnp.einsum(
        "jm,ijc->imc", sin_full.astype(jnp.bfloat16), source, preferred_element_type=jnp.float32
    )
    return (cos_part, sin_part)


def cycle_harmonics(source, first_col, cycle_length, count):
    norm_factor = cycle_length ** (-0.5)
    cos_local, sin_local = partial_harmonics(source, first_col, cycle_length, count)
    cos_part, sin_part = lax.psum((cos_local, sin_local), "lat")
    return (cos_part * norm_factor, sin_part * norm_factor)


def convolve(
    padded,
    tap_rows,
    coef_rows,
    polar_mask,
    cos_part,
    sin_part,
    cos_full,
    sin_full,
    kernel,
    bias_row,
):
    col_count = cos_full.shape[0]
    row_count = tap_rows.shape[0]
    basis_count = tap_rows.shape[1]
    channels = padded.shape[2]
    kernel_cube = kernel.reshape(basis_count, channels, kernel.shape[1])
    tap_cube = tap_rows.reshape(row_count, basis_count, 5, 5)
    col_shifted = jnp.stack([padded[:, d : d + col_count] for d in range(5)], axis=1)
    outputs = []
    for row in range(row_count):
        window = col_shifted[row : row + 5]
        near_sum = jnp.einsum(
            "krd,rdjc->kjc", tap_cube[row], window, preferred_element_type=jnp.float32
        )
        coef_row = coef_rows[row]
        cycle_term = jnp.einsum(
            "kmc,jm->kjc",
            coef_row[:, 0, :, None] * cos_part[row][None],
            cos_full,
            precision=lax.Precision.HIGHEST,
        )
        cycle_term = cycle_term + jnp.einsum(
            "kmc,jm->kjc",
            coef_row[:, 1, :, None] * sin_part[row][None],
            sin_full,
            precision=lax.Precision.HIGHEST,
        )
        feature = (near_sum + polar_mask[row] * cycle_term).astype(jnp.bfloat16)
        outputs.append(
            jnp.einsum("kjc,kco->jo", feature, kernel_cube, preferred_element_type=jnp.float32)
        )
    return jnp.stack(outputs) + bias_row


def with_margins(source):
    banded = with_halo(source, (("lon", 0),), 2, False)
    return with_halo(banded, (("lat", 1),), 2, True)


def body(
    latent,
    psi_one,
    psi_two,
    cycle_one,
    cycle_two,
    w_one,
    w_two,
    b_one,
    b_two,
    lon_start,
    lon_width,
    polar_counts,
):
    row_count, col_count, channels = latent.shape
    harm_count = cycle_one.shape[3]
    lat_total = row_count * lax.axis_size("lon")
    cycle_length = col_count * lax.axis_size("lat")
    first_row = lax.axis_index("lon") * row_count
    first_col = lax.axis_index("lat") * col_count
    own_start = lax.dynamic_slice_in_dim(lon_start, first_row, row_count, 0)
    own_width = lax.dynamic_slice_in_dim(lon_width, first_row, row_count, 0)
    taps_one = tap_weights(psi_one, own_start, own_width)
    taps_two = tap_weights(psi_two, own_start, own_width)

    def polar_of(row_global):
        return (
            (row_global < polar_counts[0]) | (row_global >= lat_total - polar_counts[1])
        ).astype(jnp.float32)

    own_rows = first_row + jnp.arange(row_count, dtype=jnp.int32)
    cos_own, sin_own = cycle_tables(
        first_col + jnp.arange(col_count, dtype=jnp.int32), cycle_length, harm_count
    )
    cos_part, sin_part = cycle_harmonics(latent, first_col, cycle_length, harm_count)
    before = convolve(
        with_margins(latent),
        taps_one,
        cycle_one,
        polar_of(own_rows),
        cos_part,
        sin_part,
        cos_own,
        sin_own,
        w_one,
        b_one,
    )
    hidden = jax.nn.gelu(before, approximate=False).astype(jnp.bfloat16)
    cos_two, sin_two = cycle_harmonics(hidden, first_col, cycle_length, harm_count)
    result = convolve(
        with_margins(hidden),
        taps_two,
        cycle_two,
        polar_of(own_rows),
        cos_two,
        sin_two,
        cos_own,
        sin_own,
        w_two,
        b_two,
    )
    return result.astype(jnp.bfloat16)


def solution(mesh):
    return jax.shard_map(
        body,
        mesh=mesh,
        in_specs=(
            P("lon", "lat", None),
            P("lon", None, None, None),
            P("lon", None, None, None),
            P("lon", None, None, None),
            P("lon", None, None, None),
            P(),
            P(),
            P(),
            P(),
            P(),
            P(),
            P(),
        ),
        out_specs=P("lon", "lat", None),
        check_vma=False,
    )
```

profile of v0, /device:TPU:0, one launch (start us, length us, event | category | flops | bytes accessed | tf_op | source)
XLA Modules:
  0.0 454.6 jit_solution(13699464949958126120)
XLA Ops:
  0.0 2.4 fusion.282
  2.4 5.8 %collective-permute-start = (bf16[2,720,256]{2,1,0:T(8,128)(2,1)}, bf16[2,720,256]{2,1,0:T(8,128)(2,1)}, u32[]{:S(2)}, u32[]{:S(2)}) collective-permute-start(bf16[2,720,256]{2,1,0:T(8,128)(2,1)} %get-tuple-element.26), channel_id=1, source_target_pairs={{0,1},{1,2},{2,3},{4,5},{5,6},{6,7},{8,9},{9,10},{10,11},{12,13},{... | collective-permute-start | bytes 2211848 | tf_op jit(solution)/shard_map/ppermute | solution.py:16
  9.5 1.7 convolution_bitcast_fusion.3
  11.3 1.7 convolution_bitcast_fusion.2
  13.3 23.8 %all-reduce.1 = (f32[4,4,256]{2,1,0:T(4,128)S(1)}, f32[4,4,256]{2,1,0:T(4,128)S(1)}) all-reduce(f32[4,4,256]{2,1,0:T(4,128)S(1)} %convolution_bitcast_fusion.3, f32[4,4,256]{2,1,0:T(4,128)S(1)} %convolution_bitcast_fusion.2), channel_id=1, replica_groups=mesh['lat'=8,'lon'=4] {'lat'}, use_global_device_ids=true, to_apply=%region_0.1 | all-reduce | flops 8192 | bytes 65536 | tf_op jit(solution)/shard_map/psum | solution.py:59
  37.8 7.6 %fusion.111 = f32[720,9,256]{2,0,1:T(8,128)} fusion(f32[4,256]{1,0:T(4,128)S(1)} %get-tuple-element.48, f32[9,4]{1,0:T(8,128)S(1)} %copy.21, s32[720]{0:T(1024)S(1)} %add_select_fusion.1), kind=kOutput, calls=%fused_computation.127 | convolution fusion | flops 79661376 | bytes 6642640 | tf_op jit(solution)/shard_map/kmc,jm->kjc/dot_general | solution.py:89
  45.4 7.5 %fusion.109 = f32[720,9,256]{2,0,1:T(8,128)} fusion(f32[4,256]{1,0:T(4,128)S(1)} %get-tuple-element.40, f32[9,4]{1,0:T(8,128)S(1)} %copy.22, s32[720]{0:T(1024)S(1)} %add_select_fusion.1), kind=kOutput, calls=%fused_computation.125 | convolution fusion | flops 79661376 | bytes 6642640 | tf_op jit(solution)/shard_map/kmc,jm->kjc/dot_general | solution.py:95
  52.9 7.6 %fusion.115 = f32[720,9,256]{2,0,1:T(8,128)} fusion(f32[4,256]{1,0:T(4,128)S(1)} %get-tuple-element.49, f32[9,4]{1,0:T(8,128)S(1)} %copy.19, s32[720]{0:T(1024)S(1)} %add_select_fusion.1), kind=kOutput, calls=%fused_computation.131 | convolution fusion | flops 79661376 | bytes 6642640 | tf_op jit(solution)/shard_map/kmc,jm->kjc/dot_general | solution.py:89
  60.6 7.6 %fusion.113 = f32[720,9,256]{2,0,1:T(8,128)} fusion(f32[4,256]{1,0:T(4,128)S(1)} %get-tuple-element.41, f32[9,4]{1,0:T(8,128)S(1)} %copy.20, s32[720]{0:T(1024)S(1)} %add_select_fusion.1), kind=kOutput, calls=%fused_computation.129 | convolution fusion | flops 79661376 | bytes 6642640 | tf_op jit(solution)/shard_map/kmc,jm->kjc/dot_general | solution.py:95
  68.1 7.6 %fusion.119 = f32[720,9,256]{2,0,1:T(8,128)} fusion(f32[4,256]{1,0:T(4,128)S(1)} %get-tuple-element.50, f32[9,4]{1,0:T(8,128)S(1)} %copy.17, s32[720]{0:T(1024)S(1)} %add_select_fusion.1), kind=kOutput, calls=%fused_computation.135 | convolution fusion | flops 79661376 | bytes 6642640 | tf_op jit(solution)/shard_map/kmc,jm->kjc/dot_general | solution.py:89
  75.7 7.8 %fusion.117 = f32[720,9,256]{2,0,1:T(8,128)} fusion(f32[4,256]{1,0:T(4,128)S(1)} %get-tuple-element.42, f32[9,4]{1,0:T(8,128)S(1)} %copy.18, s32[720]{0:T(1024)S(1)} %add_select_fusion.1), kind=kOutput, calls=%fused_computation.133 | convolution fusion | flops 79661376 | bytes 6642640 | tf_op jit(solution)/shard_map/kmc,jm->kjc/dot_general | solution.py:95
  83.6 7.6 %fusion.123 = f32[720,9,256]{2,0,1:T(8,128)} fusion(f32[4,256]{1,0:T(4,128)S(1)} %get-tuple-element.47, f32[9,4]{1,0:T(8,128)S(1)} %copy.15, s32[720]{0:T(1024)S(1)} %add_select_fusion.1), kind=kOutput, calls=%fused_computation.139 | convolution fusion | flops 79661376 | bytes 6642640 | tf_op jit(solution)/shard_map/kmc,jm->kjc/dot_general | solution.py:89
  94.6 7.6 %fusion.121 = f32[720,9,256]{2,0,1:T(8,128)} fusion(f32[4,256]{1,0:T(4,128)S(1)} %get-tuple-element.39, f32[9,4]{1,0:T(8,128)S(1)} %copy.16, s32[720]{0:T(1024)S(1)} %add_select_fusion.1), kind=kOutput, calls=%fused_computation.137 | convolution fusion | flops 79661376 | bytes 6642640 | tf_op jit(solution)/shard_map/kmc,jm->kjc/dot_general | solution.py:95
  104.6 1.6 copy-done.2
  107.7 2.6 collective-permute-start.3
  110.3 2.5 fusion.45
  115.2 22.8 %fusion.278 = (bf16[5,5,720,256]{3,2,0,1:T(8,128)(2,1)}, bf16[5,5,720,256]{3,2,0,1:T(8,128)(2,1)}, bf16[5,5,720,256]{3,2,0,1:T(8,128)(2,1)}, bf16[5,5,720,256]{3,2,0,1:T(8,128)(2,1)}) fusion(bf16[8,5,720,256]{3,2,0,1:T(8,128)(2,1)S(1)} %fusion.54), kind=kLoop, calls=%fused_computation.338 | loop fusion | bytes 73728000 | tf_op jit(solution)/shard_map/slice | solution.py:84
  138.0 14.1 %fusion.8 = f32[9,720,256,1]{2,0,3,1:T(8,128)} fusion(bf16[5,5,720,256]{3,2,0,1:T(8,128)(2,1)} %get-tuple-element.14, bf16[4,9,5,5]{1,3,2,0:T(8,128)(2,1)S(1)} %fusion.90), kind=kOutput, calls=%fused_computation.8 | convolution fusion | flops 82944000 | bytes 15861760 | tf_op jit(solution)/shard_map/krd,rdjc->kjc/dot_general | solution.py:85
  152.1 14.1 %fusion.10 = f32[9,720,256,1]{2,0,3,1:T(8,128)} fusion(bf16[5,5,720,256]{3,2,0,1:T(8,128)(2,1)} %get-tuple-element.15, bf16[4,9,5,5]{1,3,2,0:T(8,128)(2,1)S(1)} %fusion.90), kind=kOutput, calls=%fused_computation.10 | convolution fusion | flops 82944000 | bytes 15861760 | tf_op jit(solution)/shard_map/krd,rdjc->kjc/dot_general | solution.py:85
  166.3 10.9 %fusion.12 = f32[9,720,256,1]{2,0,3,1:T(8,128)} fusion(bf16[5,5,720,256]{3,2,0,1:T(8,128)(2,1)S(1)} %bitcast.360, bf16[4,9,5,5]{1,3,2,0:T(8,128)(2,1)S(1)} %fusion.90), kind=kOutput, calls=%fused_computation.12 | convolution fusion | flops 82944000 | bytes 15861760 | tf_op jit(solution)/shard_map/krd,rdjc->kjc/dot_general | solution.py:85
  177.2 11.1 %fusion.14 = f32[9,720,256,1]{2,0,3,1:T(8,128)} fusion(bf16[5,5,720,256]{3,2,0,1:T(8,128)(2,1)S(1)} %bitcast.356, bf16[4,9,5,5]{1,3,2,0:T(8,128)(2,1)S(1)} %fusion.90), kind=kOutput, calls=%fused_computation.14 | convolution fusion | flops 82944000 | bytes 15861760 | tf_op jit(solution)/shard_map/krd,rdjc->kjc/dot_general | solution.py:85
  188.4 13.2 %fusion.77 = f32[1,720,256]{2,1,0:T(8,128)S(1)} fusion(bf16[9,256,256]{2,1,0:T(8,128)(2,1)S(1)} %bitcast.354, f32[9,720,256,1]{2,0,3,1:T(8,128)} %fusion.8, f32[720,9,256]{2,0,1:T(8,128)} %fusion.111, f32[720,9,256]{2,0,1:T(8,128)} %fusion.109, f32[]{:T(128)} %bitcast.60), kind=kOutput, calls=%fused_computation.95 | convolution fusion | flops 855982080 | bytes 21823492 | tf_op jit(solution)/shard_map/kjc,kco->jo/dot_general | solution.py:103
  201.6 14.2 %fusion.80 = f32[1,720,256]{2,1,0:T(8,128)} fusion(bf16[9,256,256]{2,1,0:T(8,128)(2,1)S(1)} %bitcast.353, f32[9,720,256,1]{2,0,3,1:T(8,128)} %fusion.10, f32[720,9,256]{2,0,1:T(8,128)} %fusion.115, f32[720,9,256]{2,0,1:T(8,128)} %fusion.113, f32[]{:T(128)} %bitcast.48), kind=kOutput, calls=%fused_computation.96 | convolution fusion | flops 855982080 | bytes 21823492 | tf_op jit(solution)/shard_map/kjc,kco->jo/dot_general | solution.py:103
  215.9 11.0 %fusion.83 = f32[1,720,256]{2,1,0:T(8,128)} fusion(bf16[9,256,256]{2,1,0:T(8,128)(2,1)S(1)} %bitcast.352, f32[9,720,256,1]{2,0,3,1:T(8,128)S(1)} %bitcast.370, f32[720,9,256]{2,0,1:T(8,128)} %fusion.119, f32[720,9,256]{2,0,1:T(8,128)} %fusion.117, f32[]{:T(128)} %bitcast.36), kind=kOutput, calls=%fused_computation.97 | convolution fusion | flops 855982080 | bytes 21823492 | tf_op jit(solution)/shard_map/kjc,kco->jo/dot_general | solution.py:103
  226.9 9.5 %fusion.86 = f32[1,720,256]{2,1,0:T(8,128)S(1)} fusion(bf16[9,256,256]{2,1,0:T(8,128)(2,1)S(1)} %bitcast.351, f32[9,720,256,1]{2,0,3,1:T(8,128)S(1)} %bitcast.368, f32[720,9,256]{2,0,1:T(8,128)} %fusion.123, f32[720,9,256]{2,0,1:T(8,128)} %fusion.121, f32[]{:T(128)} %bitcast.17), kind=kOutput, calls=%fused_computation.98 | convolution fusion | flops 855982080 | bytes 21823492 | tf_op jit(solution)/shard_map/kjc,kco->jo/dot_general | solution.py:103
  236.5 6.6 %fusion.48 = bf16[4,720,256]{2,1,0:T(8,128)(2,1)S(1)} fusion(f32[1,720,256]{2,1,0:T(8,128)S(1)} %fusion.77, f32[1,720,256]{2,1,0:T(8,128)S(1)} %copy-done.7, f32[1,720,256]{2,1,0:T(8,128)S(1)} %copy-done.9, f32[1,720,256]{2,1,0:T(8,128)S(1)} %fusion.86, f32[256]{0:T(256)S(1)} %copy-done.18), kind=kLoop, calls=%fused_computation.55 | loop fusion | flops 50872320 | bytes 4424704 | tf_op jit(solution)/shard_map/convert_element_type | solution.py:160
  245.0 1.3 collective-permute-start.5
  246.3 4.9 %collective-permute-start.4 = (bf16[2,720,256]{2,1,0:T(8,128)(2,1)}, bf16[2,720,256]{2,1,0:T(8,128)(2,1)S(1)}, u32[]{:S(2)}, u32[]{:S(2)}) collective-permute-start(bf16[2,720,256]{2,1,0:T(8,128)(2,1)} %get-tuple-element.23), channel_id=1, source_target_pairs={{0,1},{1,2},{2,3},{4,5},{5,6},{6,7},{8,9},{9,10},{10,11},{12,13},{... | collective-permute-start | bytes 2211848 | tf_op jit(solution)/shard_map/ppermute | solution.py:16
  251.3 22.8 %all-reduce = (f32[4,4,256]{2,1,0:T(4,128)S(1)}, f32[4,4,256]{2,1,0:T(4,128)S(1)}) all-reduce(f32[4,4,256]{2,1,0:T(4,128)S(1)} %convolution_bitcast_fusion.1, f32[4,4,256]{2,1,0:T(4,128)S(1)} %convolution_bitcast_fusion), channel_id=1, replica_groups=mesh['lat'=8,'lon'=4] {'lat'}, use_global_device_ids=true, to_apply=%region_2.3 | all-reduce | flops 8192 | bytes 65536 | tf_op jit(solution)/shard_map/psum | solution.py:59
  274.1 7.6 %fusion.95 = f32[720,9,256]{2,0,1:T(8,128)} fusion(f32[4,256]{1,0:T(4,128)S(1)} %get-tuple-element.36, f32[9,4]{1,0:T(8,128)S(1)} %copy.29, s32[720]{0:T(1024)S(1)} %add_select_fusion.1), kind=kOutput, calls=%fused_computation.111 | convolution fusion | flops 79661376 | bytes 6642640 | tf_op jit(solution)/shard_map/kmc,jm->kjc/dot_general | solution.py:89
  281.7 7.5 %fusion.93 = f32[720,9,256]{2,0,1:T(8,128)} fusion(f32[4,256]{1,0:T(4,128)S(1)} %get-tuple-element.28, f32[9,4]{1,0:T(8,128)S(1)} %copy.30, s32[720]{0:T(1024)S(1)} %add_select_fusion.1), kind=kOutput, calls=%fused_computation.109 | convolution fusion | flops 79661376 | bytes 6642640 | tf_op jit(solution)/shard_map/kmc,jm->kjc/dot_general | solution.py:95
  289.2 7.6 %fusion.99 = f32[720,9,256]{2,0,1:T(8,128)} fusion(f32[4,256]{1,0:T(4,128)S(1)} %get-tuple-element.37, f32[9,4]{1,0:T(8,128)S(1)} %copy.27, s32[720]{0:T(1024)S(1)} %add_select_fusion.1), kind=kOutput, calls=%fused_computation.115 | convolution fusion | flops 79661376 | bytes 6642640 | tf_op jit(solution)/shard_map/kmc,jm->kjc/dot_general | solution.py:89
  296.8 7.5 %fusion.97 = f32[720,9,256]{2,0,1:T(8,128)} fusion(f32[4,256]{1,0:T(4,128)S(1)} %get-tuple-element.29, f32[9,4]{1,0:T(8,128)S(1)} %copy.28, s32[720]{0:T(1024)S(1)} %add_select_fusion.1), kind=kOutput, calls=%fused_computation.113 | convolution fusion | flops 79661376 | bytes 6642640 | tf_op jit(solution)/shard_map/kmc,jm->kjc/dot_general | solution.py:95
  304.3 7.5 %fusion.103 = f32[720,9,256]{2,0,1:T(8,128)} fusion(f32[4,256]{1,0:T(4,128)S(1)} %get-tuple-element.38, f32[9,4]{1,0:T(8,128)S(1)} %copy.25, s32[720]{0:T(1024)S(1)} %add_select_fusion.1), kind=kOutput, calls=%fused_computation.119 | convolution fusion | flops 79661376 | bytes 6642640 | tf_op jit(solution)/shard_map/kmc,jm->kjc/dot_general | solution.py:89
  311.9 8.0 %fusion.101 = f32[720,9,256]{2,0,1:T(8,128)} fusion(f32[4,256]{1,0:T(4,128)S(1)} %get-tuple-element.30, f32[9,4]{1,0:T(8,128)S(1)} %copy.26, s32[720]{0:T(1024)S(1)} %add_select_fusion.1), kind=kOutput, calls=%fused_computation.117 | convolution fusion | flops 79661376 | bytes 6642640 | tf_op jit(solution)/shard_map/kmc,jm->kjc/dot_general | solution.py:95
  319.9 7.6 %fusion.107 = f32[720,9,256]{2,0,1:T(8,128)} fusion(f32[4,256]{1,0:T(4,128)S(1)} %get-tuple-element.35, f32[9,4]{1,0:T(8,128)S(1)} %copy.23, s32[720]{0:T(1024)S(1)} %add_select_fusion.1), kind=kOutput, calls=%fused_computation.123 | convolution fusion | flops 79661376 | bytes 6642640 | tf_op jit(solution)/shard_map/kmc,jm->kjc/dot_general | solution.py:89
  328.4 7.6 %fusion.105 = f32[720,9,256]{2,0,1:T(8,128)} fusion(f32[4,256]{1,0:T(4,128)S(1)} %get-tuple-element.27, f32[9,4]{1,0:T(8,128)S(1)} %copy.24, s32[720]{0:T(1024)S(1)} %add_select_fusion.1), kind=kOutput, calls=%fused_computation.121 | convolution fusion | flops 79661376 | bytes 6642640 | tf_op jit(solution)/shard_map/kmc,jm->kjc/dot_general | solution.py:95
  336.0 3.1 pad_maximum_fusion
  341.8 12.2 %fusion.277 = (bf16[5,5,720,256]{3,2,0,1:T(8,128)(2,1)}, bf16[5,5,720,256]{3,2,0,1:T(8,128)(2,1)}, bf16[5,5,720,256]{3,2,0,1:T(8,128)(2,1)}, bf16[5,5,720,256]{3,2,0,1:T(8,128)(2,1)}) fusion(bf16[8,5,720,256]{3,2,0,1:T(8,128)(2,1)S(1)} %fusion.49), kind=kLoop, calls=%fused_computation.337 | loop fusion | bytes 73728000 | tf_op jit(solution)/shard_map/slice | solution.py:84
  354.0 14.1 %fusion = f32[9,720,256,1]{2,0,3,1:T(8,128)} fusion(bf16[5,5,720,256]{3,2,0,1:T(8,128)(2,1)} %get-tuple-element.10, bf16[4,9,5,5]{1,3,2,0:T(8,128)(2,1)S(1)} %fusion.89), kind=kOutput, calls=%fused_computation | convolution fusion | flops 82944000 | bytes 15861760 | tf_op jit(solution)/shard_map/krd,rdjc->kjc/dot_general | solution.py:85
  368.1 14.3 %fusion.2 = f32[9,720,256,1]{2,0,3,1:T(8,128)} fusion(bf16[5,5,720,256]{3,2,0,1:T(8,128)(2,1)} %get-tuple-element.11, bf16[4,9,5,5]{1,3,2,0:T(8,128)(2,1)S(1)} %fusion.89), kind=kOutput, calls=%fused_computation.2 | convolution fusion | flops 82944000 | bytes 15861760 | tf_op jit(solution)/shard_map/krd,rdjc->kjc/dot_general | solution.py:85
  382.4 10.9 %fusion.4 = f32[9,720,256,1]{2,0,3,1:T(8,128)} fusion(bf16[5,5,720,256]{3,2,0,1:T(8,128)(2,1)S(1)} %bitcast.362, bf16[4,9,5,5]{1,3,2,0:T(8,128)(2,1)S(1)} %fusion.89), kind=kOutput, calls=%fused_computation.4 | convolution fusion | flops 82944000 | bytes 15861760 | tf_op jit(solution)/shard_map/krd,rdjc->kjc/dot_general | solution.py:85
  393.3 11.2 %fusion.6 = f32[9,720,256,1]{2,0,3,1:T(8,128)} fusion(bf16[5,5,720,256]{3,2,0,1:T(8,128)(2,1)S(1)} %bitcast.358, bf16[4,9,5,5]{1,3,2,0:T(8,128)(2,1)S(1)} %fusion.89), kind=kOutput, calls=%fused_computation.6 | convolution fusion | flops 82944000 | bytes 15861760 | tf_op jit(solution)/shard_map/krd,rdjc->kjc/dot_general | solution.py:85
  404.5 13.2 %fusion.65 = f32[1,720,256]{2,1,0:T(8,128)S(1)} fusion(bf16[9,256,256]{2,1,0:T(8,128)(2,1)S(1)} %bitcast.372, f32[9,720,256,1]{2,0,3,1:T(8,128)} %fusion, f32[720,9,256]{2,0,1:T(8,128)} %fusion.95, f32[720,9,256]{2,0,1:T(8,128)} %fusion.93, f32[]{:T(128)} %bitcast.60), kind=kOutput, calls=%fused_computation.91 | convolution fusion | flops 855982080 | bytes 21823492 | tf_op jit(solution)/shard_map/kjc,kco->jo/dot_general | solution.py:103
  417.8 14.2 %fusion.68 = f32[1,720,256]{2,1,0:T(8,128)} fusion(bf16[9,256,256]{2,1,0:T(8,128)(2,1)S(1)} %bitcast.373, f32[9,720,256,1]{2,0,3,1:T(8,128)} %fusion.2, f32[720,9,256]{2,0,1:T(8,128)} %fusion.99, f32[720,9,256]{2,0,1:T(8,128)} %fusion.97, f32[]{:T(128)} %bitcast.48), kind=kOutput, calls=%fused_computation.92 | convolution fusion | flops 855982080 | bytes 21823492 | tf_op jit(solution)/shard_map/kjc,kco->jo/dot_general | solution.py:103
  432.0 10.8 %fusion.71 = f32[1,720,256]{2,1,0:T(8,128)} fusion(bf16[9,256,256]{2,1,0:T(8,128)(2,1)S(1)} %bitcast.374, f32[9,720,256,1]{2,0,3,1:T(8,128)S(1)} %bitcast.366, f32[720,9,256]{2,0,1:T(8,128)} %fusion.103, f32[720,9,256]{2,0,1:T(8,128)} %fusion.101, f32[]{:T(128)} %bitcast.36), kind=kOutput, calls=%fused_computation.93 | convolution fusion | flops 855982080 | bytes 21823492 | tf_op jit(solution)/shard_map/kjc,kco->jo/dot_general | solution.py:103
  442.9 9.9 %fusion.74 = f32[1,720,256]{2,1,0:T(8,128)S(1)} fusion(bf16[9,256,256]{2,1,0:T(8,128)(2,1)} %bitcast.371, f32[9,720,256,1]{2,0,3,1:T(8,128)S(1)} %bitcast.364, f32[720,9,256]{2,0,1:T(8,128)} %fusion.107, f32[720,9,256]{2,0,1:T(8,128)} %fusion.105, f32[]{:T(128)} %bitcast.17), kind=kOutput, calls=%fused_computation.94 | convolution fusion | flops 855982080 | bytes 21823492 | tf_op jit(solution)/shard_map/kjc,kco->jo/dot_general | solution.py:103
  452.9 1.4 fusion.57
  (169 shorter events, 17.1 us)
Async XLA Ops:
  0.0 188.3 %copy-start = (bf16[2304,256]{1,0:T(8,128)(2,1)S(1)}, bf16[2304,256]{1,0:T(8,128)(2,1)}, u32[]{:S(2)}) copy-start(bf16[2304,256]{1,0:T(8,128)(2,1)} %param.17) | copy-start | bytes 3538948
  0.0 13.0 %copy-start.20 = (s32[16]{0:T(128)S(1)}, s32[16]{0:T(128)}, u32[]{:S(2)}) copy-start(s32[16]{0:T(128)} %param.21) | copy-start | bytes 196
  0.0 13.2 %copy-start.21 = (s32[16]{0:T(128)S(1)}, s32[16]{0:T(128)}, u32[]{:S(2)}) copy-start(s32[16]{0:T(128)} %param.22) | copy-start | bytes 196
  0.0 37.1 %copy-start.12 = (f32[4,9,2,4]{1,3,2,0:T(4,128)S(1)}, f32[4,9,2,4]{1,3,2,0:T(4,128)}, u32[]{:S(2)}) copy-start(f32[4,9,2,4]{1,3,2,0:T(4,128)} %param.15) | copy-start | bytes 3460
  0.0 37.8 %copy-start.13 = (f32[4,9,2,4]{1,3,2,0:T(4,128)S(1)}, f32[4,9,2,4]{1,3,2,0:T(4,128)}, u32[]{:S(2)}) copy-start(f32[4,9,2,4]{1,3,2,0:T(4,128)} %param.16) | copy-start | bytes 3460
  2.4 99.8 %collective-permute-start = (bf16[2,720,256]{2,1,0:T(8,128)(2,1)}, bf16[2,720,256]{2,1,0:T(8,128)(2,1)}, u32[]{:S(2)}, u32[]{:S(2)}) collective-permute-start(bf16[2,720,256]{2,1,0:T(8,128)(2,1)} %get-tuple-element.26), channel_id=1, source_target_pairs={{0,1},{1,2},{2,3},{4,5},{5,6},{6,7},{8,9},{9,10},{10,11},{12,13},{... | collective-permute-start | bytes 2211848 | tf_op jit(solution)/shard_map/ppermute | solution.py:16
  8.2 95.2 %collective-permute-start.1 = (bf16[2,720,256]{2,1,0:T(8,128)(2,1)S(1)}, bf16[2,720,256]{2,1,0:T(8,128)(2,1)}, u32[]{:S(2)}, u32[]{:S(2)}) collective-permute-start(bf16[2,720,256]{2,1,0:T(8,128)(2,1)S(1)} %get-tuple-element.25), channel_id=1, source_target_pairs={{1,0},{2,1},{3,2},{5,4},{6,5},{7,6},{9,8},{10,9},{11,10},{13,12},{... | collective-permute-start | bytes 2211848 | tf_op jit(solution)/shard_map/ppermute | solution.py:19
  75.7 16.6 %copy-start.10 = (bf16[4,9,5,5]{1,0,3,2:T(4,128)(2,1)S(1)}, bf16[4,9,5,5]{1,0,3,2:T(4,128)(2,1)}, u32[]{:S(2)}) copy-start(bf16[4,9,5,5]{1,0,3,2:T(4,128)(2,1)} %param.13) | copy-start | bytes 5404
  75.7 16.8 %copy-start.17 = (s32[2]{0:T(128)S(1)}, s32[2]{0:T(128)}, u32[]{:S(2)}) copy-start(s32[2]{0:T(128)} %param.23) | copy-start | bytes 28
  75.7 18.0 %copy-start.11 = (bf16[4,9,5,5]{1,0,3,2:T(4,128)(2,1)S(1)}, bf16[4,9,5,5]{1,0,3,2:T(4,128)(2,1)}, u32[]{:S(2)}) copy-start(bf16[4,9,5,5]{1,0,3,2:T(4,128)(2,1)} %param.14) | copy-start | bytes 5404
  83.5 19.8 %copy-start.4 = (bf16[4,720,256]{2,1,0:T(8,128)(2,1)S(1)}, bf16[4,720,256]{2,1,0:T(8,128)(2,1)}, u32[]{:S(2)}) copy-start(bf16[4,720,256]{2,1,0:T(8,128)(2,1)} %param.12) | copy-start | bytes 4423684
  94.6 12.5 %copy-start.15 = (f32[9,4]{0,1:T(4,128)S(1)}, f32[9,4]{0,1:T(4,128)}, u32[]{:S(2)}) copy-start(f32[9,4]{0,1:T(4,128)} %get-tuple-element.57) | copy-start | bytes 436
  94.6 12.7 %copy-start.16 = (f32[9,4]{0,1:T(4,128)S(1)}, f32[9,4]{0,1:T(4,128)}, u32[]{:S(2)}) copy-start(f32[9,4]{0,1:T(4,128)} %get-tuple-element.54) | copy-start | bytes 436
  94.6 12.8 %copy-start.14 = (f32[9,4]{0,1:T(4,128)S(1)}, f32[9,4]{0,1:T(4,128)}, u32[]{:S(2)}) copy-start(f32[9,4]{0,1:T(4,128)} %get-tuple-element.53) | copy-start | bytes 436
  106.2 4.1 collective-permute-start.2
  107.7 6.1 %collective-permute-start.3 = (bf16[8,2,256]{2,1,0:T(2,128)(2,1)S(1)}, bf16[8,2,256]{2,1,0:T(2,128)(2,1)S(1)}, u32[]{:S(2)}, u32[]{:S(2)}) collective-permute-start(bf16[8,2,256]{2,1,0:T(2,128)(2,1)S(1)} %get-tuple-element.21), channel_id=1, source_target_pairs={{4,0},{8,4},{12,8},{16,12},{20,16},{24,20},{28,24},{0,28},{5,1},{9... | collective-permute-start | bytes 24584 | tf_op jit(solution)/shard_map/ppermute | solution.py:19
  138.0 28.3 %slice-start.6 = ((s8[9216000]{0:T(1024)(128)(4,1)}), s8[4194304]{0:T(1024)(128)(4,1)S(1)}, s32[]{:S(2)}) async-start(s8[9216000]{0:T(1024)(128)(4,1)} %bitcast.359), calls=%async_computation.6 | async-start | bytes 8388608
  138.0 28.3 %slice-start.7 = ((s8[9216000]{0:T(1024)(128)(4,1)}), s8[4194304]{0:T(1024)(128)(4,1)S(1)}, s32[]{:S(2)}) async-start(s8[9216000]{0:T(1024)(128)(4,1)} %bitcast.359), calls=%async_computation.7 | async-start | bytes 8388608
  152.1 14.1 %slice-start.8 = ((s8[9216000]{0:T(1024)(128)(4,1)}), s8[827392]{0:T(1024)(128)(4,1)S(1)}, s32[]{:S(2)}) async-start(s8[9216000]{0:T(1024)(128)(4,1)} %bitcast.359), calls=%async_computation.8 | async-start | bytes 1654784
  152.1 25.1 %slice-start = ((s8[9216000]{0:T(1024)(128)(4,1)}), s8[4194304]{0:T(1024)(128)(4,1)S(1)}, s32[]{:S(2)}) async-start(s8[9216000]{0:T(1024)(128)(4,1)} %bitcast.355), calls=%async_computation | async-start | bytes 8388608
  152.1 25.1 %slice-start.1 = ((s8[9216000]{0:T(1024)(128)(4,1)}), s8[4194304]{0:T(1024)(128)(4,1)S(1)}, s32[]{:S(2)}) async-start(s8[9216000]{0:T(1024)(128)(4,1)} %bitcast.355), calls=%async_computation.1 | async-start | bytes 8388608
  166.3 11.0 %slice-start.2 = ((s8[9216000]{0:T(1024)(128)(4,1)}), s8[827392]{0:T(1024)(128)(4,1)S(1)}, s32[]{:S(2)}) async-start(s8[9216000]{0:T(1024)(128)(4,1)} %bitcast.355), calls=%async_computation.2 | async-start | bytes 1654784
  188.4 27.5 %slice-start.21 = ((s8[11796480]{0:T(1024)(128)(4,1)}), s8[4194304]{0:T(1024)(128)(4,1)S(1)}, s32[]{:S(2)}) async-start(s8[11796480]{0:T(1024)(128)(4,1)} %bitcast.369), calls=%async_computation.21 | async-start | bytes 8388608
  188.4 27.5 %slice-start.22 = ((s8[11796480]{0:T(1024)(128)(4,1)}), s8[4194304]{0:T(1024)(128)(4,1)S(1)}, s32[]{:S(2)}) async-start(s8[11796480]{0:T(1024)(128)(4,1)} %bitcast.369), calls=%async_computation.22 | async-start | bytes 8388608
  201.6 14.3 %slice-start.23 = ((s8[11796480]{0:T(1024)(128)(4,1)}), s8[3407872]{0:T(1024)(128)(4,1)S(1)}, s32[]{:S(2)}) async-start(s8[11796480]{0:T(1024)(128)(4,1)} %bitcast.369), calls=%async_computation.23 | async-start | bytes 6815744
  201.6 25.2 %slice-start.18 = ((s8[11796480]{0:T(1024)(128)(4,1)}), s8[4194304]{0:T(1024)(128)(4,1)S(1)}, s32[]{:S(2)}) async-start(s8[11796480]{0:T(1024)(128)(4,1)} %bitcast.367), calls=%async_computation.18 | async-start | bytes 8388608
  201.6 25.2 %slice-start.19 = ((s8[11796480]{0:T(1024)(128)(4,1)}), s8[4194304]{0:T(1024)(128)(4,1)S(1)}, s32[]{:S(2)}) async-start(s8[11796480]{0:T(1024)(128)(4,1)} %bitcast.367), calls=%async_computation.19 | async-start | bytes 8388608
  215.9 11.0 %slice-start.20 = ((s8[11796480]{0:T(1024)(128)(4,1)}), s8[3407872]{0:T(1024)(128)(4,1)S(1)}, s32[]{:S(2)}) async-start(s8[11796480]{0:T(1024)(128)(4,1)} %bitcast.367), calls=%async_computation.20 | async-start | bytes 6815744
  245.0 82.4 %collective-permute-start.5 = (bf16[2,720,256]{2,1,0:T(8,128)(2,1)}, bf16[2,720,256]{2,1,0:T(8,128)(2,1)S(1)}, u32[]{:S(2)}, u32[]{:S(2)}) collective-permute-start(bf16[2,720,256]{2,1,0:T(8,128)(2,1)} %get-tuple-element.24), channel_id=1, source_target_pairs={{1,0},{2,1},{3,2},{5,4},{6,5},{7,6},{9,8},{10,9},{11,10},{13,12},{... | collective-permute-start | bytes 2211848 | tf_op jit(solution)/shard_map/ppermute | solution.py:19
  246.3 81.1 %collective-permute-start.4 = (bf16[2,720,256]{2,1,0:T(8,128)(2,1)}, bf16[2,720,256]{2,1,0:T(8,128)(2,1)S(1)}, u32[]{:S(2)}, u32[]{:S(2)}) collective-permute-start(bf16[2,720,256]{2,1,0:T(8,128)(2,1)} %get-tuple-element.23), channel_id=1, source_target_pairs={{0,1},{1,2},{2,3},{4,5},{5,6},{6,7},{8,9},{9,10},{10,11},{12,13},{... | collective-permute-start | bytes 2211848 | tf_op jit(solution)/shard_map/ppermute | solution.py:16
  327.8 8.1 %collective-permute-start.7 = (bf16[8,2,256]{2,1,0:T(2,128)(2,1)S(1)}, bf16[8,2,256]{2,1,0:T(2,128)(2,1)S(1)}, u32[]{:S(2)}, u32[]{:S(2)}) collective-permute-start(bf16[8,2,256]{2,1,0:T(2,128)(2,1)S(1)} %get-tuple-element.19), channel_id=1, source_target_pairs={{4,0},{8,4},{12,8},{16,12},{20,16},{24,20},{28,24},{0,28},{5,1},{9... | collective-permute-start | bytes 24584 | tf_op jit(solution)/shard_map/ppermute | solution.py:19
  327.9 8.1 %collective-permute-start.6 = (bf16[8,2,256]{2,1,0:T(2,128)(2,1)S(1)}, bf16[8,2,256]{2,1,0:T(2,128)(2,1)S(1)}, u32[]{:S(2)}, u32[]{:S(2)}) collective-permute-start(bf16[8,2,256]{2,1,0:T(2,128)(2,1)S(1)} %get-tuple-element.20), channel_id=1, source_target_pairs={{0,4},{4,8},{8,12},{12,16},{16,20},{20,24},{24,28},{28,0},{1,5},{5... | collective-permute-start | bytes 24584 | tf_op jit(solution)/shard_map/ppermute | solution.py:16
  354.0 28.4 %slice-start.9 = ((s8[9216000]{0:T(1024)(128)(4,1)}), s8[4194304]{0:T(1024)(128)(4,1)S(1)}, s32[]{:S(2)}) async-start(s8[9216000]{0:T(1024)(128)(4,1)} %bitcast.361), calls=%async_computation.9 | async-start | bytes 8388608
  354.0 28.4 %slice-start.10 = ((s8[9216000]{0:T(1024)(128)(4,1)}), s8[4194304]{0:T(1024)(128)(4,1)S(1)}, s32[]{:S(2)}) async-start(s8[9216000]{0:T(1024)(128)(4,1)} %bitcast.361), calls=%async_computation.10 | async-start | bytes 8388608
  368.1 14.3 %slice-start.11 = ((s8[9216000]{0:T(1024)(128)(4,1)}), s8[827392]{0:T(1024)(128)(4,1)S(1)}, s32[]{:S(2)}) async-start(s8[9216000]{0:T(1024)(128)(4,1)} %bitcast.361), calls=%async_computation.11 | async-start | bytes 1654784
  368.1 25.2 %slice-start.3 = ((s8[9216000]{0:T(1024)(128)(4,1)}), s8[4194304]{0:T(1024)(128)(4,1)S(1)}, s32[]{:S(2)}) async-start(s8[9216000]{0:T(1024)(128)(4,1)} %bitcast.357), calls=%async_computation.3 | async-start | bytes 8388608
  368.1 25.2 %slice-start.4 = ((s8[9216000]{0:T(1024)(128)(4,1)}), s8[4194304]{0:T(1024)(128)(4,1)S(1)}, s32[]{:S(2)}) async-start(s8[9216000]{0:T(1024)(128)(4,1)} %bitcast.357), calls=%async_computation.4 | async-start | bytes 8388608
  382.3 11.0 %slice-start.5 = ((s8[9216000]{0:T(1024)(128)(4,1)}), s8[827392]{0:T(1024)(128)(4,1)S(1)}, s32[]{:S(2)}) async-start(s8[9216000]{0:T(1024)(128)(4,1)} %bitcast.357), calls=%async_computation.5 | async-start | bytes 1654784
  393.3 11.2 %copy-start.5 = (bf16[2304,256]{1,0:T(8,128)(2,1)S(1)}, bf16[2304,256]{1,0:T(8,128)(2,1)}, u32[]{:S(2)}) copy-start(bf16[2304,256]{1,0:T(8,128)(2,1)} %param.18) | copy-start | bytes 3538948
  404.5 27.5 %slice-start.15 = ((s8[11796480]{0:T(1024)(128)(4,1)}), s8[4194304]{0:T(1024)(128)(4,1)S(1)}, s32[]{:S(2)}) async-start(s8[11796480]{0:T(1024)(128)(4,1)} %bitcast.365), calls=%async_computation.15 | async-start | bytes 8388608
  404.5 27.5 %slice-start.16 = ((s8[11796480]{0:T(1024)(128)(4,1)}), s8[4194304]{0:T(1024)(128)(4,1)S(1)}, s32[]{:S(2)}) async-start(s8[11796480]{0:T(1024)(128)(4,1)} %bitcast.365), calls=%async_computation.16 | async-start | bytes 8388608
  417.8 14.3 %slice-start.17 = ((s8[11796480]{0:T(1024)(128)(4,1)}), s8[3407872]{0:T(1024)(128)(4,1)S(1)}, s32[]{:S(2)}) async-start(s8[11796480]{0:T(1024)(128)(4,1)} %bitcast.365), calls=%async_computation.17 | async-start | bytes 6815744
  417.8 25.1 %slice-start.12 = ((s8[11796480]{0:T(1024)(128)(4,1)}), s8[4194304]{0:T(1024)(128)(4,1)S(1)}, s32[]{:S(2)}) async-start(s8[11796480]{0:T(1024)(128)(4,1)} %bitcast.363), calls=%async_computation.12 | async-start | bytes 8388608
  417.8 25.1 %slice-start.13 = ((s8[11796480]{0:T(1024)(128)(4,1)}), s8[4194304]{0:T(1024)(128)(4,1)S(1)}, s32[]{:S(2)}) async-start(s8[11796480]{0:T(1024)(128)(4,1)} %bitcast.363), calls=%async_computation.13 | async-start | bytes 8388608
  432.0 10.9 %slice-start.14 = ((s8[11796480]{0:T(1024)(128)(4,1)}), s8[3407872]{0:T(1024)(128)(4,1)S(1)}, s32[]{:S(2)}) async-start(s8[11796480]{0:T(1024)(128)(4,1)} %bitcast.363), calls=%async_computation.14 | async-start | bytes 6815744
  442.9 9.9 %copy-start.6 = (f32[1,720,256]{2,1,0:T(8,128)S(1)}, f32[1,720,256]{2,1,0:T(8,128)}, u32[]{:S(2)}) copy-start(f32[1,720,256]{2,1,0:T(8,128)} %fusion.68) | copy-start | bytes 2211844
  442.9 9.9 %copy-start.8 = (f32[1,720,256]{2,1,0:T(8,128)S(1)}, f32[1,720,256]{2,1,0:T(8,128)}, u32[]{:S(2)}) copy-start(f32[1,720,256]{2,1,0:T(8,128)} %fusion.71) | copy-start | bytes 2211844
  442.9 11.3 %copy-start.1 = (bf16[2304,256]{1,0:T(8,128)(2,1)S(1)}, bf16[2304,256]{1,0:T(8,128)(2,1)}, u32[]{:S(2)}) copy-start(bf16[2304,256]{1,0:T(8,128)(2,1)} %param.17) | copy-start | bytes 3538948
  (6 other events, 45.4 us)
where the time goes:
time: 463 us; the launch traced here: 455 us
  matrix products  323 us (70%)
  local copies, waits for them, and re-layouts  49.6 us (11%)
  blocking collectives  46.6 us (10%)
  other arithmetic  17 us (4%)
  starting transfers between devices  16.6 us (4%)
    dot_general x8, matrix products, convolve(): jnp.einsum('krd,rdjc->kjc', tap_cube[row], window, preferred_element_type...  101 us
    dot_general x8, matrix products, convolve(): jnp.einsum('kjc,kco->jo', feature, kernel_cube, preferred_element_type=jn...  96.1 us
    dot_general x8, matrix products, convolve(): jnp.einsum('kmc,jm->kjc', coef_row[:, 1, :, None] * sin_part[row][None],...  61.2 us
    dot_general x8, matrix products, convolve(): jnp.einsum('kmc,jm->kjc', coef_row[:, 0, :, None] * cos_part[row][None],...  60.6 us
    psum x2, blocking collectives, cycle_harmonics(): cos_part, sin_part = lax.psum((cos_local, sin_local), 'lat')  46.6 us
    slice x2, local copies, waits for them, and re-layouts, convolve(): window = col_shifted[row:row + 5]  35 us
    ppermute x4, starting transfers between devices, with_halo(): lax.ppermute(lax.slice_in_dim(block, block.shape[dim] - width, None, axis...  11.3 us
  transfers between devices with their start and end apart: 8, of which 0 were waited for; matrix products, arithmetic and copies ran while one was open for 30% of the time, Pallas kernels for 0%

commit v1 on v0

v1 whole, which is shorter than its diff:
```python
import functools
import math

import jax
import jax.numpy as jnp
from jax import lax
from jax.experimental import pallas as pl
from jax.experimental.pallas import tpu as pltpu
from jax.sharding import PartitionSpec as P

BLOCK = 16
GROUP = 6
HALO = 16
TAPS = 5
VMEM_BYTES = 40 * 1024 * 1024


def vmem_params():
    return pltpu.CompilerParams(vmem_limit_bytes=VMEM_BYTES)


def shift_pairs(axis, periodic):
    count = lax.axis_size(axis)
    forward = [(i, i + 1) for i in range(count - 1)]
    if periodic:
        forward.append((count - 1, 0))
    return forward, [(target, source) for source, target in forward]


def tap_weights(psi, lon_start, lon_width):
    offsets = jnp.arange(TAPS, dtype=jnp.int32)
    shifted = lon_start[:, None, None] + offsets[None, :, None]
    target = offsets[None, None, :] - 2
    select = ((shifted == target) & (offsets[None, :, None] < lon_width[:, None, None])).astype(
        jnp.float32
    )
    mixed_taps = jnp.einsum(
        "ikrq,iqd->ikrd", psi.astype(jnp.float32), select, precision=lax.Precision.HIGHEST
    )
    return mixed_taps.astype(jnp.bfloat16)


def tap_matrix(psi, lon_start, lon_width, first):
    rows, basis = psi.shape[0], psi.shape[1]
    taps = tap_weights(psi, lon_start, lon_width)
    spread = jnp.stack(
        [jnp.pad(taps[i], ((0, 0), (i, rows - 1 - i), (0, 0))) for i in range(rows)], axis=1
    )
    height = rows + TAPS - 1
    spread = spread.reshape(basis * rows, height * TAPS)
    shape = (height, TAPS, BLOCK, 2, height, BLOCK)
    it = lambda axis: lax.broadcasted_iota(jnp.int32, shape, axis)
    place = (it(0) == it(4)) & (it(3) * BLOCK + it(5) == first + it(2) + it(1))
    place = place.astype(jnp.bfloat16).reshape(height * TAPS, BLOCK * 2 * height * BLOCK)
    matrix = jnp.dot(spread, place, preferred_element_type=jnp.float32).astype(jnp.bfloat16)
    return matrix.reshape(basis * rows * BLOCK, 2 * height * BLOCK)


def wave_rows(columns, cycle_length, count):
    orders = jnp.arange(count, dtype=jnp.int32)
    phase_index = columns[None, :] % cycle_length * orders[:, None] % cycle_length
    angles = phase_index.astype(jnp.float32) * jnp.float32(2.0 * math.pi / cycle_length)
    return jnp.concatenate([jnp.cos(angles), jnp.sin(angles)], axis=0)


def wave_table(waves, rows):
    high = waves.astype(jnp.bfloat16)
    low = (waves - high.astype(jnp.float32)).astype(jnp.bfloat16)
    lanes = jnp.concatenate([high, low, high, jnp.zeros_like(high)], axis=0)
    blocks = waves.shape[1] // BLOCK
    lanes = lanes.T.reshape(blocks, 1, BLOCK, 1, lanes.shape[0])
    own = jnp.eye(rows, dtype=jnp.bfloat16).reshape(1, rows, 1, rows, 1)
    return (lanes * own).reshape(blocks * rows * BLOCK, rows * lanes.shape[-1])


def cycle_kernel(norm_factor, parts_ref, coef_ref, polar_ref, w_ref, out_ref):
    total = parts_ref[0]
    for p in range(1, parts_ref.shape[0]):
        total = total + parts_ref[p]
    total = total * norm_factor
    channels = total.shape[1]
    acc = jnp.zeros((2 * total.shape[0], w_ref.shape[1]), jnp.float32)
    for k in range(coef_ref.shape[1]):
        term = total * coef_ref[:, k : k + 1]
        high = term.astype(jnp.bfloat16)
        low = (term - high.astype(jnp.float32)).astype(jnp.bfloat16)
        acc += jnp.dot(
            jnp.concatenate([high, low], axis=0),
            w_ref[k * channels : (k + 1) * channels],
            preferred_element_type=jnp.float32,
        )
    mixed = (acc[: total.shape[0]] + acc[total.shape[0] :]) * polar_ref[:, 0:1]
    high = mixed.astype(jnp.bfloat16).astype(jnp.float32)
    low = mixed - high
    pieces = []
    for i in range(total.shape[0] // 8):
        own = slice(8 * i, 8 * i + 8)
        pieces += [high[own], high[own], low[own], jnp.zeros_like(low[own])]
    out_ref[...] = jnp.concatenate(pieces, axis=0).astype(jnp.bfloat16)


def conv_kernel(blocks, first_block, gelu, blocked, *refs):
    up_ref, mid_ref, low_ref, dn_ref, taps_ref, w_ref, bias_ref, waves_ref, cycle_ref = refs[:9]
    refs = refs[9:]
    if gelu:
        own_ref, top_ref, bot_ref, harm_ref, feat_ref = refs
        harm_ref[...] = jnp.zeros_like(harm_ref)
    else:
        out_ref, feat_ref = refs
    channels = w_ref.shape[1]
    basis = w_ref.shape[0] // channels
    slab = 4 * BLOCK

    def half(b):
        if blocked:
            parts = [up_ref[b], mid_ref[b], low_ref[b], dn_ref[b]]
        else:
            at = pl.ds(pl.multiple_of(b * BLOCK, BLOCK), BLOCK)
            own = pl.ds(pl.multiple_of((b + first_block) * BLOCK, BLOCK), BLOCK)
            parts = [up_ref[:, at], mid_ref[:, own], dn_ref[:, at]]
        return jnp.concatenate(parts, axis=0).reshape(8 * BLOCK, channels)

    def group(start, count):
        for t in range(count):
            window = jnp.concatenate([half(start + t), half(start + t + 1)], axis=0)
            feature = jnp.dot(taps_ref[...], window, preferred_element_type=jnp.float32)
            feature = feature.astype(jnp.bfloat16)
            for k in range(basis):
                feat_ref[t * slab : (t + 1) * slab, k * channels : (k + 1) * channels] = feature[
                    k * slab : (k + 1) * slab
                ]
        rows = pl.ds(pl.multiple_of(start * slab, slab), count * slab)
        mixed = jnp.dot(
            feat_ref[: count * slab], w_ref[...], preferred_element_type=jnp.float32
        )
        mixed += jnp.dot(waves_ref[rows], cycle_ref[...], preferred_element_type=jnp.float32)
        mixed += bias_ref[...]
        if gelu:
            mixed = 0.5 * mixed * (1.0 + lax.erf(mixed * math.sqrt(0.5)))
        value = mixed.astype(jnp.bfloat16)
        for t in range(count):
            piece = value[t * slab : (t + 1) * slab].reshape(4, BLOCK, channels)
            if gelu:
                top_ref[start + t] = piece[:2]
                bot_ref[start + t] = piece[2:]
            else:
                at = pl.ds(pl.multiple_of((start + t) * BLOCK, BLOCK), BLOCK)
                out_ref[:, at] = piece
        if gelu:
            lanes = pl.ds(pl.multiple_of(start * slab, 2 * slab), count * slab)
            harm_ref[...] += jnp.dot(
                own_ref[:, lanes], value, preferred_element_type=jnp.float32
            )

    full = blocks // GROUP

    @pl.loop(0, full)
    def _(s):
        group(s * GROUP, GROUP)

    if blocks % GROUP:
        group(full * GROUP, blocks % GROUP)


def conv_cost(blocks, channels):
    macs = blocks * BLOCK * 4 * 18 * channels * channels
    return pl.CostEstimate(flops=4 * macs, bytes_accessed=8_000_000, transcendentals=0)


def body(
    latent,
    psi_one,
    psi_two,
    cycle_one,
    cycle_two,
    w_one,
    w_two,
    b_one,
    b_two,
    lon_start,
    lon_width,
    polar_counts,
):
    row_count, col_count, channels = latent.shape
    harm_count = cycle_one.shape[3]
    lat_total = row_count * lax.axis_size("lon")
    cycle_length = col_count * lax.axis_size("lat")
    norm_factor = cycle_length ** (-0.5)
    first_row = lax.axis_index("lon") * row_count
    first_col = lax.axis_index("lat") * col_count
    east, west = shift_pairs("lat", True)
    south, north = shift_pairs("lon", False)
    out_blocks = col_count // BLOCK
    hid_blocks = out_blocks + 1
    hid_cols = hid_blocks * BLOCK

    left = lax.ppermute(latent[:, col_count - HALO :], "lat", east)
    right = lax.ppermute(latent[:, :HALO], "lat", west)
    wide = jnp.concatenate([left, latent, right], axis=1)
    up = lax.ppermute(wide[2:], "lon", south)
    down = lax.ppermute(wide[:2], "lon", north)

    own_start = lax.dynamic_slice_in_dim(lon_start, first_row, row_count, 0)
    own_width = lax.dynamic_slice_in_dim(lon_width, first_row, row_count, 0)
    taps_one = tap_matrix(psi_one, own_start, own_width, HALO - 4)
    taps_two = tap_matrix(psi_two, own_start, own_width, 0)
    columns = first_col - 2 + jnp.arange(hid_cols + 2, dtype=jnp.int32) + cycle_length
    waves = wave_rows(columns, cycle_length, harm_count)
    waves_hid, waves_out = waves[:, :hid_cols], waves[:, 2 : 2 + col_count]
    table_hid = wave_table(waves_hid, row_count)
    table_out = wave_table(waves_out, row_count)
    place = jnp.arange(hid_cols, dtype=jnp.int32)
    own = (place >= 2) & (place < 2 + col_count)
    kept = jnp.where(own[None], waves_hid, 0.0).astype(jnp.bfloat16)
    kept = kept.reshape(1, 2 * harm_count, hid_blocks, 1, BLOCK)
    eye = jnp.eye(row_count, dtype=jnp.bfloat16).reshape(row_count, 1, 1, row_count, 1)
    own_waves = (eye * kept).reshape(
        row_count * 2 * harm_count, hid_blocks * row_count * BLOCK
    )

    row_global = first_row + jnp.arange(row_count, dtype=jnp.int32)
    polar = (
        (row_global < polar_counts[0]) | (row_global >= lat_total - polar_counts[1])
    ).astype(jnp.float32)

    def cycle_mix(part, coef, w):
        lanes = row_count * 2 * harm_count
        coef_rows = coef.transpose(0, 2, 3, 1).reshape(lanes, coef.shape[1])
        polar_rows = jnp.repeat(polar, 2 * harm_count)[:, None]
        parts = lax.all_gather(part, "lat")
        return pl.pallas_call(
            functools.partial(cycle_kernel, norm_factor),
            out_shape=jax.ShapeDtypeStruct((row_count * 32, channels), jnp.bfloat16),
            compiler_params=vmem_params(),
        )(parts, coef_rows, polar_rows, w)

    part_one = jnp.einsum(
        "mj,ijc->imc",
        waves_out.astype(jnp.bfloat16),
        latent,
        preferred_element_type=jnp.float32,
    ).reshape(row_count * 2 * harm_count, channels)
    mix_one = cycle_mix(part_one, cycle_one, w_one)

    hid_half = jax.ShapeDtypeStruct((hid_blocks, 2, BLOCK, channels), jnp.bfloat16)
    feat = pltpu.VMEM((GROUP * row_count * BLOCK, w_one.shape[0]), jnp.bfloat16)

    def first_kernel(up_ref, mid_ref, dn_ref, *rest):
        conv_kernel(hid_blocks, 0, True, False, up_ref, mid_ref, None, dn_ref, *rest)

    top, bottom, part_two = pl.pallas_call(
        first_kernel,
        out_shape=(
            hid_half,
            hid_half,
            jax.ShapeDtypeStruct((row_count * 2 * harm_count, channels), jnp.float32),
        ),
        scratch_shapes=[feat],
        compiler_params=vmem_params(),
        cost_estimate=conv_cost(hid_blocks, channels),
    )(up, wide, down, taps_one, w_one, b_one[None], table_hid, mix_one, own_waves)

    hid_up = lax.ppermute(bottom, "lon", south)
    hid_down = lax.ppermute(top, "lon", north)
    mix_two = cycle_mix(part_two, cycle_two, w_two)

    def second_kernel(*refs):
        conv_kernel(out_blocks, 0, False, True, *refs)

    return pl.pallas_call(
        second_kernel,
        out_shape=jax.ShapeDtypeStruct((row_count, col_count, channels), jnp.bfloat16),
        scratch_shapes=[feat],
        compiler_params=vmem_params(),
        cost_estimate=conv_cost(out_blocks, channels),
    )(hid_up, top, bottom, hid_down, taps_two, w_two, b_two[None], table_out, mix_two)


def solution(mesh):
    return jax.shard_map(
        body,
        mesh=mesh,
        in_specs=(
            P("lon", "lat", None),
            P("lon", None, None, None),
            P("lon", None, None, None),
            P("lon", None, None, None),
            P("lon", None, None, None),
            P(),
            P(),
            P(),
            P(),
            P(),
            P(),
            P(),
        ),
        out_specs=P("lon", "lat", None),
        check_vma=False,
    )
```

time: 463 us -> 112 us (0.24); the launches traced: 455 us -> 111 us
  matrix products: 323 us -> 3.65 us
  Pallas kernels: 0 us -> 35.8 us
  blocking collectives: 46.6 us -> 17.9 us
  local copies, waits for them, and re-layouts: 49.6 us -> 25.8 us
  other arithmetic: 17 us -> 9.6 us
    dot_general x36 -> x3, matrix products: 323 us -> 3.26 us  [the longest x1 1.76 us: body(): jnp.einsum('mj,ijc->imc', waves_out.astype(jnp.bfloat16), latent, preferr...]
    psum x2 -> x0, blocking collectives: 46.6 us -> none  [cycle_harmonics(): cos_part, sin_part = lax.psum((cos_local, sin_local), 'lat')]
    slice x8 -> x3, local copies, waits for them, and re-layouts: 39.9 us -> 2.66 us  [the longest x1 1.24 us: body(): down = lax.ppermute(wide[:2], 'lon', north)]
    pallas_call x0 -> x4, Pallas kernels: none -> 35.8 us  [the longest x1 18.1 us: body(): pl.pallas_call(first_kernel, out_shape=(hid_half, hid_half, jax.ShapeDtyp...]
    all_gather x0 -> x2, blocking collectives: none -> 17.9 us  [cycle_mix(): parts = lax.all_gather(part, 'lat')]
    convert_element_type x3 -> x6, other arithmetic: 8.56 us -> 1.58 us  [the longest x2 0.82 us: wave_table(): low = (waves - high.astype(jnp.float32)).astype(jnp.bfloat16)]
    mul x24 -> x4, local copies, waits for them, and re-layouts: 2.69 us -> 9.6 us  [the longest x2 7.76 us: wave_table(): return (lanes * own).reshape(blocks * rows * BLOCK, rows * lanes.shape[-1])]
    mul x3 -> x4, other arithmetic: 0.03 us -> 6.21 us  [the longest x2 5.55 us: wave_table(): return (lanes * own).reshape(blocks * rows * BLOCK, rows * lanes.shape[-1])]
  transfers between devices with their start and end apart: 8 -> 6, of which waited for: 0 -> 1; matrix products, arithmetic and copies ran while one was open for 30% -> 33% of each run, Pallas kernels for 0% -> 1%
where the time goes in v1:
time: 112 us; the launch traced here: 111 us
  Pallas kernels  35.8 us (32%)
  local copies, waits for them, and re-layouts  25.8 us (23%)
  blocking collectives  17.9 us (16%)
  starting transfers between devices  15.9 us (14%)
  other arithmetic  9.6 us (9%)
  matrix products  3.65 us (3%)
  between operations  1.17 us (1%)
  waiting for transfers between devices  1.14 us (1%)
    pallas_call x1, Pallas kernels, body(): pl.pallas_call(first_kernel, out_shape=(hid_half, hid_half, jax.ShapeDtyp...  18.1 us
    all_gather x2, blocking collectives, cycle_mix(): parts = lax.all_gather(part, 'lat')  17.9 us
    pallas_call x1, Pallas kernels, body(): pl.pallas_call(second_kernel, out_shape=jax.ShapeDtypeStruct((row_count,...  17 us
    mul x2, local copies, waits for them, and re-layouts, wave_table(): return (lanes * own).reshape(blocks * rows * BLOCK, rows * lanes.shape[-1])  7.76 us
    mul x2, other arithmetic, wave_table(): return (lanes * own).reshape(blocks * rows * BLOCK, rows * lanes.shape[-1])  5.55 us
    ppermute x1, starting transfers between devices, body(): up = lax.ppermute(wide[2:], 'lon', south)  5.2 us
    ppermute x1, starting transfers between devices, body(): hid_up = lax.ppermute(bottom, 'lon', south)  4.58 us
    ppermute x1, starting transfers between devices, body(): right = lax.ppermute(latent[:, :HALO], 'lat', west)  2.93 us
  transfers between devices with their start and end apart: 6, of which 1 were waited for; matrix products, arithmetic and copies ran while one was open for 33% of the time, Pallas kernels for 1%

profile of v1, /device:TPU:0, one launch (start us, length us, event | category | flops | bytes accessed | tf_op | source)
XLA Modules:
  0.0 111.1 jit_solution(6004778708491676842)
XLA Ops:
  0.0 0.8 fusion.40
  0.8 0.5 collective-permute-start
  1.3 2.9 %collective-permute-start.1 = (bf16[4,16,256]{2,1,0:T(8,128)(2,1)S(1)}, bf16[4,16,256]{2,1,0:T(8,128)(2,1)S(1)}, u32[]{:S(2)}, u32[]{:S(2)}) collective-permute-start(bf16[4,16,256]{2,1,0:T(8,128)(2,1)S(1)} %get-tuple-element.15), channel_id=1, source_target_pairs={{4,0},{8,4},{12,8},{16,12},{20,16},{24,20},{28,24},{0,28},{5,1},{9... | collective-permute-start | bytes 98312 | tf_op jit(solution)/shard_map/ppermute | solution.py:198
  4.2 0.7 dynamic_slice.6
  5.0 0.7 dynamic_slice.7
  5.8 0.2 fusion
  6.1 0.3 copy.28
  6.4 0.1 reshape.151
  7.3 0.1 fusion.30
  7.6 0.2 copy.29
  7.8 0.6 fusion.41
  8.5 0.1 mul.103
  8.6 2.8 %broadcast_multiply_fusion = bf16[46,4,16,4,32]{4,3,2,1,0:T(4,128)(2,1)} fusion(bf16[4,4]{1,0:T(4,128)(2,1)S(1)} %fusion.35, bf16[46,16,32]{2,1,0:T(8,128)(2,1)S(1)} %bitcast.87), kind=kLoop, calls=%fused_computation.2 | loop fusion | flops 376832 | bytes 800800 | tf_op jit(solution)/shard_map/mul | solution.py:73
  11.4 0.7 broadcast_multiply_fusion.2
  12.1 0.2 fusion.1
  12.3 0.6 slice_bitcast_fusion.3
  13.6 0.6 pad_bitcast_fusion
  14.2 0.4 convolution_convert_fusion.1
  14.6 0.7 or_convert_fusion
  15.3 0.9 reshape.152.rest_0_
  16.1 3.9 %mul.101.rest_3_ = bf16[2944,128]{1,0:T(8,128)(2,1)S(1)} reshape(bf16[46,4,16,4,32]{4,3,2,1,0:T(4,128)(2,1)} %broadcast_multiply_fusion) | data formatting | bytes 1507328 | tf_op jit(solution)/shard_map/mul | solution.py:73
  20.1 1.7 %mul.106.rest_5_ = bf16[32,2944]{1,0:T(8,128)(2,1)} reshape(bf16[4,8,46,4,16]{4,3,2,1,0:T(4,128)(2,1)S(1)} %broadcast_multiply_fusion.2) | data formatting | bytes 376832 | tf_op jit(solution)/shard_map/mul | solution.py:217
  21.9 1.5 %constant_dynamic-update-slice_fusion.1 = bf16[4,752,256]{2,1,0:T(8,128)(2,1)S(1)} fusion(bf16[4,752,256]{2,1,0:T(8,128)(2,1)S(1)} %constant_dynamic-update-slice_fusion.2, bf16[4,720,256]{2,1,0:T(8,128)(2,1)} %param.12), kind=kLoop, calls=%fused_computation.65 | loop fusion | bytes 2949120
  23.4 1.2 %fusion.39 = (bf16[2,752,256]{2,1,0:T(8,128)(2,1)}, bf16[2,752,256]{2,1,0:T(8,128)(2,1)}) fusion(bf16[4,752,256]{2,1,0:T(8,128)(2,1)S(1)} %constant_dynamic-update-slice_fusion.mid_ref), kind=kLoop, calls=%fused_computation.92 | loop fusion | bytes 3080192 | tf_op jit(solution)/shard_map/slice | solution.py:201
  24.6 5.2 %collective-permute-start.2 = (bf16[2,752,256]{2,1,0:T(8,128)(2,1)}, bf16[2,752,256]{2,1,0:T(8,128)(2,1)}, u32[]{:S(2)}, u32[]{:S(2)}) collective-permute-start(bf16[2,752,256]{2,1,0:T(8,128)(2,1)} %get-tuple-element.14), channel_id=1, source_target_pairs={{0,1},{1,2},{2,3},{4,5},{5,6},{6,7},{8,9},{9,10},{10,11},{12,13},{... | collective-permute-start | bytes 2310152 | tf_op jit(solution)/shard_map/ppermute | solution.py:200
  29.8 1.3 %collective-permute-start.3 = (bf16[2,752,256]{2,1,0:T(8,128)(2,1)}, bf16[2,752,256]{2,1,0:T(8,128)(2,1)}, u32[]{:S(2)}, u32[]{:S(2)}) collective-permute-start(bf16[2,752,256]{2,1,0:T(8,128)(2,1)} %get-tuple-element.13), channel_id=1, source_target_pairs={{1,0},{2,1},{3,2},{5,4},{6,5},{7,6},{9,8},{10,9},{11,10},{13,12},{... | collective-permute-start | bytes 2310152 | tf_op jit(solution)/shard_map/ppermute | solution.py:201
  31.2 0.6 pad_maximum_fusion.1
  31.8 1.8 %copy.32 = bf16[9,4,8,5]{3,2,1,0:T(8,128)(2,1)} copy(bf16[9,4,8,5]{0,3,2,1:T(8,128)(2,1)} %pad_maximum_fusion.1) | data formatting | bytes 5760 | tf_op jit(solution)/shard_map/stack | solution.py:46
  33.6 1.6 %reshape.154 = bf16[36,40]{1,0:T(8,128)(2,1)} reshape(bf16[9,4,8,5]{3,2,1,0:T(8,128)(2,1)} %copy.32) | data formatting | bytes 5760 | tf_op jit(solution)/shard_map/reshape | solution.py:50
  35.2 0.7 iota.201
  35.8 1.6 %iota.202 = s32[4096]{0:T(1024)} reshape(s32[16,2,8,16]{3,2,1,0:T(8,128)} %iota.201) | data formatting | bytes 32768 | tf_op jit(solution)/shard_map/iota | solution.py:52
  37.5 1.8 %convolution_bitcast_fusion = f32[1,32,256]{2,1,0:T(8,128)S(1)} fusion(bf16[4,720,256]{2,1,0:T(8,128)(2,1)} %param.12, f32[4,738]{1,0:T(4,128)} %copy-done.11, f32[4,738]{1,0:T(4,128)S(1)} %get-tuple-element.25), kind=kOutput, calls=%fused_computation.8 | convolution fusion | flops 11819520 | bytes 1530944 | tf_op jit(solution)/shard_map/mj,ijc->imc/dot_general | solution.py:237
  39.3 9.5 %all_gather.9.parts_ref = f32[8,32,256]{2,1,0:T(8,128)S(1)} all-gather(f32[1,32,256]{2,1,0:T(8,128)S(1)} %convolution_bitcast_fusion), channel_id=1, replica_groups=mesh['lat'=8,'lon'=4] {'lat'}, dimensions={0}, use_global_device_ids=true | all-gather | bytes 294912 | tf_op jit(solution)/shard_map/all_gather | solution.py:230
  48.7 0.4 shard_map.118.rest_4_
  49.2 1.1 %convolution_convert_fusion = bf16[36,4096]{1,0:T(8,128)(2,1)} fusion(bf16[36,40]{1,0:T(8,128)(2,1)S(1)} %copy-done.23, s32[4096]{0:T(1024)S(1)} %copy-done.22, s32[40]{0:T(128)S(1)} %copy-done.29, s32[4096]{0:T(1024)S(1)} %copy-done.19, s32[4096]{0:T(1024)S(1)} %copy-done.21, s32[40]{0:T(128)S(1)} %copy-done.27), kind=kOutput, calls=%fused_computation | convolution fusion | flops 12599296 | bytes 347264 | tf_op jit(solution)/shard_map/dot_general | solution.py:55
  50.3 18.1 %shard_map.119 = (bf16[46,2,16,256]{3,2,1,0:T(8,128)(2,1)}, bf16[46,2,16,256]{3,2,1,0:T(8,128)(2,1)}, f32[32,256]{1,0:T(8,128)S(1)}) custom-call(bf16[2,752,256]{2,1,0:T(8,128)(2,1)} %collective-permute-done.2.up_ref, bf16[4,752,256]{2,1,0:T(8,128)(2,1)S(1)} %constant_dynamic-update-slice_fusion.mid_ref, bf16[2,752,256]{2,1,0:T(8,128)(2,1)} %collective-permute-done.3.dn_ref, ...), custom_call_target="tpu_custom_call" | custom-call | flops 13891534848 | bytes 8000000 | tf_op jit(solution)/shard_map/pallas_call | solution.py:251
  68.4 4.6 %collective-permute-start.4 = (bf16[46,2,16,256]{3,2,1,0:T(8,128)(2,1)}, bf16[46,2,16,256]{3,2,1,0:T(8,128)(2,1)S(1)}, u32[]{:S(2)}, u32[]{:S(2)}) collective-permute-start(bf16[46,2,16,256]{3,2,1,0:T(8,128)(2,1)} %get-tuple-element.8.refs_2_), channel_id=1, source_target_pairs={{0,1},{1,2},{2,3},{4,5},{5,6},{6,7},{8,9},{9,10},{10,11},{12,13},{... | collective-permute-start | bytes 2261000 | tf_op jit(solution)/shard_map/ppermute | solution.py:263
  73.0 1.5 %collective-permute-start.5 = (bf16[46,2,16,256]{3,2,1,0:T(8,128)(2,1)}, bf16[46,2,16,256]{3,2,1,0:T(8,128)(2,1)}, u32[]{:S(2)}, u32[]{:S(2)}) collective-permute-start(bf16[46,2,16,256]{3,2,1,0:T(8,128)(2,1)} %get-tuple-element.9.refs_1_), channel_id=1, source_target_pairs={{1,0},{2,1},{3,2},{5,4},{6,5},{7,6},{9,8},{10,9},{11,10},{13,12},{... | collective-permute-start | bytes 2261000 | tf_op jit(solution)/shard_map/ppermute | solution.py:264
  74.6 1.1 %reshape.155.refs_4_ = bf16[576,256]{1,0:T(8,128)(2,1)S(1)} reshape(bf16[36,4096]{1,0:T(8,128)(2,1)} %convolution_convert_fusion) | data formatting | bytes 589824 | tf_op jit(solution)/shard_map/reshape | solution.py:56
  75.7 0.8 subtract_convert_fusion
  76.5 0.7 maximum_bitcast_fusion.1
  77.2 0.2 copy.33
  77.4 2.8 %broadcast_multiply_fusion.1 = bf16[45,4,16,4,32]{4,3,2,1,0:T(4,128)(2,1)} fusion(bf16[4,4]{1,0:T(4,128)(2,1)S(1)} %fusion.35, bf16[45,16,32]{2,1,0:T(8,128)(2,1)S(1)} %bitcast.88), kind=kLoop, calls=%fused_computation.3 | loop fusion | flops 368640 | bytes 783392 | tf_op jit(solution)/shard_map/mul | solution.py:73
  80.2 3.9 %mul.111.refs_7_ = bf16[2880,128]{1,0:T(8,128)(2,1)S(1)} reshape(bf16[45,4,16,4,32]{4,3,2,1,0:T(4,128)(2,1)} %broadcast_multiply_fusion.1) | data formatting | bytes 1474560 | tf_op jit(solution)/shard_map/mul | solution.py:73
  84.1 8.4 %all-gather = f32[256,256]{1,0:T(8,128)S(1)} all-gather(f32[32,256]{1,0:T(8,128)S(1)} %get-tuple-element.10), channel_id=2, replica_groups=mesh['lat'=8,'lon'=4] {'lat'}, dimensions={0}, use_global_device_ids=true | all-gather | bytes 294912 | tf_op jit(solution)/shard_map/all_gather | solution.py:230
  92.5 0.4 shard_map.120.refs_8_
  92.9 1.1 %collective-permute-done.5.refs_3_ = bf16[46,2,16,256]{3,2,1,0:T(8,128)(2,1)} collective-permute-done((bf16[46,2,16,256]{3,2,1,0:T(8,128)(2,1)}, bf16[46,2,16,256]{3,2,1,0:T(8,128)(2,1)}, u32[]{:S(2)}, u32[]{:S(2)}) %collective-permute-start.5) | collective-permute-done | bytes 753696 | tf_op jit(solution)/shard_map/ppermute | solution.py:264
  94.0 17.0 %shard_map.121 = bf16[4,720,256]{2,1,0:T(8,128)(2,1)} custom-call(bf16[46,2,16,256]{3,2,1,0:T(8,128)(2,1)S(1)} %collective-permute-done.4.refs_0_, bf16[46,2,16,256]{3,2,1,0:T(8,128)(2,1)} %get-tuple-element.9.refs_1_, bf16[46,2,16,256]{3,2,1,0:T(8,128)(2,1)} %get-tuple-element.8.refs_2_, bf16[46,2,16,256]{3,2,1,0:T(8,128)(2,1)} %collective-permute-done.5.refs_3_, ...), custom_call_target="tpu_custom_call" | custom-call | flops 13589544960 | bytes 8000000 | tf_op jit(solution)/shard_map/pallas_call | solution.py:270
  (98 shorter events, 1.5 us)
Async XLA Ops:
  0.0 5.8 %copy-start = (bf16[4,9,5,5]{1,0,3,2:T(4,128)(2,1)S(1)}, bf16[4,9,5,5]{1,0,3,2:T(4,128)(2,1)}, u32[]{:S(2)}) copy-start(bf16[4,9,5,5]{1,0,3,2:T(4,128)(2,1)} %param.13) | copy-start | bytes 5404
  0.0 7.8 %copy-start.25 = (s32[2]{0:T(128)S(1)}, s32[2]{0:T(128)}, u32[]{:S(2)}) copy-start(s32[2]{0:T(128)} %param.23) | copy-start | bytes 28
  0.8 21.1 %collective-permute-start = (bf16[4,16,256]{2,1,0:T(8,128)(2,1)S(1)}, bf16[4,16,256]{2,1,0:T(8,128)(2,1)S(1)}, u32[]{:S(2)}, u32[]{:S(2)}) collective-permute-start(bf16[4,16,256]{2,1,0:T(8,128)(2,1)S(1)} %get-tuple-element.16), channel_id=1, source_target_pairs={{0,4},{4,8},{8,12},{12,16},{16,20},{20,24},{24,28},{28,0},{1,5},{5... | collective-permute-start | bytes 98312 | tf_op jit(solution)/shard_map/ppermute | solution.py:197
  1.3 22.1 %collective-permute-start.1 = (bf16[4,16,256]{2,1,0:T(8,128)(2,1)S(1)}, bf16[4,16,256]{2,1,0:T(8,128)(2,1)S(1)}, u32[]{:S(2)}, u32[]{:S(2)}) collective-permute-start(bf16[4,16,256]{2,1,0:T(8,128)(2,1)S(1)} %get-tuple-element.15), channel_id=1, source_target_pairs={{4,0},{8,4},{12,8},{16,12},{20,16},{24,20},{28,24},{0,28},{5,1},{9... | collective-permute-start | bytes 98312 | tf_op jit(solution)/shard_map/ppermute | solution.py:198
  6.8 7.4 %copy-start.18 = (s32[4096]{0:T(1024)}, s32[4096]{0:T(1024)S(1)}, u32[]{:S(2)}) copy-start(s32[4096]{0:T(1024)S(1)} %add.133) | copy-start | bytes 49156
  6.9 7.3 %copy-start.20 = (s32[4096]{0:T(1024)}, s32[4096]{0:T(1024)S(1)}, u32[]{:S(2)}) copy-start(s32[4096]{0:T(1024)S(1)} %iota.183) | copy-start | bytes 49156
  7.0 7.2 %copy-start.26 = (s32[40]{0:T(128)}, s32[40]{0:T(128)S(1)}, u32[]{:S(2)}) copy-start(s32[40]{0:T(128)S(1)} %iota.180) | copy-start | bytes 484
  7.1 7.1 %copy-start.28 = (s32[40]{0:T(128)}, s32[40]{0:T(128)S(1)}, u32[]{:S(2)}) copy-start(s32[40]{0:T(128)S(1)} %iota.194) | copy-start | bytes 484
  7.4 4.0 %copy-start.11 = (f32[4,738]{1,0:T(4,128)}, f32[4,738]{1,0:T(4,128)S(1)}, u32[]{:S(2)}) copy-start(f32[4,738]{1,0:T(4,128)S(1)} %get-tuple-element.26) | copy-start | bytes 35428
  7.4 30.0 %copy-start.9 = (f32[4,738]{1,0:T(4,128)}, f32[4,738]{1,0:T(4,128)S(1)}, u32[]{:S(2)}) copy-start(f32[4,738]{1,0:T(4,128)S(1)} %get-tuple-element.25) | copy-start | bytes 35428
  7.6 3.8 %copy-start.24 = (bf16[32]{0:T(256)(128)(2,1)}, bf16[32]{0:T(256)(128)(2,1)S(1)}, u32[]{:S(2)}) copy-start(bf16[32]{0:T(256)(128)(2,1)S(1)} %pad.47.clone) | copy-start | bytes 196
  11.4 0.7 copy-start.13
  23.3 7.8 %copy-start.16 = (bf16[9,5,5]{0,2,1:T(8,128)(2,1)S(1)}, bf16[9,5,5]{0,2,1:T(8,128)(2,1)}, u32[]{:S(2)}) copy-start(bf16[9,5,5]{0,2,1:T(8,128)(2,1)} %get-tuple-element.17) | copy-start | bytes 1354
  23.4 7.8 %copy-start.17 = (bf16[9,5,5]{0,2,1:T(8,128)(2,1)S(1)}, bf16[9,5,5]{0,2,1:T(8,128)(2,1)}, u32[]{:S(2)}) copy-start(bf16[9,5,5]{0,2,1:T(8,128)(2,1)} %get-tuple-element.20) | copy-start | bytes 1354
  23.4 7.8 %copy-start.14 = (bf16[9,1,8,5]{0,3,2,1:T(8,128)(2,1)S(1)}, bf16[9,1,8,5]{0,3,2,1:T(8,128)(2,1)}, u32[]{:S(2)}) copy-start(bf16[9,1,8,5]{0,3,2,1:T(8,128)(2,1)} %get-tuple-element.33) | copy-start | bytes 2164
  23.4 7.8 %copy-start.15 = (bf16[9,1,8,5]{0,3,2,1:T(8,128)(2,1)S(1)}, bf16[9,1,8,5]{0,3,2,1:T(8,128)(2,1)}, u32[]{:S(2)}) copy-start(bf16[9,1,8,5]{0,3,2,1:T(8,128)(2,1)} %get-tuple-element.34) | copy-start | bytes 2164
  24.6 24.1 %copy-start.1 = (bf16[2304,256]{1,0:T(8,128)(2,1)S(1)}, bf16[2304,256]{1,0:T(8,128)(2,1)}, u32[]{:S(2)}) copy-start(bf16[2304,256]{1,0:T(8,128)(2,1)} %rest_1_.1) | copy-start | bytes 3538948
  24.6 24.1 %copy-start.5 = (f32[4,9,2,4]{1,3,2,0:T(4,128)S(1)}, f32[4,9,2,4]{1,3,2,0:T(4,128)}, u32[]{:S(2)}) copy-start(f32[4,9,2,4]{1,3,2,0:T(4,128)} %param.15) | copy-start | bytes 3460
  24.6 25.7 %collective-permute-start.2 = (bf16[2,752,256]{2,1,0:T(8,128)(2,1)}, bf16[2,752,256]{2,1,0:T(8,128)(2,1)}, u32[]{:S(2)}, u32[]{:S(2)}) collective-permute-start(bf16[2,752,256]{2,1,0:T(8,128)(2,1)} %get-tuple-element.14), channel_id=1, source_target_pairs={{0,1},{1,2},{2,3},{4,5},{5,6},{6,7},{8,9},{9,10},{10,11},{12,13},{... | collective-permute-start | bytes 2310152 | tf_op jit(solution)/shard_map/ppermute | solution.py:200
  29.8 20.5 %collective-permute-start.3 = (bf16[2,752,256]{2,1,0:T(8,128)(2,1)}, bf16[2,752,256]{2,1,0:T(8,128)(2,1)}, u32[]{:S(2)}, u32[]{:S(2)}) collective-permute-start(bf16[2,752,256]{2,1,0:T(8,128)(2,1)} %get-tuple-element.13), channel_id=1, source_target_pairs={{1,0},{2,1},{3,2},{5,4},{6,5},{7,6},{9,8},{10,9},{11,10},{13,12},{... | collective-permute-start | bytes 2310152 | tf_op jit(solution)/shard_map/ppermute | solution.py:201
  37.4 11.7 %copy-start.19 = (s32[4096]{0:T(1024)S(1)}, s32[4096]{0:T(1024)}, u32[]{:S(2)}) copy-start(s32[4096]{0:T(1024)} %copy-done.18) | copy-start | bytes 49156
  37.5 11.7 %copy-start.21 = (s32[4096]{0:T(1024)S(1)}, s32[4096]{0:T(1024)}, u32[]{:S(2)}) copy-start(s32[4096]{0:T(1024)} %copy-done.20) | copy-start | bytes 49156
  37.5 11.7 %copy-start.22 = (s32[4096]{0:T(1024)S(1)}, s32[4096]{0:T(1024)}, u32[]{:S(2)}) copy-start(s32[4096]{0:T(1024)} %iota.202) | copy-start | bytes 49156
  37.5 11.7 %copy-start.23 = (bf16[36,40]{1,0:T(8,128)(2,1)S(1)}, bf16[36,40]{1,0:T(8,128)(2,1)}, u32[]{:S(2)}) copy-start(bf16[36,40]{1,0:T(8,128)(2,1)} %reshape.154) | copy-start | bytes 8644
  37.5 11.7 %copy-start.27 = (s32[40]{0:T(128)S(1)}, s32[40]{0:T(128)}, u32[]{:S(2)}) copy-start(s32[40]{0:T(128)} %copy-done.26) | copy-start | bytes 484
  37.5 11.7 %copy-start.29 = (s32[40]{0:T(128)S(1)}, s32[40]{0:T(128)}, u32[]{:S(2)}) copy-start(s32[40]{0:T(128)} %copy-done.28) | copy-start | bytes 484
  39.3 11.0 %copy-start.3 = (bf16[576,256]{1,0:T(8,128)(2,1)S(1)}, bf16[576,256]{1,0:T(8,128)(2,1)}, u32[]{:S(2)}) copy-start(bf16[576,256]{1,0:T(8,128)(2,1)} %reshape.152.rest_0_) | copy-start | bytes 884740
  39.3 11.0 %copy-start.4 = (bf16[32,2944]{1,0:T(8,128)(2,1)S(1)}, bf16[32,2944]{1,0:T(8,128)(2,1)}, u32[]{:S(2)}) copy-start(bf16[32,2944]{1,0:T(8,128)(2,1)} %mul.106.rest_5_) | copy-start | bytes 565252
  39.3 11.1 %copy-start.7 = (f32[256]{0:T(256)S(1)}, f32[256]{0:T(256)}, u32[]{:S(2)}) copy-start(f32[256]{0:T(256)} %param.19) | copy-start | bytes 3076
  50.3 24.2 %copy-start.10 = (f32[4,738]{1,0:T(4,128)S(1)}, f32[4,738]{1,0:T(4,128)}, u32[]{:S(2)}) copy-start(f32[4,738]{1,0:T(4,128)} %copy-done.9) | copy-start | bytes 35428
  50.3 24.2 %copy-start.12 = (f32[4,738]{1,0:T(4,128)S(1)}, f32[4,738]{1,0:T(4,128)}, u32[]{:S(2)}) copy-start(f32[4,738]{1,0:T(4,128)} %copy-done.11) | copy-start | bytes 35428
  68.4 24.5 %collective-permute-start.4 = (bf16[46,2,16,256]{3,2,1,0:T(8,128)(2,1)}, bf16[46,2,16,256]{3,2,1,0:T(8,128)(2,1)S(1)}, u32[]{:S(2)}, u32[]{:S(2)}) collective-permute-start(bf16[46,2,16,256]{3,2,1,0:T(8,128)(2,1)} %get-tuple-element.8.refs_2_), channel_id=1, source_target_pairs={{0,1},{1,2},{2,3},{4,5},{5,6},{6,7},{8,9},{9,10},{10,11},{12,13},{... | collective-permute-start | bytes 2261000 | tf_op jit(solution)/shard_map/ppermute | solution.py:263
  73.0 21.0 %collective-permute-start.5 = (bf16[46,2,16,256]{3,2,1,0:T(8,128)(2,1)}, bf16[46,2,16,256]{3,2,1,0:T(8,128)(2,1)}, u32[]{:S(2)}, u32[]{:S(2)}) collective-permute-start(bf16[46,2,16,256]{3,2,1,0:T(8,128)(2,1)} %get-tuple-element.9.refs_1_), channel_id=1, source_target_pairs={{1,0},{2,1},{3,2},{5,4},{6,5},{7,6},{9,8},{10,9},{11,10},{13,12},{... | collective-permute-start | bytes 2261000 | tf_op jit(solution)/shard_map/ppermute | solution.py:264
  80.2 12.3 %copy-start.2 = (bf16[2304,256]{1,0:T(8,128)(2,1)S(1)}, bf16[2304,256]{1,0:T(8,128)(2,1)}, u32[]{:S(2)}) copy-start(bf16[2304,256]{1,0:T(8,128)(2,1)} %refs_5_.1) | copy-start | bytes 3538948
  80.2 12.3 %copy-start.6 = (f32[4,9,2,4]{1,3,2,0:T(4,128)S(1)}, f32[4,9,2,4]{1,3,2,0:T(4,128)}, u32[]{:S(2)}) copy-start(f32[4,9,2,4]{1,3,2,0:T(4,128)} %param.16) | copy-start | bytes 3460
  84.1 10.0 %copy-start.8 = (f32[256]{0:T(256)S(1)}, f32[256]{0:T(256)}, u32[]{:S(2)}) copy-start(f32[256]{0:T(256)} %param.20) | copy-start | bytes 3076

commit v2 on v0

v2 whole, which is shorter than its diff:
```python
import functools
import math

import jax
import jax.numpy as jnp
import ml_dtypes
import numpy as np
from jax import lax
from jax.experimental import pallas as pl
from jax.experimental.pallas import tpu as pltpu
from jax.sharding import PartitionSpec as P

BLOCK = 16
EDGE = 4
TAPS = 5
FIRST_PARTS = 2
SECOND_PARTS = 3
VMEM_BYTES = 40 * 1024 * 1024
SMEM = pl.BlockSpec(memory_space=pltpu.SMEM)
VMEM = pl.BlockSpec(memory_space=pltpu.VMEM)


def vmem_params():
    return pltpu.CompilerParams(vmem_limit_bytes=VMEM_BYTES)


def wave_tables(sectors, sector_cols, rows, count):
    length = sectors * sector_cols
    cols = sector_cols + BLOCK
    first = np.array([-2, 0])[None, :, None] + sector_cols * np.arange(sectors)[:, None, None]
    place = (first + np.arange(cols)) % length
    phase = place[..., None] * np.arange(count) % length
    angles = phase * (2.0 * np.pi / length)
    waves = np.concatenate([np.cos(angles), np.sin(angles)], axis=-1).astype(np.float32)
    high = waves.astype(ml_dtypes.bfloat16).astype(np.float32)
    terms = np.concatenate([high, waves - high, high, np.zeros_like(high)], axis=-1)
    return np.tile(terms, rows).astype(ml_dtypes.bfloat16)


def taps_kernel(first, psi_ref, start_ref, width_ref, out_ref):
    rows = psi_ref.shape[0]
    width = out_ref.shape[1]
    basis = out_ref.shape[0] // (rows * BLOCK)
    first_row = lax.axis_index("lon") * rows
    source = lax.broadcasted_iota(jnp.int32, (32, TAPS * width), 0)
    lane = lax.broadcasted_iota(jnp.int32, (32, TAPS * width), 1)
    offset, height = lane // width, lane % (width // 2) // BLOCK
    r, q = source // TAPS, source % TAPS
    place_j = lax.broadcasted_iota(jnp.int32, (BLOCK, width), 0)
    place_l = lax.broadcasted_iota(jnp.int32, (BLOCK, width), 1)
    ahead = place_l // (width // 2) * BLOCK + place_l % BLOCK - place_j
    for i in range(rows):
        start, count = start_ref[first_row + i], width_ref[first_row + i]
        chosen = (r + i == height) & (start + q == offset - 2) & (q < count) & (source < TAPS * TAPS)
        chosen = jnp.where(chosen, 1.0, 0.0).astype(jnp.bfloat16)
        spread = jnp.dot(psi_ref[i], chosen, preferred_element_type=jnp.float32)
        for k in range(basis):
            taps = jnp.zeros((BLOCK, width), jnp.float32)
            for d in range(TAPS):
                row = spread[k : k + 1, d * width : (d + 1) * width]
                taps = jnp.where(ahead == first + d, row, taps)
            at = (k * rows + i) * BLOCK
            out_ref[at : at + BLOCK] = taps.astype(jnp.bfloat16)


def tap_matrix(psi, lon_start, lon_width, first):
    rows, basis = psi.shape[0], psi.shape[1]
    psi = psi.reshape(rows, basis, TAPS * TAPS)
    psi = jnp.pad(psi, ((0, 0), (0, 16 - basis), (0, 32 - TAPS * TAPS)))
    width = 2 * (rows + TAPS - 1) * BLOCK
    return pl.pallas_call(
        functools.partial(taps_kernel, first),
        out_shape=jax.ShapeDtypeStruct((basis * rows * BLOCK, width), jnp.bfloat16),
        in_specs=[VMEM, SMEM, SMEM],
        compiler_params=vmem_params(),
    )(psi, lon_start, lon_width)


def harmonic_rows(waves, row):
    part = lax.dot_general(waves, row, (((0,), (0,)), ((), ())), preferred_element_type=jnp.float32)
    return part[:8]


def packet_kernel(latent_ref, waves_ref, out_ref, edges_ref):
    rows, cols = latent_ref.shape[0], latent_ref.shape[1]
    even = lax.axis_index("lat") % 2 == 0
    waves = waves_ref[1, :cols]
    for i in range(rows):
        out_ref[8 * i : 8 * i + 8] = harmonic_rows(waves, latent_ref[i])
        left = latent_ref[i, :BLOCK].astype(jnp.float32)[:EDGE]
        right = latent_ref[i, cols - BLOCK :].astype(jnp.float32)[BLOCK - EDGE :]
        at = EDGE * i
        edges_ref[0, at : at + EDGE] = left
        edges_ref[1, at : at + EDGE] = right
        at += 8 * rows
        out_ref[at : at + EDGE] = jnp.where(even, right, left)


def sector_place():
    return lax.axis_index("lat"), lax.axis_size("lat")


def step_kernel(mask, packet_ref, got_ref, edges_ref, out_ref):
    lanes = packet_ref.shape[0] - edges_ref.shape[1]
    me, count = sector_place()
    to_right = (me ^ mask) == (me + 1) % count
    out_ref[:lanes] = packet_ref[:lanes] + got_ref[:lanes]
    out_ref[lanes:] = jnp.where(to_right, edges_ref[1], edges_ref[0])


def sides_kernel(masks, *refs):
    packet_ref, got_refs, (total_ref, upper_ref, lower_ref) = refs[0], refs[1:-3], refs[-3:]
    lanes = total_ref.shape[0]
    me, count = sector_place()
    total_ref[...] = packet_ref[:lanes] + got_refs[-1][:lanes]
    left = right = got_refs[0][lanes:]
    for mask, got_ref in zip(masks[1:], got_refs[1:]):
        left = jnp.where((me ^ mask) == (me + count - 1) % count, got_ref[lanes:], left)
        right = jnp.where((me ^ mask) == (me + 1) % count, got_ref[lanes:], right)
    blank = jnp.zeros((BLOCK - EDGE, left.shape[1]), jnp.float32)
    for i in range(4):
        own = slice(EDGE * i, EDGE * i + EDGE)
        out_ref = upper_ref if i < 2 else lower_ref
        out_ref[0, i % 2] = jnp.concatenate([blank, left[own]], axis=0).astype(jnp.bfloat16)
        out_ref[1, i % 2] = jnp.concatenate([right[own], blank], axis=0).astype(jnp.bfloat16)


def cycle_kernel(norm_factor, lat_total, total_ref, coef_ref, counts_ref, w_ref, out_ref):
    rows, basis = coef_ref.shape[0], coef_ref.shape[1]
    lanes, channels = total_ref.shape
    first_row = lax.axis_index("lon") * rows
    columns = []
    for i in range(rows):
        polar = (first_row + i < counts_ref[0]) | (first_row + i >= lat_total - counts_ref[1])
        columns.append(jnp.where(polar, coef_ref[i].T * norm_factor, 0.0))
    coefs = jnp.concatenate(columns, axis=0)
    total = total_ref[...]
    acc = jnp.zeros((2 * lanes, w_ref.shape[1]), jnp.float32)
    for k in range(basis):
        term = total * coefs[:, k : k + 1]
        high = term.astype(jnp.bfloat16)
        low = (term - high.astype(jnp.float32)).astype(jnp.bfloat16)
        acc += jnp.dot(
            jnp.concatenate([high, low], axis=0),
            w_ref[k * channels : (k + 1) * channels],
            preferred_element_type=jnp.float32,
        )
    mixed = acc[:lanes] + acc[lanes:]
    high = mixed.astype(jnp.bfloat16).astype(jnp.float32)
    low = mixed - high
    pieces = []
    for i in range(rows):
        own = slice(8 * i, 8 * i + 8)
        pieces += [high[own], high[own], low[own], jnp.zeros_like(low[own])]
    out_ref[...] = jnp.concatenate(pieces, axis=0).astype(jnp.bfloat16)


def group_values(start, count, half, taps_ref, w_ref, bias_ref, wave_block, cycle_ref, feat_ref, lift_ref):
    channels = w_ref.shape[1]
    basis = w_ref.shape[0] // channels
    slab = 4 * BLOCK
    lane = lax.broadcasted_iota(jnp.int32, (BLOCK, lift_ref.shape[1]), 1) // (lift_ref.shape[1] // 4)
    for t in range(count):
        window = jnp.concatenate([half(start, t), half(start, t + 1)], axis=0)
        feature = jnp.dot(taps_ref[...], window, preferred_element_type=jnp.float32)
        feature = feature.astype(jnp.bfloat16)
        for k in range(basis):
            feat_ref[t * slab : (t + 1) * slab, k * channels : (k + 1) * channels] = feature[
                k * slab : (k + 1) * slab
            ]
        waves = wave_block(start + t).astype(jnp.float32)
        lift = jnp.concatenate([jnp.where(lane == i, waves, 0.0) for i in range(4)], axis=0)
        lift_ref[t * slab : (t + 1) * slab] = lift.astype(jnp.bfloat16)
    size = count * slab
    mixed = jnp.dot(feat_ref[:size], w_ref[...], preferred_element_type=jnp.float32)
    mixed += jnp.dot(lift_ref[:size], cycle_ref[...], preferred_element_type=jnp.float32)
    return mixed + bias_ref[...]


def aligned(block):
    at = block * BLOCK
    return pl.ds(at if isinstance(at, int) else pl.multiple_of(at, BLOCK), BLOCK)


def first_kernel(groups, cut, up_ref, mid_ref, dn_ref, side_up_ref, side_upper_ref, side_lower_ref, side_dn_ref,
                 taps_ref, w_ref, bias_ref, waves_ref, cycle_ref,
                 top_a_ref, bot_a_ref, top_b_ref, bot_b_ref, harm_ref, feat_ref, lift_ref):
    rows, cols, channels = mid_ref.shape
    blocks = cols // BLOCK + 1

    def half(start, t):
        b = start + t
        if b in (0, blocks):
            side = 0 if b == 0 else 1
            parts = [ref[side] for ref in (side_up_ref, side_upper_ref, side_lower_ref, side_dn_ref)]
        else:
            parts = [ref[:, aligned(b - 1)] for ref in (up_ref, mid_ref, dn_ref)]
        return jnp.concatenate(parts, axis=0).reshape(8 * BLOCK, channels)

    start = 0
    for count in groups:
        mixed = group_values(start, count, half, taps_ref, w_ref, bias_ref, lambda b: waves_ref[0, aligned(b)],
                             cycle_ref, feat_ref, lift_ref)
        value = (0.5 * mixed * (1.0 + lax.erf(mixed * math.sqrt(0.5)))).astype(jnp.bfloat16)
        for t in range(count):
            b = start + t
            piece = value[t * 4 * BLOCK : (t + 1) * 4 * BLOCK].reshape(4, BLOCK, channels)
            if b <= cut:
                top_a_ref[b] = piece[:2]
                bot_a_ref[b] = piece[2:]
            if b >= cut:
                top_b_ref[b - cut] = piece[:2]
                bot_b_ref[b - cut] = piece[2:]
        start += count

    place = lax.broadcasted_iota(jnp.int32, (blocks * BLOCK, waves_ref.shape[2]), 0)
    inside = (place >= 2) & (place < 2 + cols)
    waves = jnp.where(inside, waves_ref[0].astype(jnp.float32), 0.0).astype(jnp.bfloat16)
    for i in range(rows):
        a_ref, b_ref = (top_a_ref, top_b_ref) if i < 2 else (bot_a_ref, bot_b_ref)
        row_a = a_ref[:cut, i % 2].reshape(cut * BLOCK, channels)
        row_b = b_ref[:, i % 2].reshape((blocks - cut) * BLOCK, channels)
        harm_ref[8 * i : 8 * i + 8] = harmonic_rows(waves[: cut * BLOCK], row_a) + harmonic_rows(
            waves[cut * BLOCK :], row_b
        )


def second_kernel(count, up_ref, top_ref, bot_ref, dn_ref, taps_ref, w_ref, bias_ref, waves_ref, cycle_ref, *refs):
    out_ref, feat_ref, lift_ref = refs[-3:]
    channels = top_ref.shape[3]

    def half(start, t):
        b = start + t
        parts = [ref[b] for ref in (up_ref, top_ref, bot_ref, dn_ref)]
        return jnp.concatenate(parts, axis=0).reshape(8 * BLOCK, channels)

    start = pl.program_id(0) * count
    mixed = group_values(start, count, half, taps_ref, w_ref, bias_ref,
                         lambda b: waves_ref[0, aligned(b - start)], cycle_ref, feat_ref, lift_ref)
    value = mixed.astype(jnp.bfloat16)
    for t in range(count):
        piece = value[t * 4 * BLOCK : (t + 1) * 4 * BLOCK].reshape(4, BLOCK, channels)
        out_ref[:, t * BLOCK : (t + 1) * BLOCK] = piece


def conv_cost(blocks, channels):
    macs = blocks * BLOCK * 4 * 18 * channels * channels
    return pl.CostEstimate(flops=4 * macs, bytes_accessed=8_000_000, transcendentals=0)


def swap(value, mask):
    return lax.ppermute(value, "lat", [(i, i ^ mask) for i in range(lax.axis_size("lat"))])


def body(
    latent,
    psi_one,
    psi_two,
    cycle_one,
    cycle_two,
    w_one,
    w_two,
    b_one,
    b_two,
    lon_start,
    lon_width,
    polar_counts,
):
    row_count, col_count, channels = latent.shape
    basis, harm_count = cycle_one.shape[1], cycle_one.shape[3]
    lat_total = row_count * lax.axis_size("lon")
    sectors = lax.axis_size("lat")
    norm_factor = (col_count * sectors) ** (-0.5)
    south = [(i, i + 1) for i in range(lax.axis_size("lon") - 1)]
    north = [(target, source) for source, target in south]
    out_blocks = col_count // BLOCK
    hid_blocks = out_blocks + 1
    lanes = row_count * 2 * harm_count
    masks = [2**t - 1 for t in range(1, sectors.bit_length())]
    tables = wave_tables(sectors, col_count, row_count, harm_count)
    waves = lax.dynamic_index_in_dim(jnp.asarray(tables), lax.axis_index("lat"), 0, keepdims=False)
    f32 = lambda *shape: jax.ShapeDtypeStruct(shape, jnp.float32)
    bf16 = lambda *shape: jax.ShapeDtypeStruct(shape, jnp.bfloat16)

    edge_rows = row_count * EDGE
    packet, edges = pl.pallas_call(
        packet_kernel,
        out_shape=(f32(lanes + edge_rows, channels), f32(2, edge_rows, channels)),
        compiler_params=vmem_params(),
    )(latent, waves)
    up = lax.ppermute(latent[2:], "lon", south)
    down = lax.ppermute(latent[:2], "lon", north)
    gots = [swap(packet, masks[0])]
    for mask in masks[1:]:
        packet = pl.pallas_call(
            functools.partial(step_kernel, mask),
            out_shape=f32(*packet.shape),
            compiler_params=vmem_params(),
        )(packet, gots[-1], edges)
        gots.append(swap(packet, mask))
    side = bf16(2, 2, BLOCK, channels)
    total_one, side_upper, side_lower = pl.pallas_call(
        functools.partial(sides_kernel, masks),
        out_shape=(f32(lanes, channels), side, side),
        compiler_params=vmem_params(),
    )(packet, *gots)
    side_up = lax.ppermute(side_lower, "lon", south)
    side_down = lax.ppermute(side_upper, "lon", north)

    def cycle_mix(total, cycle, w):
        return pl.pallas_call(
            functools.partial(cycle_kernel, norm_factor, lat_total),
            out_shape=bf16(row_count * 32, channels),
            in_specs=[VMEM, VMEM, SMEM, VMEM],
            compiler_params=vmem_params(),
        )(total, cycle.reshape(row_count, basis, 2 * harm_count), polar_counts, w)

    def scratch(count):
        size = count * row_count * BLOCK
        return [
            pltpu.VMEM((size, basis * channels), jnp.bfloat16),
            pltpu.VMEM((size, row_count * 32), jnp.bfloat16),
        ]

    taps_one = tap_matrix(psi_one, lon_start, lon_width, BLOCK - EDGE)
    mix_one = cycle_mix(total_one, cycle_one, w_one)
    part = -(-hid_blocks // FIRST_PARTS)
    groups = [min(part, hid_blocks - at) for at in range(0, hid_blocks, part)]
    tail = out_blocks // SECOND_PARTS
    cut = out_blocks - tail
    hid_a = bf16(cut + 1, 2, BLOCK, channels)
    hid_b = bf16(hid_blocks - cut, 2, BLOCK, channels)
    top_a, bot_a, top_b, bot_b, part_two = pl.pallas_call(
        functools.partial(first_kernel, groups, cut),
        out_shape=(hid_a, hid_a, hid_b, hid_b, f32(lanes, channels)),
        scratch_shapes=scratch(part),
        compiler_params=vmem_params(),
        cost_estimate=conv_cost(hid_blocks, channels),
    )(up, latent, down, side_up, side_upper, side_lower, side_down, taps_one, w_one, b_one[None], waves, mix_one)

    up_a = lax.ppermute(bot_a, "lon", south)
    down_a = lax.ppermute(top_a, "lon", north)
    up_b = lax.ppermute(bot_b, "lon", south)
    down_b = lax.ppermute(top_b, "lon", north)
    total_two = part_two
    for mask in masks:
        total_two = total_two + swap(total_two, mask)
    psi_two, _ = lax.optimization_barrier((psi_two, part_two))
    taps_two = tap_matrix(psi_two, lon_start, lon_width, 0)
    mix_two = cycle_mix(total_two, cycle_two, w_two)

    def second(first, steps, sources, result):
        count = tail
        whole = lambda value: pl.BlockSpec(value.shape, lambda s: (0,) * value.ndim)
        operands = list(sources) + [taps_two, w_two, b_two[None], waves, mix_two]
        in_specs = [whole(value) for value in operands]
        in_specs[-2] = pl.BlockSpec((1, count * BLOCK, waves.shape[2]), lambda s: (1, first + s, 0))
        aliases = {}
        if result is not None:
            aliases = {len(operands): 0}
            operands.append(result)
            in_specs.append(pl.BlockSpec(memory_space=pl.ANY))
        return pl.pallas_call(
            functools.partial(second_kernel, count),
            grid=(steps,),
            out_shape=bf16(row_count, col_count, channels),
            in_specs=in_specs,
            out_specs=pl.BlockSpec((row_count, count * BLOCK, channels), lambda s: (0, first + s, 0)),
            input_output_aliases=aliases,
            scratch_shapes=scratch(count),
            compiler_params=vmem_params(),
            cost_estimate=conv_cost(count * steps, channels),
        )(*operands)

    steps = SECOND_PARTS - 1
    result = second(0, steps, (up_a, top_a, bot_a, down_a), None)
    return second(steps, 1, (up_b, top_b, bot_b, down_b), result)


def solution(mesh):
    return jax.shard_map(
        body,
        mesh=mesh,
        in_specs=(
            P("lon", "lat", None),
            P("lon", None, None, None),
            P("lon", None, None, None),
            P("lon", None, None, None),
            P("lon", None, None, None),
            P(),
            P(),
            P(),
            P(),
            P(),
            P(),
            P(),
        ),
        out_specs=P("lon", "lat", None),
        check_vma=False,
    )
```

time: 463 us -> 76.1 us (0.16); the launches traced: 455 us -> 75.6 us
  matrix products: 323 us -> 0 us
  blocking collectives: 46.6 us -> 0 us
  local copies, waits for them, and re-layouts: 49.6 us -> 7.44 us
  Pallas kernels: 0 us -> 25.3 us
  other arithmetic: 17 us -> 0.02 us
  starting transfers between devices: 16.6 us -> 31.4 us
  waiting for transfers between devices: 0.02 us -> 11.1 us
    dot_general x38 -> x0, matrix products: 323 us -> none  [the longest x8 101 us: convolve(): jnp.einsum('krd,rdjc->kjc', tap_cube[row], window, preferred_element_type...]
    psum x2 -> x0, blocking collectives: 46.6 us -> none  [cycle_harmonics(): cos_part, sin_part = lax.psum((cos_local, sin_local), 'lat')]
    slice x8 -> x1, local copies, waits for them, and re-layouts: 39.9 us -> 2.66 us  [body(): down = lax.ppermute(latent[:2], 'lon', north)]
    pallas_call x0 -> x11, Pallas kernels: none -> 25.3 us  [the longest x2 11 us: second(): pl.pallas_call(functools.partial(second_kernel, count), grid=(steps,), ou...]
    ppermute x8 -> x14, starting transfers between devices: 16.6 us -> 31.4 us  [the longest x6 7.9 us: swap(): lax.ppermute(value, 'lat', [(i, i ^ mask) for i in range(lax.axis_size('l...]
    ppermute x8 -> x14, waiting for transfers between devices: 0.02 us -> 11.1 us  [the longest x6 8.76 us: swap(): lax.ppermute(value, 'lat', [(i, i ^ mask) for i in range(lax.axis_size('l...]
    convert_element_type x3 -> x0, other arithmetic: 8.56 us -> none  [the longest x1 6.58 us: body(): hidden = jax.nn.gelu(before, approximate=False).astype(jnp.bfloat16)]
  transfers between devices with their start and end apart: 8 -> 14, of which waited for: 0 -> 6; matrix products, arithmetic and copies ran while one was open for 30% -> 2% of each run, Pallas kernels for 0% -> 15%
where the time goes in v2:
time: 76.1 us; the launch traced here: 75.6 us
  starting transfers between devices  31.4 us (41%)
  Pallas kernels  25.3 us (33%)
  waiting for transfers between devices  11.1 us (15%)
  local copies, waits for them, and re-layouts  7.44 us (10%)
    pallas_call x2, Pallas kernels, second(): pl.pallas_call(functools.partial(second_kernel, count), grid=(steps,), ou...  11 us
    pallas_call x1, Pallas kernels, body(): pl.pallas_call(functools.partial(first_kernel, groups, cut), out_shape=(h...  10.1 us
    ppermute x6, waiting for transfers between devices, swap(): lax.ppermute(value, 'lat', [(i, i ^ mask) for i in range(lax.axis_size('l...  8.76 us
    ppermute x6, starting transfers between devices, swap(): lax.ppermute(value, 'lat', [(i, i ^ mask) for i in range(lax.axis_size('l...  7.9 us
    ppermute x1, starting transfers between devices, body(): up = lax.ppermute(latent[2:], 'lon', south)  5.81 us
    ppermute x1, starting transfers between devices, body(): up_b = lax.ppermute(bot_b, 'lon', south)  4.56 us
    ppermute x1, starting transfers between devices, body(): side_up = lax.ppermute(side_lower, 'lon', south)  4.55 us
    unnamed x32, local copies, waits for them, and re-layouts  3.29 us
  transfers between devices with their start and end apart: 14, of which 6 were waited for; matrix products, arithmetic and copies ran while one was open for 2% of the time, Pallas kernels for 15%

profile of v2, /device:TPU:0, one launch (start us, length us, event | category | flops | bytes accessed | tf_op | source)
XLA Modules:
  0.0 75.6 jit_solution(4921055088573685493)
XLA Ops:
  0.0 2.7 %fusion = (bf16[2,720,256]{2,1,0:T(8,128)(2,1)}, bf16[2,720,256]{2,1,0:T(8,128)(2,1)}) fusion(bf16[4,720,256]{2,1,0:T(8,128)(2,1)} %mid_ref.1), kind=kLoop, calls=%fused_computation.1 | loop fusion | bytes 2949120 | tf_op jit(solution)/shard_map/slice | solution.py:292
  2.7 5.8 %collective-permute-start = (bf16[2,720,256]{2,1,0:T(8,128)(2,1)}, bf16[2,720,256]{2,1,0:T(8,128)(2,1)}, u32[]{:S(2)}, u32[]{:S(2)}) collective-permute-start(bf16[2,720,256]{2,1,0:T(8,128)(2,1)} %get-tuple-element.28), channel_id=1, source_target_pairs={{0,1},{1,2},{2,3},{4,5},{5,6},{6,7},{8,9},{9,10},{10,11},{12,13},{... | collective-permute-start | bytes 2211848 | tf_op jit(solution)/shard_map/ppermute | solution.py:291
  8.5 1.3 %collective-permute-start.1 = (bf16[2,720,256]{2,1,0:T(8,128)(2,1)}, bf16[2,720,256]{2,1,0:T(8,128)(2,1)}, u32[]{:S(2)}, u32[]{:S(2)}) collective-permute-start(bf16[2,720,256]{2,1,0:T(8,128)(2,1)} %get-tuple-element.27), channel_id=1, source_target_pairs={{1,0},{2,1},{3,2},{5,4},{6,5},{7,6},{9,8},{10,9},{11,10},{13,12},{... | collective-permute-start | bytes 2211848 | tf_op jit(solution)/shard_map/ppermute | solution.py:292
  9.8 0.0 copy-start.14
  9.8 0.0 copy-start.12
  9.8 0.0 copy-start.5
  9.8 0.0 copy-start.6
  9.8 1.0 %dynamic-slice_bitcast_fusion.waves_ref = bf16[2,736,128]{2,1,0:T(8,128)(2,1)S(1)} fusion(bf16[8,2,736,128]{3,2,1,0:T(8,128)(2,1)} %constant.17.clone, s32[]{:T(128)S(6)} %select_n.4), kind=kLoop, calls=%fused_computation | loop fusion | bytes 753668 | tf_op jit(solution)/shard_map/jit(dynamic_index_in_dim)/squeeze | solution.py:281
  10.9 0.0 copy-start.1
  10.9 0.0 copy-start.7
  10.9 0.4 shard_map.127
  11.3 0.0 copy-start.10
  11.3 0.1 collective-permute-start.2
  11.4 1.2 %collective-permute-done.2.got_ref.refs_1_ = f32[48,256]{1,0:T(8,128)S(1)} collective-permute-done((f32[48,256]{1,0:T(8,128)S(1)}, f32[48,256]{1,0:T(8,128)S(1)}, u32[]{:S(2)}, u32[]{:S(2)}) %collective-permute-start.2) | collective-permute-done | bytes 49184 | tf_op jit(solution)/shard_map/ppermute | solution.py:252
  12.6 1.3 %collective-permute-start.3 = (f32[48,256]{1,0:T(8,128)S(1)}, f32[48,256]{1,0:T(8,128)S(1)}, u32[]{:S(2)}, u32[]{:S(2)}) collective-permute-start(f32[48,256]{1,0:T(8,128)S(1)} %shard_map.128.packet_ref), channel_id=1, source_target_pairs={{0,12},{4,8},{8,4},{12,0},{16,28},{20,24},{24,20},{28,16},{1,13},{... | collective-permute-start | bytes 147464 | tf_op jit(solution)/shard_map/ppermute | solution.py:252
  13.9 2.5 %collective-permute-done.3.got_ref.refs_2_ = f32[48,256]{1,0:T(8,128)S(1)} collective-permute-done((f32[48,256]{1,0:T(8,128)S(1)}, f32[48,256]{1,0:T(8,128)S(1)}, u32[]{:S(2)}, u32[]{:S(2)}) %collective-permute-start.3) | collective-permute-done | bytes 49184 | tf_op jit(solution)/shard_map/ppermute | solution.py:252
  16.4 2.7 %collective-permute-start.4 = (f32[48,256]{1,0:T(8,128)S(1)}, f32[48,256]{1,0:T(8,128)S(1)}, u32[]{:S(2)}, u32[]{:S(2)}) collective-permute-start(f32[48,256]{1,0:T(8,128)S(1)} %shard_map.129.refs_0_), channel_id=1, source_target_pairs={{0,28},{4,24},{8,20},{12,16},{16,12},{20,8},{24,4},{28,0},{1,29},{... | collective-permute-start | bytes 147464 | tf_op jit(solution)/shard_map/ppermute | solution.py:252
  19.1 1.8 %collective-permute-done.4.refs_3_ = f32[48,256]{1,0:T(8,128)S(1)} collective-permute-done((f32[48,256]{1,0:T(8,128)S(1)}, f32[48,256]{1,0:T(8,128)S(1)}, u32[]{:S(2)}, u32[]{:S(2)}) %collective-permute-start.4) | collective-permute-done | bytes 49184 | tf_op jit(solution)/shard_map/ppermute | solution.py:252
  20.9 4.6 %collective-permute-start.5 = (bf16[2,2,16,256]{3,2,1,0:T(8,128)(2,1)S(1)}, bf16[2,2,16,256]{3,2,1,0:T(8,128)(2,1)S(1)}, u32[]{:S(2)}, u32[]{:S(2)}) collective-permute-start(bf16[2,2,16,256]{3,2,1,0:T(8,128)(2,1)S(1)} %get-tuple-element.18.side_lower_ref), channel_id=1, source_target_pairs={{0,1},{1,2},{2,3},{4,5},{5,6},{6,7},{8,9},{9,10},{10,11},{12,13},{... | collective-permute-start | bytes 98312 | tf_op jit(solution)/shard_map/ppermute | solution.py:307
  25.5 1.3 %collective-permute-start.6 = (bf16[2,2,16,256]{3,2,1,0:T(8,128)(2,1)S(1)}, bf16[2,2,16,256]{3,2,1,0:T(8,128)(2,1)S(1)}, u32[]{:S(2)}, u32[]{:S(2)}) collective-permute-start(bf16[2,2,16,256]{3,2,1,0:T(8,128)(2,1)S(1)} %get-tuple-element.19.side_upper_ref), channel_id=1, source_target_pairs={{1,0},{2,1},{3,2},{5,4},{6,5},{7,6},{9,8},{10,9},{11,10},{13,12},{... | collective-permute-start | bytes 98312 | tf_op jit(solution)/shard_map/ppermute | solution.py:308
  26.8 0.1 copy.20.coef_ref
  26.9 0.1 copy.19
  27.0 0.9 %shard_map.131.taps_ref = bf16[576,256]{1,0:T(8,128)(2,1)S(1)} custom-call(bf16[4,16,32]{2,1,0:T(8,128)(2,1)S(1)} %pad.7.psi_ref, s32[16]{0:T(128)S(1)} %copy-done.5, s32[16]{0:T(128)S(1)} %copy-done.6), custom_call_target="tpu_custom_call" | custom-call | tf_op jit(solution)/shard_map/pallas_call | solution.py:71
  27.9 1.0 %shard_map.132.cycle_ref = bf16[128,256]{1,0:T(8,128)(2,1)S(1)} custom-call(f32[32,256]{1,0:T(8,128)S(1)} %get-tuple-element.20.total_ref, f32[4,9,8]{2,1,0:T(8,128)S(1)} %copy.20.coef_ref, s32[2]{0:T(128)S(1)} %copy-done.7, bf16[2304,256]{1,0:T(8,128)(2,1)S(1)} %copy-done.1), custom_call_target="tpu_custom_call" | custom-call | tf_op jit(solution)/shard_map/pallas_call | solution.py:311
  28.9 2.3 %collective-permute-done.6.side_dn_ref = bf16[2,2,16,256]{3,2,1,0:T(8,128)(2,1)S(1)} collective-permute-done((bf16[2,2,16,256]{3,2,1,0:T(8,128)(2,1)S(1)}, bf16[2,2,16,256]{3,2,1,0:T(8,128)(2,1)S(1)}, u32[]{:S(2)}, u32[]{:S(2)}) %collective-permute-start.6) | collective-permute-done | bytes 32800 | tf_op jit(solution)/shard_map/ppermute | solution.py:308
  31.3 0.0 copy-start.15
  31.3 0.0 copy-start.13
  31.3 10.1 %shard_map.133 = (bf16[31,2,16,256]{3,2,1,0:T(8,128)(2,1)}, bf16[31,2,16,256]{3,2,1,0:T(8,128)(2,1)}, bf16[16,2,16,256]{3,2,1,0:T(8,128)(2,1)S(1)}, bf16[16,2,16,256]{3,2,1,0:T(8,128)(2,1)S(1)}, f32[32,256]{1,0:T(8,128)S(1)}) custom-call(bf16[2,720,256]{2,1,0:T(8,128)(2,1)} %collective-permute-done.up_ref, bf16[4,720,256]{2,1,0:T(8,128)(2,1)S(1)} %copy-done, ...), custom_call_target="tpu_custom_call" | custom-call | flops 13891534848 | bytes 8000000 | tf_op jit(solution)/shard_map/pallas_call | solution.py:333
  41.4 0.7 copy-done.8
  42.1 3.2 %collective-permute-start.12 = (bf16[31,2,16,256]{3,2,1,0:T(8,128)(2,1)}, bf16[31,2,16,256]{3,2,1,0:T(8,128)(2,1)S(1)}, u32[]{:S(2)}, u32[]{:S(2)}) collective-permute-start(bf16[31,2,16,256]{3,2,1,0:T(8,128)(2,1)} %get-tuple-element.25.bot_ref), channel_id=1, source_target_pairs={{0,1},{1,2},{2,3},{4,5},{5,6},{6,7},{8,9},{9,10},{10,11},{12,13},{... | collective-permute-start | bytes 1523720 | tf_op jit(solution)/shard_map/ppermute | solution.py:341
  45.3 1.3 %collective-permute-start.13 = (bf16[31,2,16,256]{3,2,1,0:T(8,128)(2,1)}, bf16[31,2,16,256]{3,2,1,0:T(8,128)(2,1)S(1)}, u32[]{:S(2)}, u32[]{:S(2)}) collective-permute-start(bf16[31,2,16,256]{3,2,1,0:T(8,128)(2,1)} %get-tuple-element.26.top_ref), channel_id=1, source_target_pairs={{1,0},{2,1},{3,2},{5,4},{6,5},{7,6},{9,8},{10,9},{11,10},{13,12},{... | collective-permute-start | bytes 1523720 | tf_op jit(solution)/shard_map/ppermute | solution.py:342
  46.6 0.1 collective-permute-start.9
  46.7 1.2 %collective-permute-done.9 = f32[32,256]{1,0:T(8,128)S(1)} collective-permute-done((f32[32,256]{1,0:T(8,128)S(1)}, f32[32,256]{1,0:T(8,128)S(1)}, u32[]{:S(2)}, u32[]{:S(2)}) %collective-permute-start.9) | collective-permute-done | bytes 32800 | tf_op jit(solution)/shard_map/ppermute | solution.py:252
  47.9 1.3 %collective-permute-start.10 = (f32[32,256]{1,0:T(8,128)S(1)}, f32[32,256]{1,0:T(8,128)S(1)}, u32[]{:S(2)}, u32[]{:S(2)}) collective-permute-start(f32[32,256]{1,0:T(8,128)S(1)} %add.18), channel_id=1, source_target_pairs={{0,12},{4,8},{8,4},{12,0},{16,28},{20,24},{24,20},{28,16},{1,13},{... | collective-permute-start | bytes 98312 | tf_op jit(solution)/shard_map/ppermute | solution.py:252
  49.2 2.1 %collective-permute-done.10 = f32[32,256]{1,0:T(8,128)S(1)} collective-permute-done((f32[32,256]{1,0:T(8,128)S(1)}, f32[32,256]{1,0:T(8,128)S(1)}, u32[]{:S(2)}, u32[]{:S(2)}) %collective-permute-start.10) | collective-permute-done | bytes 32800 | tf_op jit(solution)/shard_map/ppermute | solution.py:252
  51.3 2.5 %collective-permute-start.11 = (f32[32,256]{1,0:T(8,128)S(1)}, f32[32,256]{1,0:T(8,128)S(1)}, u32[]{:S(2)}, u32[]{:S(2)}) collective-permute-start(f32[32,256]{1,0:T(8,128)S(1)} %add.19), channel_id=1, source_target_pairs={{0,28},{4,24},{8,20},{12,16},{16,12},{20,8},{24,4},{28,0},{1,29},{... | collective-permute-start | bytes 98312 | tf_op jit(solution)/shard_map/ppermute | solution.py:252
  53.8 0.1 copy.22.coef_ref
  53.9 0.1 copy.21
  54.0 0.9 %shard_map.134.taps_ref = bf16[576,256]{1,0:T(8,128)(2,1)S(1)} custom-call(bf16[4,16,32]{2,1,0:T(8,128)(2,1)S(1)} %pad.8.psi_ref, s32[16]{0:T(128)S(1)} %copy-done.5, s32[16]{0:T(128)S(1)} %copy-done.6), custom_call_target="tpu_custom_call" | custom-call | tf_op jit(solution)/shard_map/pallas_call | solution.py:71
  54.9 4.6 %collective-permute-start.7 = (bf16[16,2,16,256]{3,2,1,0:T(8,128)(2,1)}, bf16[16,2,16,256]{3,2,1,0:T(8,128)(2,1)S(1)}, u32[]{:S(2)}, u32[]{:S(2)}) collective-permute-start(bf16[16,2,16,256]{3,2,1,0:T(8,128)(2,1)} %copy-done.8), channel_id=1, source_target_pairs={{0,1},{1,2},{2,3},{4,5},{5,6},{6,7},{8,9},{9,10},{10,11},{12,13},{... | collective-permute-start | bytes 786440 | tf_op jit(solution)/shard_map/ppermute | solution.py:343
  59.5 1.5 %collective-permute-start.8 = (bf16[16,2,16,256]{3,2,1,0:T(8,128)(2,1)S(1)}, bf16[16,2,16,256]{3,2,1,0:T(8,128)(2,1)S(1)}, u32[]{:S(2)}, u32[]{:S(2)}) collective-permute-start(bf16[16,2,16,256]{3,2,1,0:T(8,128)(2,1)S(1)} %get-tuple-element.22.top_ref), channel_id=1, source_target_pairs={{1,0},{2,1},{3,2},{5,4},{6,5},{7,6},{9,8},{10,9},{11,10},{13,12},{... | collective-permute-start | bytes 786440 | tf_op jit(solution)/shard_map/ppermute | solution.py:344
  61.0 0.0 copy-start.2
  61.0 1.3 %copy-done.2 = bf16[2304,256]{1,0:T(8,128)(2,1)S(1)} copy-done((bf16[2304,256]{1,0:T(8,128)(2,1)S(1)}, bf16[2304,256]{1,0:T(8,128)(2,1)}, u32[]{:S(2)}) %copy-start.2) | copy-done | bytes 1179672
  62.3 1.0 %shard_map.135.cycle_ref = bf16[128,256]{1,0:T(8,128)(2,1)S(1)} custom-call(f32[32,256]{1,0:T(8,128)S(1)} %add.20.total_ref, f32[4,9,8]{2,1,0:T(8,128)S(1)} %copy.22.coef_ref, s32[2]{0:T(128)S(1)} %copy-done.7, bf16[2304,256]{1,0:T(8,128)(2,1)S(1)} %copy-done.2), custom_call_target="tpu_custom_call" | custom-call | tf_op jit(solution)/shard_map/pallas_call | solution.py:311
  63.3 0.0 copy-start.3
  63.3 1.3 %copy-done.3 = bf16[2304,256]{1,0:T(8,128)(2,1)S(1)} copy-done((bf16[2304,256]{1,0:T(8,128)(2,1)S(1)}, bf16[2304,256]{1,0:T(8,128)(2,1)}, u32[]{:S(2)}) %copy-start.3) | copy-done | bytes 1179672
  64.6 7.5 %shard_map.136.refs_0_ = bf16[4,720,256]{2,1,0:T(8,128)(2,1)} custom-call(bf16[31,2,16,256]{3,2,1,0:T(8,128)(2,1)S(1)} %collective-permute-done.12.up_ref, bf16[31,2,16,256]{3,2,1,0:T(8,128)(2,1)} %get-tuple-element.26.top_ref, bf16[31,2,16,256]{3,2,1,0:T(8,128)(2,1)} %get-tuple-element.25.bot_ref, ...), custom_call_target="tpu_custom_call" | custom-call | flops 9059696640 | bytes 8000000 | tf_op jit(solution)/shard_map/pallas_call | solution.py:363
  72.1 3.5 %shard_map.137 = bf16[4,720,256]{2,1,0:T(8,128)(2,1)} custom-call(bf16[16,2,16,256]{3,2,1,0:T(8,128)(2,1)S(1)} %collective-permute-done.7.up_ref, bf16[16,2,16,256]{3,2,1,0:T(8,128)(2,1)S(1)} %get-tuple-element.22.top_ref, bf16[16,2,16,256]{3,2,1,0:T(8,128)(2,1)S(1)} %copy-done.9, ...), custom_call_target="tpu_custom_call", output_to_operand_aliasing={{}: (9, {})} | custom-call | flops 4529848320 | bytes 8000000 | tf_op jit(solution)/shard_map/pallas_call | solution.py:363
  (34 shorter events, 0.1 us)
Async XLA Ops:
  0.0 10.9 %copy-start = (bf16[4,720,256]{2,1,0:T(8,128)(2,1)S(1)}, bf16[4,720,256]{2,1,0:T(8,128)(2,1)}, u32[]{:S(2)}) copy-start(bf16[4,720,256]{2,1,0:T(8,128)(2,1)} %mid_ref.1) | copy-start | bytes 4423684
  2.7 28.6 %collective-permute-start = (bf16[2,720,256]{2,1,0:T(8,128)(2,1)}, bf16[2,720,256]{2,1,0:T(8,128)(2,1)}, u32[]{:S(2)}, u32[]{:S(2)}) collective-permute-start(bf16[2,720,256]{2,1,0:T(8,128)(2,1)} %get-tuple-element.28), channel_id=1, source_target_pairs={{0,1},{1,2},{2,3},{4,5},{5,6},{6,7},{8,9},{9,10},{10,11},{12,13},{... | collective-permute-start | bytes 2211848 | tf_op jit(solution)/shard_map/ppermute | solution.py:291
  8.5 22.8 %collective-permute-start.1 = (bf16[2,720,256]{2,1,0:T(8,128)(2,1)}, bf16[2,720,256]{2,1,0:T(8,128)(2,1)}, u32[]{:S(2)}, u32[]{:S(2)}) collective-permute-start(bf16[2,720,256]{2,1,0:T(8,128)(2,1)} %get-tuple-element.27), channel_id=1, source_target_pairs={{1,0},{2,1},{3,2},{5,4},{6,5},{7,6},{9,8},{10,9},{11,10},{13,12},{... | collective-permute-start | bytes 2211848 | tf_op jit(solution)/shard_map/ppermute | solution.py:292
  9.8 17.0 %copy-start.14 = (f32[4,9,2,4]{1,3,2,0:T(4,128)S(1)}, f32[4,9,2,4]{1,3,2,0:T(4,128)}, u32[]{:S(2)}) copy-start(f32[4,9,2,4]{1,3,2,0:T(4,128)} %param.16) | copy-start | bytes 3460
  9.8 17.1 %copy-start.12 = (bf16[4,9,5,5]{1,0,3,2:T(4,128)(2,1)S(1)}, bf16[4,9,5,5]{1,0,3,2:T(4,128)(2,1)}, u32[]{:S(2)}) copy-start(bf16[4,9,5,5]{1,0,3,2:T(4,128)(2,1)} %param.14) | copy-start | bytes 5404
  9.8 17.2 %copy-start.5 = (s32[16]{0:T(128)S(1)}, s32[16]{0:T(128)}, u32[]{:S(2)}) copy-start(s32[16]{0:T(128)} %start_ref.3) | copy-start | bytes 196
  9.8 17.2 %copy-start.6 = (s32[16]{0:T(128)S(1)}, s32[16]{0:T(128)}, u32[]{:S(2)}) copy-start(s32[16]{0:T(128)} %width_ref.3) | copy-start | bytes 196
  10.9 17.1 %copy-start.1 = (bf16[2304,256]{1,0:T(8,128)(2,1)S(1)}, bf16[2304,256]{1,0:T(8,128)(2,1)}, u32[]{:S(2)}) copy-start(bf16[2304,256]{1,0:T(8,128)(2,1)} %w_ref.6) | copy-start | bytes 3538948
  10.9 17.1 %copy-start.7 = (s32[2]{0:T(128)S(1)}, s32[2]{0:T(128)}, u32[]{:S(2)}) copy-start(s32[2]{0:T(128)} %counts_ref.3) | copy-start | bytes 28
  11.3 20.0 %copy-start.10 = (f32[256]{0:T(256)S(1)}, f32[256]{0:T(256)}, u32[]{:S(2)}) copy-start(f32[256]{0:T(256)} %param.20) | copy-start | bytes 3076
  11.3 1.3 %collective-permute-start.2 = (f32[48,256]{1,0:T(8,128)S(1)}, f32[48,256]{1,0:T(8,128)S(1)}, u32[]{:S(2)}, u32[]{:S(2)}) collective-permute-start(f32[48,256]{1,0:T(8,128)S(1)} %get-tuple-element.16.packet_ref), channel_id=1, source_target_pairs={{0,4},{4,0},{8,12},{12,8},{16,20},{20,16},{24,28},{28,24},{1,5},{5... | collective-permute-start | bytes 147464 | tf_op jit(solution)/shard_map/ppermute | solution.py:252
  12.6 3.8 %collective-permute-start.3 = (f32[48,256]{1,0:T(8,128)S(1)}, f32[48,256]{1,0:T(8,128)S(1)}, u32[]{:S(2)}, u32[]{:S(2)}) collective-permute-start(f32[48,256]{1,0:T(8,128)S(1)} %shard_map.128.packet_ref), channel_id=1, source_target_pairs={{0,12},{4,8},{8,4},{12,0},{16,28},{20,24},{24,20},{28,16},{1,13},{... | collective-permute-start | bytes 147464 | tf_op jit(solution)/shard_map/ppermute | solution.py:252
  16.4 4.5 %collective-permute-start.4 = (f32[48,256]{1,0:T(8,128)S(1)}, f32[48,256]{1,0:T(8,128)S(1)}, u32[]{:S(2)}, u32[]{:S(2)}) collective-permute-start(f32[48,256]{1,0:T(8,128)S(1)} %shard_map.129.refs_0_), channel_id=1, source_target_pairs={{0,28},{4,24},{8,20},{12,16},{16,12},{20,8},{24,4},{28,0},{1,29},{... | collective-permute-start | bytes 147464 | tf_op jit(solution)/shard_map/ppermute | solution.py:252
  20.9 8.0 %collective-permute-start.5 = (bf16[2,2,16,256]{3,2,1,0:T(8,128)(2,1)S(1)}, bf16[2,2,16,256]{3,2,1,0:T(8,128)(2,1)S(1)}, u32[]{:S(2)}, u32[]{:S(2)}) collective-permute-start(bf16[2,2,16,256]{3,2,1,0:T(8,128)(2,1)S(1)} %get-tuple-element.18.side_lower_ref), channel_id=1, source_target_pairs={{0,1},{1,2},{2,3},{4,5},{5,6},{6,7},{8,9},{9,10},{10,11},{12,13},{... | collective-permute-start | bytes 98312 | tf_op jit(solution)/shard_map/ppermute | solution.py:307
  25.5 5.8 %collective-permute-start.6 = (bf16[2,2,16,256]{3,2,1,0:T(8,128)(2,1)S(1)}, bf16[2,2,16,256]{3,2,1,0:T(8,128)(2,1)S(1)}, u32[]{:S(2)}, u32[]{:S(2)}) collective-permute-start(bf16[2,2,16,256]{3,2,1,0:T(8,128)(2,1)S(1)} %get-tuple-element.19.side_upper_ref), channel_id=1, source_target_pairs={{1,0},{2,1},{3,2},{5,4},{6,5},{7,6},{9,8},{10,9},{11,10},{13,12},{... | collective-permute-start | bytes 98312 | tf_op jit(solution)/shard_map/ppermute | solution.py:308
  31.3 22.5 %copy-start.15 = (f32[4,9,2,4]{1,3,2,0:T(4,128)S(1)}, f32[4,9,2,4]{1,3,2,0:T(4,128)}, u32[]{:S(2)}) copy-start(f32[4,9,2,4]{1,3,2,0:T(4,128)} %param.17) | copy-start | bytes 3460
  31.3 22.6 %copy-start.13 = (bf16[4,9,5,5]{1,0,3,2:T(4,128)(2,1)S(1)}, bf16[4,9,5,5]{1,0,3,2:T(4,128)(2,1)}, u32[]{:S(2)}) copy-start(bf16[4,9,5,5]{1,0,3,2:T(4,128)(2,1)} %param.15) | copy-start | bytes 5404
  41.4 0.7 copy-start.8
  42.1 21.2 %copy-start.11 = (f32[256]{0:T(256)S(1)}, f32[256]{0:T(256)}, u32[]{:S(2)}) copy-start(f32[256]{0:T(256)} %param.21) | copy-start | bytes 3076
  42.1 21.1 %collective-permute-start.12 = (bf16[31,2,16,256]{3,2,1,0:T(8,128)(2,1)}, bf16[31,2,16,256]{3,2,1,0:T(8,128)(2,1)S(1)}, u32[]{:S(2)}, u32[]{:S(2)}) collective-permute-start(bf16[31,2,16,256]{3,2,1,0:T(8,128)(2,1)} %get-tuple-element.25.bot_ref), channel_id=1, source_target_pairs={{0,1},{1,2},{2,3},{4,5},{5,6},{6,7},{8,9},{9,10},{10,11},{12,13},{... | collective-permute-start | bytes 1523720 | tf_op jit(solution)/shard_map/ppermute | solution.py:341
  45.3 17.9 %collective-permute-start.13 = (bf16[31,2,16,256]{3,2,1,0:T(8,128)(2,1)}, bf16[31,2,16,256]{3,2,1,0:T(8,128)(2,1)S(1)}, u32[]{:S(2)}, u32[]{:S(2)}) collective-permute-start(bf16[31,2,16,256]{3,2,1,0:T(8,128)(2,1)} %get-tuple-element.26.top_ref), channel_id=1, source_target_pairs={{1,0},{2,1},{3,2},{5,4},{6,5},{7,6},{9,8},{10,9},{11,10},{13,12},{... | collective-permute-start | bytes 1523720 | tf_op jit(solution)/shard_map/ppermute | solution.py:342
  46.6 1.3 %collective-permute-start.9 = (f32[32,256]{1,0:T(8,128)S(1)}, f32[32,256]{1,0:T(8,128)S(1)}, u32[]{:S(2)}, u32[]{:S(2)}) collective-permute-start(f32[32,256]{1,0:T(8,128)S(1)} %get-tuple-element.23), channel_id=1, source_target_pairs={{0,4},{4,0},{8,12},{12,8},{16,20},{20,16},{24,28},{28,24},{1,5},{5... | collective-permute-start | bytes 98312 | tf_op jit(solution)/shard_map/ppermute | solution.py:252
  47.9 3.3 %collective-permute-start.10 = (f32[32,256]{1,0:T(8,128)S(1)}, f32[32,256]{1,0:T(8,128)S(1)}, u32[]{:S(2)}, u32[]{:S(2)}) collective-permute-start(f32[32,256]{1,0:T(8,128)S(1)} %add.18), channel_id=1, source_target_pairs={{0,12},{4,8},{8,4},{12,0},{16,28},{20,24},{24,20},{28,16},{1,13},{... | collective-permute-start | bytes 98312 | tf_op jit(solution)/shard_map/ppermute | solution.py:252
  51.3 9.7 %collective-permute-start.11 = (f32[32,256]{1,0:T(8,128)S(1)}, f32[32,256]{1,0:T(8,128)S(1)}, u32[]{:S(2)}, u32[]{:S(2)}) collective-permute-start(f32[32,256]{1,0:T(8,128)S(1)} %add.19), channel_id=1, source_target_pairs={{0,28},{4,24},{8,20},{12,16},{16,12},{20,8},{24,4},{28,0},{1,29},{... | collective-permute-start | bytes 98312 | tf_op jit(solution)/shard_map/ppermute | solution.py:252
  54.9 17.2 %collective-permute-start.7 = (bf16[16,2,16,256]{3,2,1,0:T(8,128)(2,1)}, bf16[16,2,16,256]{3,2,1,0:T(8,128)(2,1)S(1)}, u32[]{:S(2)}, u32[]{:S(2)}) collective-permute-start(bf16[16,2,16,256]{3,2,1,0:T(8,128)(2,1)} %copy-done.8), channel_id=1, source_target_pairs={{0,1},{1,2},{2,3},{4,5},{5,6},{6,7},{8,9},{9,10},{10,11},{12,13},{... | collective-permute-start | bytes 786440 | tf_op jit(solution)/shard_map/ppermute | solution.py:343
  59.5 12.6 %collective-permute-start.8 = (bf16[16,2,16,256]{3,2,1,0:T(8,128)(2,1)S(1)}, bf16[16,2,16,256]{3,2,1,0:T(8,128)(2,1)S(1)}, u32[]{:S(2)}, u32[]{:S(2)}) collective-permute-start(bf16[16,2,16,256]{3,2,1,0:T(8,128)(2,1)S(1)} %get-tuple-element.22.top_ref), channel_id=1, source_target_pairs={{1,0},{2,1},{3,2},{5,4},{6,5},{7,6},{9,8},{10,9},{11,10},{13,12},{... | collective-permute-start | bytes 786440 | tf_op jit(solution)/shard_map/ppermute | solution.py:344
  61.0 1.3 %copy-start.2 = (bf16[2304,256]{1,0:T(8,128)(2,1)S(1)}, bf16[2304,256]{1,0:T(8,128)(2,1)}, u32[]{:S(2)}) copy-start(bf16[2304,256]{1,0:T(8,128)(2,1)} %w_ref.9) | copy-start | bytes 3538948
  63.3 1.3 %copy-start.3 = (bf16[2304,256]{1,0:T(8,128)(2,1)S(1)}, bf16[2304,256]{1,0:T(8,128)(2,1)}, u32[]{:S(2)}) copy-start(bf16[2304,256]{1,0:T(8,128)(2,1)} %w_ref.9) | copy-start | bytes 3538948
  64.6 7.5 %copy-start.4 = (bf16[2304,256]{1,0:T(8,128)(2,1)S(1)}, bf16[2304,256]{1,0:T(8,128)(2,1)}, u32[]{:S(2)}) copy-start(bf16[2304,256]{1,0:T(8,128)(2,1)} %w_ref.9) | copy-start | bytes 3538948
  64.6 7.5 %copy-start.9 = (bf16[16,2,16,256]{3,2,1,0:T(8,128)(2,1)S(1)}, bf16[16,2,16,256]{3,2,1,0:T(8,128)(2,1)}, u32[]{:S(2)}) copy-start(bf16[16,2,16,256]{3,2,1,0:T(8,128)(2,1)} %copy-done.8) | copy-start | bytes 786436

commit v3 on v2

v3 whole, which is shorter than its diff:
```python
import functools
import math

import jax
import jax.numpy as jnp
import ml_dtypes
import numpy as np
from jax import lax
from jax.experimental import pallas as pl
from jax.experimental.pallas import tpu as pltpu
from jax.sharding import PartitionSpec as P

BLOCK = 16
EDGE = 4
TAPS = 5
VMEM_BYTES = 40 * 1024 * 1024
SMALL_BYTES = 16 * 1024 * 1024
SMEM = pl.BlockSpec(memory_space=pltpu.SMEM)
VMEM = pl.BlockSpec(memory_space=pltpu.VMEM)
HBM = pl.BlockSpec(memory_space=pltpu.HBM)
LITTLE = pl.CostEstimate(flops=1, bytes_accessed=1, transcendentals=0)


def vmem_params(size=SMALL_BYTES):
    return pltpu.CompilerParams(vmem_limit_bytes=size)


def wave_tables(sectors, sector_cols, rows, count):
    length = sectors * sector_cols
    cols = sector_cols + BLOCK
    first = np.array([-2, 0])[None, :, None] + sector_cols * np.arange(sectors)[:, None, None]
    place = (first + np.arange(cols)) % length
    phase = place[..., None] * np.arange(count) % length
    angles = phase * (2.0 * np.pi / length)
    waves = np.concatenate([np.cos(angles), np.sin(angles)], axis=-1).astype(np.float32)
    high = waves.astype(ml_dtypes.bfloat16).astype(np.float32)
    terms = np.concatenate([high, waves - high, high, np.zeros_like(high)], axis=-1)
    lanes = np.tile(terms, rows).astype(ml_dtypes.bfloat16)
    across = high[:, 1, :sector_cols].transpose(0, 2, 1)
    across = np.concatenate([across, np.zeros_like(across)], axis=1).astype(ml_dtypes.bfloat16)
    return jnp.asarray(lanes), jnp.asarray(across)


def band_pairs(count):
    pairs = []
    for first in (0, 1):
        south = [(i, i + 1) for i in range(first, count - 1, 2)]
        pairs.append(south + [(target, source) for source, target in south])
    return pairs


def exchange(payloads):
    pairs = band_pairs(lax.axis_size("lon"))
    return [lax.ppermute(value, "lon", pair) for value, pair in zip(payloads, pairs)]


def first_is_south():
    return lax.axis_index("lon") % 2 == 0


def payloads(upper, lower):
    south = first_is_south()
    return jnp.where(south, lower, upper), jnp.where(south, upper, lower)


def start_copies(pairs, sems):
    copies = [pltpu.make_async_copy(source, target, sems.at[n]) for n, (source, target) in enumerate(pairs)]
    for copy in copies:
        copy.start()
    return copies


def taps_kernel(first, sent, psi_ref, start_ref, width_ref, out_ref):
    rows = psi_ref.shape[0]
    width = out_ref.shape[1]
    basis = out_ref.shape[0] // (rows * BLOCK)
    first_row = lax.axis_index("lon") * rows
    source = lax.broadcasted_iota(jnp.int32, (32, TAPS * width), 0)
    lane = lax.broadcasted_iota(jnp.int32, (32, TAPS * width), 1)
    offset, height = lane // width, lane % (width // 2) // BLOCK
    swapped = 6 - height // 2 * 2 + height % 2
    if not sent:
        swapped = jnp.where((height < 2) | (height >= 6), swapped, height)
    height = jnp.where(first_is_south(), swapped, height)
    r, q = source // TAPS, source % TAPS
    place_j = lax.broadcasted_iota(jnp.int32, (BLOCK, width), 0)
    place_l = lax.broadcasted_iota(jnp.int32, (BLOCK, width), 1)
    ahead = place_l // (width // 2) * BLOCK + place_l % BLOCK - place_j
    for i in range(rows):
        start, count = start_ref[first_row + i], width_ref[first_row + i]
        chosen = (r + i == height) & (start + q == offset - 2) & (q < count) & (source < TAPS * TAPS)
        chosen = jnp.where(chosen, 1.0, 0.0).astype(jnp.bfloat16)
        spread = jnp.dot(psi_ref[i], chosen, preferred_element_type=jnp.float32)
        for k in range(basis):
            taps = jnp.zeros((BLOCK, width), jnp.float32)
            for d in range(TAPS):
                row = spread[k : k + 1, d * width : (d + 1) * width]
                taps = jnp.where(ahead == first + d, row, taps)
            at = (k * rows + i) * BLOCK
            out_ref[at : at + BLOCK] = taps.astype(jnp.bfloat16)


def tap_matrix(psi, lon_start, lon_width, first, sent):
    rows, basis = psi.shape[0], psi.shape[1]
    psi = psi.reshape(rows, basis, TAPS * TAPS)
    psi = jnp.pad(psi, ((0, 0), (0, 16 - basis), (0, 32 - TAPS * TAPS)))
    width = 2 * (rows + TAPS - 1) * BLOCK
    return pl.pallas_call(
        functools.partial(taps_kernel, first, sent),
        out_shape=jax.ShapeDtypeStruct((basis * rows * BLOCK, width), jnp.bfloat16),
        in_specs=[VMEM, SMEM, SMEM],
        cost_estimate=LITTLE,
        compiler_params=vmem_params(),
    )(psi, lon_start, lon_width)


def harmonic_rows(waves, row):
    part = lax.dot_general(waves, row, (((0,), (0,)), ((), ())), preferred_element_type=jnp.float32)
    return part[:8]


def packet_kernel(latent_ref, across_ref, out_ref, edges_ref, one_ref, two_ref, out_sems):
    rows, cols = latent_ref.shape[0], latent_ref.shape[1]
    even = lax.axis_index("lat") % 2 == 0
    first = jnp.where(first_is_south(), 2, 0)
    payload = [(latent_ref.at[pl.ds(at, 2)], ref) for at, ref in ((first, one_ref), (2 - first, two_ref))]
    sends = start_copies(payload, out_sems)
    across = across_ref[lax.axis_index("lat")]
    for i in range(rows):
        part = jnp.dot(across, latent_ref[i], preferred_element_type=jnp.float32)
        out_ref[8 * i : 8 * i + 8] = part[:8]
        left = latent_ref[i, :BLOCK].astype(jnp.float32)[:EDGE]
        right = latent_ref[i, cols - BLOCK :].astype(jnp.float32)[BLOCK - EDGE :]
        at = EDGE * i
        edges_ref[0, at : at + EDGE] = left
        edges_ref[1, at : at + EDGE] = right
        at += 8 * rows
        out_ref[at : at + EDGE] = jnp.where(even, right, left)
    for copy in sends:
        copy.wait()


def sector_place():
    return lax.axis_index("lat"), lax.axis_size("lat")


def step_kernel(mask, packet_ref, got_ref, edges_ref, out_ref):
    lanes = packet_ref.shape[0] - edges_ref.shape[1]
    me, count = sector_place()
    to_right = (me ^ mask) == (me + 1) % count
    out_ref[:lanes] = packet_ref[:lanes] + got_ref[:lanes]
    out_ref[lanes:] = jnp.where(to_right, edges_ref[1], edges_ref[0])


def sides_kernel(masks, *refs):
    packet_ref, got_refs, (total_ref, upper_ref, lower_ref, one_ref, two_ref) = refs[0], refs[1:-5], refs[-5:]
    lanes = total_ref.shape[0]
    me, count = sector_place()
    total_ref[...] = packet_ref[:lanes] + got_refs[-1][:lanes]
    left = right = got_refs[0][lanes:]
    for mask, got_ref in zip(masks[1:], got_refs[1:]):
        left = jnp.where((me ^ mask) == (me + count - 1) % count, got_ref[lanes:], left)
        right = jnp.where((me ^ mask) == (me + 1) % count, got_ref[lanes:], right)
    blank = jnp.zeros((BLOCK - EDGE, left.shape[1]), jnp.float32)
    for i in range(4):
        own = slice(EDGE * i, EDGE * i + EDGE)
        out_ref = upper_ref if i < 2 else lower_ref
        out_ref[0, i % 2] = jnp.concatenate([blank, left[own]], axis=0).astype(jnp.bfloat16)
        out_ref[1, i % 2] = jnp.concatenate([right[own], blank], axis=0).astype(jnp.bfloat16)
    one_ref[...], two_ref[...] = payloads(upper_ref[...], lower_ref[...])


def cycle_mix(norm_factor, lat_total, total_ref, coef_ref, counts_ref, w_ref):
    rows, basis = coef_ref.shape[0], coef_ref.shape[1]
    lanes, channels = total_ref.shape
    first_row = lax.axis_index("lon") * rows
    columns = []
    for i in range(rows):
        polar = (first_row + i < counts_ref[0]) | (first_row + i >= lat_total - counts_ref[1])
        columns.append(jnp.where(polar, coef_ref[i].T * norm_factor, 0.0))
    coefs = jnp.concatenate(columns, axis=0)
    total = total_ref[...]
    acc = jnp.zeros((2 * lanes, w_ref.shape[1]), jnp.float32)
    for k in range(basis):
        term = total * coefs[:, k : k + 1]
        high = term.astype(jnp.bfloat16)
        low = (term - high.astype(jnp.float32)).astype(jnp.bfloat16)
        acc += jnp.dot(
            jnp.concatenate([high, low], axis=0),
            w_ref[k * channels : (k + 1) * channels],
            preferred_element_type=jnp.float32,
        )
    mixed = acc[:lanes] + acc[lanes:]
    high = mixed.astype(jnp.bfloat16).astype(jnp.float32)
    low = mixed - high
    pieces = []
    for i in range(rows):
        own = slice(8 * i, 8 * i + 8)
        pieces += [high[own], high[own], low[own], jnp.zeros_like(low[own])]
    return jnp.concatenate(pieces, axis=0).astype(jnp.bfloat16)


def group_values(start, count, half, taps_ref, w_ref, bias_ref, wave_block, cycle_ref, feat_ref, lift_ref):
    channels = w_ref.shape[1]
    basis = w_ref.shape[0] // channels
    slab = 4 * BLOCK
    lane = lax.broadcasted_iota(jnp.int32, (BLOCK, lift_ref.shape[1]), 1) // (lift_ref.shape[1] // 4)
    for t in range(count):
        window = jnp.concatenate([half(start, t), half(start, t + 1)], axis=0)
        feature = jnp.dot(taps_ref[...], window, preferred_element_type=jnp.float32)
        feature = feature.astype(jnp.bfloat16)
        for k in range(basis):
            feat_ref[t * slab : (t + 1) * slab, k * channels : (k + 1) * channels] = feature[
                k * slab : (k + 1) * slab
            ]
        waves = wave_block(start + t).astype(jnp.float32)
        lift = jnp.concatenate([jnp.where(lane == i, waves, 0.0) for i in range(4)], axis=0)
        lift_ref[t * slab : (t + 1) * slab] = lift.astype(jnp.bfloat16)
    size = count * slab
    mixed = jnp.dot(feat_ref[:size], w_ref[...], preferred_element_type=jnp.float32)
    mixed += jnp.dot(lift_ref[:size], cycle_ref[...], preferred_element_type=jnp.float32)
    return mixed + bias_ref[...]


def aligned(block):
    at = block * BLOCK
    return pl.ds(at if isinstance(at, int) else pl.multiple_of(at, BLOCK), BLOCK)


def first_kernel(mix, first, count, one_hbm, two_hbm, mid_ref, waves_ref, w_ref, side_one_ref, side_upper_ref,
                 side_lower_ref, side_two_ref, taps_ref, bias_ref, *refs):
    feat_ref, lift_ref, one_ref, two_ref, sems = refs[-5:]
    if first:
        before_ref, cycle_ref, pay_one_ref, pay_two_ref, harm_ref = refs[:-5]
    else:
        total_ref, coef_ref, counts_ref, pay_one_ref, pay_two_ref, harm_ref, cycle_ref = refs[:-5]
    rows, cols, channels = mid_ref.shape
    blocks = cols // BLOCK + 1
    low = max(first - 1, 0)
    own = pl.ds(low * BLOCK, one_ref.shape[1])
    copies = start_copies([(one_hbm.at[:, own], one_ref), (two_hbm.at[:, own], two_ref)], sems)
    if not first:
        cycle_ref[...] = mix(total_ref, coef_ref, counts_ref, w_ref)

    def half(start, t):
        b = start + t
        if b in (0, blocks):
            side = 0 if b == 0 else 1
            parts = [ref[side] for ref in (side_one_ref, side_upper_ref, side_lower_ref, side_two_ref)]
        else:
            at = aligned(b - 1 - low)
            parts = [one_ref[:, at], mid_ref[:, aligned(b - 1)], two_ref[:, at]]
        return jnp.concatenate(parts, axis=0).reshape(8 * BLOCK, channels)

    for copy in copies:
        copy.wait()
    mixed = group_values(first, count, half, taps_ref, w_ref, bias_ref,
                         lambda b: waves_ref[0, aligned(b)], cycle_ref, feat_ref, lift_ref)
    value = (0.5 * mixed * (1.0 + lax.erf(mixed * math.sqrt(0.5)))).astype(jnp.bfloat16)
    for t in range(count):
        piece = value[t * 4 * BLOCK : (t + 1) * 4 * BLOCK].reshape(4, BLOCK, channels)
        pay_one_ref[t], pay_two_ref[t] = payloads(piece[:2], piece[2:])

    size = count * BLOCK
    place = lax.broadcasted_iota(jnp.int32, (size, waves_ref.shape[2]), 0) + first * BLOCK
    inside = (place >= 2) & (place < 2 + cols)
    waves = waves_ref[0, first * BLOCK : first * BLOCK + size].astype(jnp.float32)
    waves = jnp.where(inside, waves, 0.0).astype(jnp.bfloat16)
    parts = [
        jnp.concatenate([harmonic_rows(waves, ref[:, r].reshape(size, channels)) for r in range(2)], axis=0)
        for ref in (pay_one_ref, pay_two_ref)
    ]
    total = jnp.concatenate(payloads(*parts), axis=0)
    if first:
        total += before_ref[...]
    harm_ref[...] = total


def second_kernel(mix, groups, *refs):
    parts = [refs[at : at + 4] for at in range(0, 4 * len(groups), 4)]
    refs = refs[4 * len(groups) :]
    total_ref, coef_ref, counts_ref, waves_ref, w_ref, taps_ref, bias_ref, out_hbm, feat_ref, lift_ref, cycle_ref = refs[:11]
    refs = refs[11:]
    out_refs, out_sems = refs[:-1], refs[-1]
    channels = w_ref.shape[1]
    cycle_ref[...] = mix(total_ref, coef_ref, counts_ref, w_ref)
    place = [(part, at) for part in range(len(groups)) for at in range(parts[part][0].shape[0])]

    def half(start, t):
        part, at = place[start + t]
        return jnp.concatenate([ref[at] for ref in parts[part]], axis=0).reshape(8 * BLOCK, channels)

    start, sends = 0, []
    for n, (count, out_ref) in enumerate(zip(groups, out_refs)):
        mixed = group_values(start, count, half, taps_ref, w_ref, bias_ref, lambda b: waves_ref[1, aligned(b)],
                             cycle_ref, feat_ref, lift_ref)
        value = mixed.astype(jnp.bfloat16)
        for t in range(count):
            out_ref[:, aligned(t)] = value[t * 4 * BLOCK : (t + 1) * 4 * BLOCK].reshape(4, BLOCK, channels)
        at = pl.ds(start * BLOCK, count * BLOCK)
        send = pltpu.make_async_copy(out_ref, out_hbm.at[:, at], out_sems.at[n])
        send.start()
        sends.append(send)
        start += count
    for send in sends:
        send.wait()


def conv_cost(blocks, channels):
    macs = blocks * BLOCK * 4 * 18 * channels * channels
    return pl.CostEstimate(flops=4 * macs, bytes_accessed=8_000_000, transcendentals=0)


def swap(value, mask):
    return lax.ppermute(value, "lat", [(i, i ^ mask) for i in range(lax.axis_size("lat"))])


def body(
    latent,
    psi_one,
    psi_two,
    cycle_one,
    cycle_two,
    w_one,
    w_two,
    b_one,
    b_two,
    lon_start,
    lon_width,
    polar_counts,
):
    row_count, col_count, channels = latent.shape
    basis, harm_count = cycle_one.shape[1], cycle_one.shape[3]
    lat_total = row_count * lax.axis_size("lon")
    sectors = lax.axis_size("lat")
    norm_factor = (col_count * sectors) ** (-0.5)
    out_blocks = col_count // BLOCK
    hid_blocks = out_blocks + 1
    lanes = row_count * 2 * harm_count
    masks = [2**t - 1 for t in range(1, sectors.bit_length())]
    tables, across = wave_tables(sectors, col_count, row_count, harm_count)
    waves = lax.dynamic_index_in_dim(tables, lax.axis_index("lat"), 0, keepdims=False)
    f32 = lambda *shape: jax.ShapeDtypeStruct(shape, jnp.float32)
    bf16 = lambda *shape: jax.ShapeDtypeStruct(shape, jnp.bfloat16)
    held = lambda *shape: pltpu.VMEM(shape, jnp.bfloat16)
    sems = lambda count: pltpu.SemaphoreType.DMA((count,))

    edge_rows = row_count * EDGE
    rows_shape = bf16(2, col_count, channels)
    packet, edges, *rows = pl.pallas_call(
        packet_kernel,
        out_shape=(f32(lanes + edge_rows, channels), f32(2, edge_rows, channels), rows_shape, rows_shape),
        in_specs=[VMEM, VMEM],
        out_specs=[VMEM, VMEM, HBM, HBM],
        scratch_shapes=[sems(2)],
        cost_estimate=LITTLE,
        compiler_params=vmem_params(),
    )(latent, across)
    row_one, row_two = exchange(rows)
    gots = [swap(packet, masks[0])]
    for mask in masks[1:]:
        packet = pl.pallas_call(
            functools.partial(step_kernel, mask),
            cost_estimate=LITTLE,
            out_shape=f32(*packet.shape),
            compiler_params=vmem_params(),
        )(packet, gots[-1], edges)
        gots.append(swap(packet, mask))
    side = bf16(2, 2, BLOCK, channels)
    total_one, side_upper, side_lower, *sides = pl.pallas_call(
        functools.partial(sides_kernel, masks),
        cost_estimate=LITTLE,
        out_shape=(f32(lanes, channels), side, side, side, side),
        compiler_params=vmem_params(),
    )(packet, *gots)
    side_one, side_two = exchange(sides)

    mix = functools.partial(cycle_mix, norm_factor, lat_total)
    mix_shape = (row_count * 32, channels)
    coefs = lambda cycle: cycle.reshape(row_count, basis, 2 * harm_count)

    def scratch(count):
        size = count * row_count * BLOCK
        return [held(size, basis * channels), held(size, mix_shape[0])]

    taps_one = tap_matrix(psi_one, lon_start, lon_width, BLOCK - EDGE, False)
    cut = hid_blocks // 2
    hidden = []
    for first, count in ((0, cut), (cut, hid_blocks - cut)):
        operands = (row_one, row_two, latent, waves, w_one, side_one, side_upper, side_lower, side_two, taps_one)
        operands += (b_one[None],)
        half = bf16(count, 2, BLOCK, channels)
        out_shape = (half, half, f32(lanes, channels))
        in_specs = [HBM] * 2 + [VMEM] * (len(operands) - 2)
        if first:
            operands += (harmonics, mix_one)
            in_specs += [VMEM, VMEM]
        else:
            operands += (total_one, coefs(cycle_one), polar_counts)
            in_specs += [VMEM, VMEM, SMEM]
            out_shape += (bf16(*mix_shape),)
        own = (min(first + count, out_blocks) - max(first - 1, 0)) * BLOCK
        pay_one, pay_two, harmonics, *made = pl.pallas_call(
            functools.partial(first_kernel, mix, first, count),
            out_shape=out_shape,
            in_specs=in_specs,
            scratch_shapes=scratch(count) + [held(2, own, channels), held(2, own, channels), sems(2)],
            compiler_params=vmem_params(VMEM_BYTES),
            cost_estimate=LITTLE,
        )(*operands)
        mix_one = made[0] if made else mix_one
        got_one, got_two = exchange((pay_one, pay_two))
        hidden += [got_one, pay_one, pay_two, got_two]

    total_two = harmonics + swap(harmonics, masks[0])
    for got in (hidden[0], hidden[3]):
        total_two += 0.0 * got[0, 0, :1].astype(jnp.float32)
    for mask in masks[1:]:
        total_two = total_two + swap(total_two, mask)
    psi_two, _ = lax.optimization_barrier((psi_two, harmonics))
    taps_two = tap_matrix(psi_two, lon_start, lon_width, 0, True)
    groups = (cut, out_blocks - cut)
    operands = (*hidden, total_two, coefs(cycle_two), polar_counts, waves, w_two, taps_two, b_two[None])
    return pl.pallas_call(
        functools.partial(second_kernel, mix, groups),
        out_shape=bf16(row_count, col_count, channels),
        in_specs=[VMEM] * (len(hidden) + 2) + [SMEM] + [VMEM] * 4,
        out_specs=HBM,
        scratch_shapes=scratch(max(groups))
        + [held(*mix_shape)]
        + [held(row_count, count * BLOCK, channels) for count in groups]
        + [sems(len(groups))],
        compiler_params=vmem_params(56 * 1024 * 1024),
        cost_estimate=conv_cost(out_blocks, channels),
    )(*operands)


def solution(mesh):
    return jax.shard_map(
        body,
        mesh=mesh,
        in_specs=(
            P("lon", "lat", None),
            P("lon", None, None, None),
            P("lon", None, None, None),
            P("lon", None, None, None),
            P("lon", None, None, None),
            P(),
            P(),
            P(),
            P(),
            P(),
            P(),
            P(),
        ),
        out_specs=P("lon", "lat", None),
        check_vma=False,
    )
```

time: 76.1 us -> 67.9 us (0.89)
  starting transfers between devices: 31.4 us -> 25.4 us
  waiting for transfers between devices: 11.1 us -> 7.6 us
  Pallas kernels: 25.3 us -> 27.4 us
  local copies, waits for them, and re-layouts: 7.44 us -> 5.99 us
    ppermute x8, starting transfers between devices: 23.5 us -> 17.5 us  [exchange(): lax.ppermute(value, 'lon', pair)]
    slice x1 -> x0, local copies, waits for them, and re-layouts: 2.66 us -> none  [body(): down = lax.ppermute(latent[:2], 'lon', north)]
    ppermute x8, waiting for transfers between devices: 2.35 us -> 0.02 us  [exchange(): lax.ppermute(value, 'lon', pair)]
    pallas_call x10 -> x8, Pallas kernels: 24.9 us -> 26.2 us  [the longest x2 12.5 us: body(): pl.pallas_call(functools.partial(first_kernel, mix, first, count), out_sh...]
    ppermute x6, waiting for transfers between devices: 8.76 us -> 7.58 us  [swap(): lax.ppermute(value, 'lat', [(i, i ^ mask) for i in range(lax.axis_size('l...]
    pallas_call x1, Pallas kernels: 0.39 us -> 1.19 us  [body(): pl.pallas_call(packet_kernel, out_shape=(f32(lanes + edge_rows, channels)...]
    unnamed x32 -> x40, local copies, waits for them, and re-layouts: 3.29 us -> 3.92 us
  transfers between devices with their start and end apart: 14 -> 14, of which waited for: 6 -> 4; matrix products, arithmetic and copies ran while one was open for 2% -> 4% of each run, Pallas kernels for 15% -> 13%
where the time goes in v3:
time: 67.9 us; the launch traced here: 67.5 us
  Pallas kernels  27.4 us (40%)
  starting transfers between devices  25.4 us (37%)
  waiting for transfers between devices  7.6 us (11%)
  local copies, waits for them, and re-layouts  5.99 us (9%)
    ppermute x8, starting transfers between devices, exchange(): lax.ppermute(value, 'lon', pair)  17.5 us
    pallas_call x2, Pallas kernels, body(): pl.pallas_call(functools.partial(first_kernel, mix, first, count), out_sh...  12.5 us
    pallas_call x1, Pallas kernels, body(): pl.pallas_call(functools.partial(second_kernel, mix, groups), out_shape=b...  11.2 us
    ppermute x6, starting transfers between devices, swap(): lax.ppermute(value, 'lat', [(i, i ^ mask) for i in range(lax.axis_size('l...  7.9 us
    ppermute x6, waiting for transfers between devices, swap(): lax.ppermute(value, 'lat', [(i, i ^ mask) for i in range(lax.axis_size('l...  7.58 us
    unnamed x40, local copies, waits for them, and re-layouts  3.92 us
    pallas_call x2, Pallas kernels, tap_matrix(): pl.pallas_call(functools.partial(taps_kernel, first, sent), out_shape=jax...  1.85 us
  transfers between devices with their start and end apart: 14, of which 4 were waited for; matrix products, arithmetic and copies ran while one was open for 4% of the time, Pallas kernels for 13%

profile of v3, /device:TPU:0, one launch (start us, length us, event | category | flops | bytes accessed | tf_op | source)
XLA Modules:
  0.0 67.5 jit_solution(3854852558144576973)
XLA Ops:
  0.0 1.4 %copy-done = bf16[4,720,256]{2,1,0:T(8,128)(2,1)S(1)} copy-done((bf16[4,720,256]{2,1,0:T(8,128)(2,1)S(1)}, bf16[4,720,256]{2,1,0:T(8,128)(2,1)}, u32[]{:S(2)}) %copy-start) | copy-done | bytes 1474584
  1.4 0.9 %copy-done.5 = bf16[8,16,720]{2,1,0:T(8,128)(2,1)S(1)} copy-done((bf16[8,16,720]{2,1,0:T(8,128)(2,1)S(1)}, bf16[8,16,720]{2,1,0:T(8,128)(2,1)}, u32[]{:S(2)}) %copy-start.5) | copy-done | bytes 184344
  2.3 0.0 copy-start.9
  2.4 1.2 %shard_map.136 = (f32[48,256]{1,0:T(8,128)S(1)}, f32[2,16,256]{2,1,0:T(8,128)S(1)}, bf16[2,720,256]{2,1,0:T(8,128)(2,1)}, bf16[2,720,256]{2,1,0:T(8,128)(2,1)}) custom-call(bf16[4,720,256]{2,1,0:T(8,128)(2,1)S(1)} %copy-done, bf16[8,16,720]{2,1,0:T(8,128)(2,1)S(1)} %copy-done.5), custom_call_target="tpu_custom_call" | custom-call | flops 1 | bytes 1 | tf_op jit(solution)/shard_map/pallas_call | solution.py:350
  3.5 3.1 %collective-permute-start = (bf16[2,720,256]{2,1,0:T(8,128)(2,1)}, bf16[2,720,256]{2,1,0:T(8,128)(2,1)}, u32[]{:S(2)}, u32[]{:S(2)}) collective-permute-start(bf16[2,720,256]{2,1,0:T(8,128)(2,1)} %get-tuple-element.22), channel_id=1, source_target_pairs={{0,1},{2,3},{1,0},{3,2},{4,5},{6,7},{5,4},{7,6},{8,9},{10,11},{9,8... | collective-permute-start | bytes 2211848 | tf_op jit(solution)/shard_map/ppermute | solution.py:54
  6.6 1.5 %collective-permute-start.1 = (bf16[2,720,256]{2,1,0:T(8,128)(2,1)}, bf16[2,720,256]{2,1,0:T(8,128)(2,1)}, u32[]{:S(2)}, u32[]{:S(2)}) collective-permute-start(bf16[2,720,256]{2,1,0:T(8,128)(2,1)} %get-tuple-element.23), channel_id=1, source_target_pairs={{1,2},{2,1},{5,6},{6,5},{9,10},{10,9},{13,14},{14,13},{17,18},{18,... | collective-permute-start | bytes 2211848 | tf_op jit(solution)/shard_map/ppermute | solution.py:54
  8.2 0.0 collective-permute-start.2
  8.2 1.2 %collective-permute-done.2.got_ref.refs_1_ = f32[48,256]{1,0:T(8,128)S(1)} collective-permute-done((f32[48,256]{1,0:T(8,128)S(1)}, f32[48,256]{1,0:T(8,128)S(1)}, u32[]{:S(2)}, u32[]{:S(2)}) %collective-permute-start.2) | collective-permute-done | bytes 49184 | tf_op jit(solution)/shard_map/ppermute | solution.py:315
  9.4 1.3 %collective-permute-start.3 = (f32[48,256]{1,0:T(8,128)S(1)}, f32[48,256]{1,0:T(8,128)S(1)}, u32[]{:S(2)}, u32[]{:S(2)}) collective-permute-start(f32[48,256]{1,0:T(8,128)S(1)} %shard_map.137.packet_ref), channel_id=1, source_target_pairs={{0,12},{4,8},{8,4},{12,0},{16,28},{20,24},{24,20},{28,16},{1,13},{... | collective-permute-start | bytes 147464 | tf_op jit(solution)/shard_map/ppermute | solution.py:315
  10.7 2.5 %collective-permute-done.3.got_ref.refs_2_ = f32[48,256]{1,0:T(8,128)S(1)} collective-permute-done((f32[48,256]{1,0:T(8,128)S(1)}, f32[48,256]{1,0:T(8,128)S(1)}, u32[]{:S(2)}, u32[]{:S(2)}) %collective-permute-start.3) | collective-permute-done | bytes 49184 | tf_op jit(solution)/shard_map/ppermute | solution.py:315
  13.2 2.7 %collective-permute-start.4 = (f32[48,256]{1,0:T(8,128)S(1)}, f32[48,256]{1,0:T(8,128)S(1)}, u32[]{:S(2)}, u32[]{:S(2)}) collective-permute-start(f32[48,256]{1,0:T(8,128)S(1)} %shard_map.138.refs_0_), channel_id=1, source_target_pairs={{0,28},{4,24},{8,20},{12,16},{16,12},{20,8},{24,4},{28,0},{1,29},{... | collective-permute-start | bytes 147464 | tf_op jit(solution)/shard_map/ppermute | solution.py:315
  15.9 1.8 %collective-permute-done.4.refs_3_ = f32[48,256]{1,0:T(8,128)S(1)} collective-permute-done((f32[48,256]{1,0:T(8,128)S(1)}, f32[48,256]{1,0:T(8,128)S(1)}, u32[]{:S(2)}, u32[]{:S(2)}) %collective-permute-start.4) | collective-permute-done | bytes 49184 | tf_op jit(solution)/shard_map/ppermute | solution.py:315
  17.7 0.6 shard_map.139
  18.3 3.6 %collective-permute-start.5 = (bf16[2,2,16,256]{3,2,1,0:T(8,128)(2,1)}, bf16[2,2,16,256]{3,2,1,0:T(8,128)(2,1)S(1)}, u32[]{:S(2)}, u32[]{:S(2)}) collective-permute-start(bf16[2,2,16,256]{3,2,1,0:T(8,128)(2,1)} %get-tuple-element.26), channel_id=1, source_target_pairs={{0,1},{2,3},{1,0},{3,2},{4,5},{6,7},{5,4},{7,6},{8,9},{10,11},{9,8... | collective-permute-start | bytes 98312 | tf_op jit(solution)/shard_map/ppermute | solution.py:54
  21.9 0.7 collective-permute-start.6
  22.6 1.0 %dynamic-slice_bitcast_fusion.waves_ref.refs_11_ = bf16[2,736,128]{2,1,0:T(8,128)(2,1)S(1)} fusion(bf16[8,2,736,128]{3,2,1,0:T(8,128)(2,1)} %constant.21.clone, s32[]{:T(128)S(6)} %select_n.4), kind=kLoop, calls=%fused_computation | loop fusion | bytes 753668 | tf_op jit(solution)/shard_map/jit(dynamic_index_in_dim)/squeeze | solution.py:342
  23.6 0.1 copy.19
  23.8 0.9 %shard_map.140.taps_ref = bf16[576,256]{1,0:T(8,128)(2,1)S(1)} custom-call(bf16[4,16,32]{2,1,0:T(8,128)(2,1)S(1)} %pad.7.psi_ref, s32[16]{0:T(128)S(1)} %copy-done.7, s32[16]{0:T(128)S(1)} %copy-done.8), custom_call_target="tpu_custom_call" | custom-call | flops 1 | bytes 1 | tf_op jit(solution)/shard_map/pallas_call | solution.py:108
  24.7 0.1 copy.20.refs_1_
  24.8 0.0 collective-permute-done.5.side_one_ref
  24.8 0.0 collective-permute-done.6.side_two_ref
  24.8 0.0 collective-permute-done.one_hbm
  24.8 0.0 collective-permute-done.1.two_hbm
  24.9 6.3 %shard_map.141 = (bf16[23,2,16,256]{3,2,1,0:T(8,128)(2,1)S(1)}, bf16[23,2,16,256]{3,2,1,0:T(8,128)(2,1)S(1)}, f32[32,256]{1,0:T(8,128)S(1)}, bf16[128,256]{1,0:T(8,128)(2,1)S(1)}) custom-call(bf16[2,720,256]{2,1,0:T(8,128)(2,1)} %collective-permute-done.one_hbm, bf16[2,720,256]{2,1,0:T(8,128)(2,1)} %collective-permute-done.1.two_hbm, ...), custom_call_target="tpu_custom_call" | custom-call | flops 1 | bytes 1 | tf_op jit(solution)/shard_map/pallas_call | solution.py:403
  31.2 4.0 %collective-permute-start.7 = (bf16[23,2,16,256]{3,2,1,0:T(8,128)(2,1)S(1)}, bf16[23,2,16,256]{3,2,1,0:T(8,128)(2,1)S(1)}, u32[]{:S(2)}, u32[]{:S(2)}) collective-permute-start(bf16[23,2,16,256]{3,2,1,0:T(8,128)(2,1)S(1)} %get-tuple-element.31.refs_1_), channel_id=1, source_target_pairs={{0,1},{2,3},{1,0},{3,2},{4,5},{6,7},{5,4},{7,6},{8,9},{10,11},{9,8... | collective-permute-start | bytes 1130504 | tf_op jit(solution)/shard_map/ppermute | solution.py:54
  35.3 0.7 collective-permute-start.8
  36.0 0.0 copy-start.13
  36.0 0.0 copy-start.15
  36.0 6.2 %shard_map.142 = (bf16[23,2,16,256]{3,2,1,0:T(8,128)(2,1)}, bf16[23,2,16,256]{3,2,1,0:T(8,128)(2,1)}, f32[32,256]{1,0:T(8,128)S(1)}) custom-call(bf16[2,720,256]{2,1,0:T(8,128)(2,1)} %collective-permute-done.one_hbm, bf16[2,720,256]{2,1,0:T(8,128)(2,1)} %collective-permute-done.1.two_hbm, bf16[4,720,256]{2,1,0:T(8,128)(2,1)S(1)} %copy-done.1, ...), custom_call_target="tpu_custom_call" | custom-call | flops 1 | bytes 1 | tf_op jit(solution)/shard_map/pallas_call | solution.py:403
  42.2 0.1 collective-permute-start.11
  42.3 3.0 %collective-permute-start.9 = (bf16[23,2,16,256]{3,2,1,0:T(8,128)(2,1)}, bf16[23,2,16,256]{3,2,1,0:T(8,128)(2,1)S(1)}, u32[]{:S(2)}, u32[]{:S(2)}) collective-permute-start(bf16[23,2,16,256]{3,2,1,0:T(8,128)(2,1)} %get-tuple-element.35.refs_5_), channel_id=1, source_target_pairs={{0,1},{2,3},{1,0},{3,2},{4,5},{6,7},{5,4},{7,6},{8,9},{10,11},{9,8... | collective-permute-start | bytes 1130504 | tf_op jit(solution)/shard_map/ppermute | solution.py:54
  45.3 0.9 %collective-permute-start.10 = (bf16[23,2,16,256]{3,2,1,0:T(8,128)(2,1)}, bf16[23,2,16,256]{3,2,1,0:T(8,128)(2,1)S(1)}, u32[]{:S(2)}, u32[]{:S(2)}) collective-permute-start(bf16[23,2,16,256]{3,2,1,0:T(8,128)(2,1)} %get-tuple-element.36.refs_6_), channel_id=1, source_target_pairs={{1,2},{2,1},{5,6},{6,5},{9,10},{10,9},{13,14},{14,13},{17,18},{18,... | collective-permute-start | bytes 1130504 | tf_op jit(solution)/shard_map/ppermute | solution.py:54
  46.2 0.0 collective-permute-done.7.refs_0_
  46.2 0.0 collective-permute-done.8.refs_3_
  46.3 0.0 collective-permute-done.11
  46.3 1.3 %collective-permute-start.12 = (f32[32,256]{1,0:T(8,128)S(1)}, f32[32,256]{1,0:T(8,128)S(1)}, u32[]{:S(2)}, u32[]{:S(2)}) collective-permute-start(f32[32,256]{1,0:T(8,128)S(1)} %add_add_fusion), channel_id=1, source_target_pairs={{0,12},{4,8},{8,4},{12,0},{16,28},{20,24},{24,20},{28,16},{1,13},{... | collective-permute-start | bytes 98312 | tf_op jit(solution)/shard_map/ppermute | solution.py:315
  47.6 2.1 %collective-permute-done.12 = f32[32,256]{1,0:T(8,128)S(1)} collective-permute-done((f32[32,256]{1,0:T(8,128)S(1)}, f32[32,256]{1,0:T(8,128)S(1)}, u32[]{:S(2)}, u32[]{:S(2)}) %collective-permute-start.12) | collective-permute-done | bytes 32800 | tf_op jit(solution)/shard_map/ppermute | solution.py:315
  49.7 2.5 %collective-permute-start.13 = (f32[32,256]{1,0:T(8,128)S(1)}, f32[32,256]{1,0:T(8,128)S(1)}, u32[]{:S(2)}, u32[]{:S(2)}) collective-permute-start(f32[32,256]{1,0:T(8,128)S(1)} %add.39), channel_id=1, source_target_pairs={{0,28},{4,24},{8,20},{12,16},{16,12},{20,8},{24,4},{28,0},{1,29},{... | collective-permute-start | bytes 98312 | tf_op jit(solution)/shard_map/ppermute | solution.py:315
  52.2 0.1 copy.21
  52.4 0.7 %copy.22.refs_9_ = f32[4,9,8]{2,1,0:T(8,128)} copy(f32[4,9,8]{1,2,0:T(8,128)S(1)} %bitcast.15) | data formatting | bytes 2304 | tf_op jit(solution)/shard_map/reshape | solution.py:380
  53.1 0.9 %shard_map.143.refs_13_ = bf16[576,256]{1,0:T(8,128)(2,1)S(1)} custom-call(bf16[4,16,32]{2,1,0:T(8,128)(2,1)S(1)} %pad.8.psi_ref, s32[16]{0:T(128)S(1)} %copy-done.7, s32[16]{0:T(128)S(1)} %copy-done.8), custom_call_target="tpu_custom_call" | custom-call | flops 1 | bytes 1 | tf_op jit(solution)/shard_map/pallas_call | solution.py:108
  54.0 0.7 %copy-done.4 = bf16[576,256]{1,0:T(8,128)(2,1)} copy-done((bf16[576,256]{1,0:T(8,128)(2,1)}, bf16[576,256]{1,0:T(8,128)(2,1)S(1)}, u32[]{:S(2)}) %copy-start.4) | copy-done | bytes 294936
  54.7 0.0 collective-permute-done.13
  54.7 0.6 add.40.refs_8_
  55.3 0.0 collective-permute-done.9.refs_4_
  55.4 0.7 %copy-done.18 = bf16[23,2,16,256]{3,2,1,0:T(8,128)(2,1)} copy-done((bf16[23,2,16,256]{3,2,1,0:T(8,128)(2,1)}, bf16[23,2,16,256]{3,2,1,0:T(8,128)(2,1)S(1)}, u32[]{:S(2)}) %copy-start.18) | copy-done | bytes 376856
  56.1 0.1 copy-done.19
  56.2 11.2 %shard_map.144 = bf16[4,720,256]{2,1,0:T(8,128)(2,1)} custom-call(bf16[23,2,16,256]{3,2,1,0:T(8,128)(2,1)} %copy-done.16, bf16[23,2,16,256]{3,2,1,0:T(8,128)(2,1)} %copy-done.10, bf16[23,2,16,256]{3,2,1,0:T(8,128)(2,1)} %copy-done.11, bf16[23,2,16,256]{3,2,1,0:T(8,128)(2,1)} %copy-done.17, bf16[23,2,16,256]{3,2,1,0:T(8,128)(2,1)} %copy-done.18, ...), custom_call_target="tpu_custom_call" | custom-call | flops 13589544960 | bytes 8000000 | tf_op jit(solution)/shard_map/pallas_call | solution.py:424
  (41 shorter events, 0.1 us)
Async XLA Ops:
  0.0 1.4 %copy-start = (bf16[4,720,256]{2,1,0:T(8,128)(2,1)S(1)}, bf16[4,720,256]{2,1,0:T(8,128)(2,1)}, u32[]{:S(2)}) copy-start(bf16[4,720,256]{2,1,0:T(8,128)(2,1)} %mid_ref.3) | copy-start | bytes 4423684
  1.4 0.9 %copy-start.5 = (bf16[8,16,720]{2,1,0:T(8,128)(2,1)S(1)}, bf16[8,16,720]{2,1,0:T(8,128)(2,1)}, u32[]{:S(2)}) copy-start(bf16[8,16,720]{2,1,0:T(8,128)(2,1)} %constant.22.clone.across_ref) | copy-start | bytes 552964
  2.3 21.3 %copy-start.12 = (bf16[4,9,5,5]{1,0,3,2:T(4,128)(2,1)S(1)}, bf16[4,9,5,5]{1,0,3,2:T(4,128)(2,1)}, u32[]{:S(2)}) copy-start(bf16[4,9,5,5]{1,0,3,2:T(4,128)(2,1)} %param.15) | copy-start | bytes 5404
  2.3 21.5 %copy-start.7 = (s32[16]{0:T(128)S(1)}, s32[16]{0:T(128)}, u32[]{:S(2)}) copy-start(s32[16]{0:T(128)} %start_ref.3) | copy-start | bytes 196
  2.3 21.5 %copy-start.8 = (s32[16]{0:T(128)S(1)}, s32[16]{0:T(128)}, u32[]{:S(2)}) copy-start(s32[16]{0:T(128)} %width_ref.3) | copy-start | bytes 196
  2.3 22.4 %copy-start.14 = (f32[4,9,2,4]{1,3,2,0:T(4,128)S(1)}, f32[4,9,2,4]{1,3,2,0:T(4,128)}, u32[]{:S(2)}) copy-start(f32[4,9,2,4]{1,3,2,0:T(4,128)} %param.17) | copy-start | bytes 3460
  2.3 22.5 %copy-start.1 = (bf16[4,720,256]{2,1,0:T(8,128)(2,1)S(1)}, bf16[4,720,256]{2,1,0:T(8,128)(2,1)}, u32[]{:S(2)}) copy-start(bf16[4,720,256]{2,1,0:T(8,128)(2,1)} %mid_ref.3) | copy-start | bytes 4423684
  2.3 22.5 %copy-start.2 = (bf16[2304,256]{1,0:T(8,128)(2,1)S(1)}, bf16[2304,256]{1,0:T(8,128)(2,1)}, u32[]{:S(2)}) copy-start(bf16[2304,256]{1,0:T(8,128)(2,1)} %w_ref.3) | copy-start | bytes 3538948
  2.3 22.5 %copy-start.6 = (f32[256]{0:T(256)S(1)}, f32[256]{0:T(256)}, u32[]{:S(2)}) copy-start(f32[256]{0:T(256)} %param.21) | copy-start | bytes 3076
  2.3 22.5 %copy-start.9 = (s32[2]{0:T(128)S(1)}, s32[2]{0:T(128)}, u32[]{:S(2)}) copy-start(s32[2]{0:T(128)} %refs_10_.1) | copy-start | bytes 28
  3.5 21.3 %collective-permute-start = (bf16[2,720,256]{2,1,0:T(8,128)(2,1)}, bf16[2,720,256]{2,1,0:T(8,128)(2,1)}, u32[]{:S(2)}, u32[]{:S(2)}) collective-permute-start(bf16[2,720,256]{2,1,0:T(8,128)(2,1)} %get-tuple-element.22), channel_id=1, source_target_pairs={{0,1},{2,3},{1,0},{3,2},{4,5},{6,7},{5,4},{7,6},{8,9},{10,11},{9,8... | collective-permute-start | bytes 2211848 | tf_op jit(solution)/shard_map/ppermute | solution.py:54
  6.6 18.2 %collective-permute-start.1 = (bf16[2,720,256]{2,1,0:T(8,128)(2,1)}, bf16[2,720,256]{2,1,0:T(8,128)(2,1)}, u32[]{:S(2)}, u32[]{:S(2)}) collective-permute-start(bf16[2,720,256]{2,1,0:T(8,128)(2,1)} %get-tuple-element.23), channel_id=1, source_target_pairs={{1,2},{2,1},{5,6},{6,5},{9,10},{10,9},{13,14},{14,13},{17,18},{18,... | collective-permute-start | bytes 2211848 | tf_op jit(solution)/shard_map/ppermute | solution.py:54
  8.2 1.2 %collective-permute-start.2 = (f32[48,256]{1,0:T(8,128)S(1)}, f32[48,256]{1,0:T(8,128)S(1)}, u32[]{:S(2)}, u32[]{:S(2)}) collective-permute-start(f32[48,256]{1,0:T(8,128)S(1)} %get-tuple-element.24.packet_ref), channel_id=1, source_target_pairs={{0,4},{4,0},{8,12},{12,8},{16,20},{20,16},{24,28},{28,24},{1,5},{5... | collective-permute-start | bytes 147464 | tf_op jit(solution)/shard_map/ppermute | solution.py:315
  9.4 3.8 %collective-permute-start.3 = (f32[48,256]{1,0:T(8,128)S(1)}, f32[48,256]{1,0:T(8,128)S(1)}, u32[]{:S(2)}, u32[]{:S(2)}) collective-permute-start(f32[48,256]{1,0:T(8,128)S(1)} %shard_map.137.packet_ref), channel_id=1, source_target_pairs={{0,12},{4,8},{8,4},{12,0},{16,28},{20,24},{24,20},{28,16},{1,13},{... | collective-permute-start | bytes 147464 | tf_op jit(solution)/shard_map/ppermute | solution.py:315
  13.2 4.5 %collective-permute-start.4 = (f32[48,256]{1,0:T(8,128)S(1)}, f32[48,256]{1,0:T(8,128)S(1)}, u32[]{:S(2)}, u32[]{:S(2)}) collective-permute-start(f32[48,256]{1,0:T(8,128)S(1)} %shard_map.138.refs_0_), channel_id=1, source_target_pairs={{0,28},{4,24},{8,20},{12,16},{16,12},{20,8},{24,4},{28,0},{1,29},{... | collective-permute-start | bytes 147464 | tf_op jit(solution)/shard_map/ppermute | solution.py:315
  18.3 6.5 %collective-permute-start.5 = (bf16[2,2,16,256]{3,2,1,0:T(8,128)(2,1)}, bf16[2,2,16,256]{3,2,1,0:T(8,128)(2,1)S(1)}, u32[]{:S(2)}, u32[]{:S(2)}) collective-permute-start(bf16[2,2,16,256]{3,2,1,0:T(8,128)(2,1)} %get-tuple-element.26), channel_id=1, source_target_pairs={{0,1},{2,3},{1,0},{3,2},{4,5},{6,7},{5,4},{7,6},{8,9},{10,11},{9,8... | collective-permute-start | bytes 98312 | tf_op jit(solution)/shard_map/ppermute | solution.py:54
  21.9 2.9 %collective-permute-start.6 = (bf16[2,2,16,256]{3,2,1,0:T(8,128)(2,1)}, bf16[2,2,16,256]{3,2,1,0:T(8,128)(2,1)S(1)}, u32[]{:S(2)}, u32[]{:S(2)}) collective-permute-start(bf16[2,2,16,256]{3,2,1,0:T(8,128)(2,1)} %get-tuple-element.29), channel_id=1, source_target_pairs={{1,2},{2,1},{5,6},{6,5},{9,10},{10,9},{13,14},{14,13},{17,18},{18,... | collective-permute-start | bytes 98312 | tf_op jit(solution)/shard_map/ppermute | solution.py:54
  23.6 12.3 %copy-start.3 = (bf16[2,736,128]{2,1,0:T(8,128)(2,1)}, bf16[2,736,128]{2,1,0:T(8,128)(2,1)S(1)}, u32[]{:S(2)}) copy-start(bf16[2,736,128]{2,1,0:T(8,128)(2,1)S(1)} %dynamic-slice_bitcast_fusion.waves_ref.refs_11_) | copy-start | bytes 1130500
  31.2 11.0 %copy-start.10 = (bf16[23,2,16,256]{3,2,1,0:T(8,128)(2,1)}, bf16[23,2,16,256]{3,2,1,0:T(8,128)(2,1)S(1)}, u32[]{:S(2)}) copy-start(bf16[23,2,16,256]{3,2,1,0:T(8,128)(2,1)S(1)} %get-tuple-element.31.refs_1_) | copy-start | bytes 1130500
  31.2 11.0 %copy-start.11 = (bf16[23,2,16,256]{3,2,1,0:T(8,128)(2,1)}, bf16[23,2,16,256]{3,2,1,0:T(8,128)(2,1)S(1)}, u32[]{:S(2)}) copy-start(bf16[23,2,16,256]{3,2,1,0:T(8,128)(2,1)S(1)} %get-tuple-element.32.refs_2_) | copy-start | bytes 1130500
  31.2 15.0 %collective-permute-start.7 = (bf16[23,2,16,256]{3,2,1,0:T(8,128)(2,1)S(1)}, bf16[23,2,16,256]{3,2,1,0:T(8,128)(2,1)S(1)}, u32[]{:S(2)}, u32[]{:S(2)}) collective-permute-start(bf16[23,2,16,256]{3,2,1,0:T(8,128)(2,1)S(1)} %get-tuple-element.31.refs_1_), channel_id=1, source_target_pairs={{0,1},{2,3},{1,0},{3,2},{4,5},{6,7},{5,4},{7,6},{8,9},{10,11},{9,8... | collective-permute-start | bytes 1130504 | tf_op jit(solution)/shard_map/ppermute | solution.py:54
  35.3 11.0 %collective-permute-start.8 = (bf16[23,2,16,256]{3,2,1,0:T(8,128)(2,1)S(1)}, bf16[23,2,16,256]{3,2,1,0:T(8,128)(2,1)S(1)}, u32[]{:S(2)}, u32[]{:S(2)}) collective-permute-start(bf16[23,2,16,256]{3,2,1,0:T(8,128)(2,1)S(1)} %get-tuple-element.32.refs_2_), channel_id=1, source_target_pairs={{1,2},{2,1},{5,6},{6,5},{9,10},{10,9},{13,14},{14,13},{17,18},{18,... | collective-permute-start | bytes 1130504 | tf_op jit(solution)/shard_map/ppermute | solution.py:54
  36.0 16.3 %copy-start.13 = (bf16[4,9,5,5]{1,0,3,2:T(4,128)(2,1)S(1)}, bf16[4,9,5,5]{1,0,3,2:T(4,128)(2,1)}, u32[]{:S(2)}) copy-start(bf16[4,9,5,5]{1,0,3,2:T(4,128)(2,1)} %param.16) | copy-start | bytes 5404
  36.0 16.4 %copy-start.15 = (f32[4,9,2,4]{1,3,2,0:T(4,128)S(1)}, f32[4,9,2,4]{1,3,2,0:T(4,128)}, u32[]{:S(2)}) copy-start(f32[4,9,2,4]{1,3,2,0:T(4,128)} %param.18) | copy-start | bytes 3460
  42.2 4.1 %collective-permute-start.11 = (f32[32,256]{1,0:T(8,128)S(1)}, f32[32,256]{1,0:T(8,128)S(1)}, u32[]{:S(2)}, u32[]{:S(2)}) collective-permute-start(f32[32,256]{1,0:T(8,128)S(1)} %get-tuple-element.37), channel_id=1, source_target_pairs={{0,4},{4,0},{8,12},{12,8},{16,20},{20,16},{24,28},{28,24},{1,5},{5... | collective-permute-start | bytes 98312 | tf_op jit(solution)/shard_map/ppermute | solution.py:315
  42.3 13.1 %collective-permute-start.9 = (bf16[23,2,16,256]{3,2,1,0:T(8,128)(2,1)}, bf16[23,2,16,256]{3,2,1,0:T(8,128)(2,1)S(1)}, u32[]{:S(2)}, u32[]{:S(2)}) collective-permute-start(bf16[23,2,16,256]{3,2,1,0:T(8,128)(2,1)} %get-tuple-element.35.refs_5_), channel_id=1, source_target_pairs={{0,1},{2,3},{1,0},{3,2},{4,5},{6,7},{5,4},{7,6},{8,9},{10,11},{9,8... | collective-permute-start | bytes 1130504 | tf_op jit(solution)/shard_map/ppermute | solution.py:54
  45.3 10.0 %collective-permute-start.10 = (bf16[23,2,16,256]{3,2,1,0:T(8,128)(2,1)}, bf16[23,2,16,256]{3,2,1,0:T(8,128)(2,1)S(1)}, u32[]{:S(2)}, u32[]{:S(2)}) collective-permute-start(bf16[23,2,16,256]{3,2,1,0:T(8,128)(2,1)} %get-tuple-element.36.refs_6_), channel_id=1, source_target_pairs={{1,2},{2,1},{5,6},{6,5},{9,10},{10,9},{13,14},{14,13},{17,18},{18,... | collective-permute-start | bytes 1130504 | tf_op jit(solution)/shard_map/ppermute | solution.py:54
  46.2 6.0 %copy-start.16 = (bf16[23,2,16,256]{3,2,1,0:T(8,128)(2,1)}, bf16[23,2,16,256]{3,2,1,0:T(8,128)(2,1)S(1)}, u32[]{:S(2)}) copy-start(bf16[23,2,16,256]{3,2,1,0:T(8,128)(2,1)S(1)} %collective-permute-done.7.refs_0_) | copy-start | bytes 1130500
  46.2 6.0 %copy-start.17 = (bf16[23,2,16,256]{3,2,1,0:T(8,128)(2,1)}, bf16[23,2,16,256]{3,2,1,0:T(8,128)(2,1)S(1)}, u32[]{:S(2)}) copy-start(bf16[23,2,16,256]{3,2,1,0:T(8,128)(2,1)S(1)} %collective-permute-done.8.refs_3_) | copy-start | bytes 1130500
  46.3 3.4 %collective-permute-start.12 = (f32[32,256]{1,0:T(8,128)S(1)}, f32[32,256]{1,0:T(8,128)S(1)}, u32[]{:S(2)}, u32[]{:S(2)}) collective-permute-start(f32[32,256]{1,0:T(8,128)S(1)} %add_add_fusion), channel_id=1, source_target_pairs={{0,12},{4,8},{8,4},{12,0},{16,28},{20,24},{24,20},{28,16},{1,13},{... | collective-permute-start | bytes 98312 | tf_op jit(solution)/shard_map/ppermute | solution.py:315
  49.7 5.0 %collective-permute-start.13 = (f32[32,256]{1,0:T(8,128)S(1)}, f32[32,256]{1,0:T(8,128)S(1)}, u32[]{:S(2)}, u32[]{:S(2)}) collective-permute-start(f32[32,256]{1,0:T(8,128)S(1)} %add.39), channel_id=1, source_target_pairs={{0,28},{4,24},{8,20},{12,16},{16,12},{20,8},{24,4},{28,0},{1,29},{... | collective-permute-start | bytes 98312 | tf_op jit(solution)/shard_map/ppermute | solution.py:315
  54.0 0.7 %copy-start.4 = (bf16[576,256]{1,0:T(8,128)(2,1)}, bf16[576,256]{1,0:T(8,128)(2,1)S(1)}, u32[]{:S(2)}) copy-start(bf16[576,256]{1,0:T(8,128)(2,1)S(1)} %shard_map.143.refs_13_) | copy-start | bytes 884740
  55.3 0.7 %copy-start.18 = (bf16[23,2,16,256]{3,2,1,0:T(8,128)(2,1)}, bf16[23,2,16,256]{3,2,1,0:T(8,128)(2,1)S(1)}, u32[]{:S(2)}) copy-start(bf16[23,2,16,256]{3,2,1,0:T(8,128)(2,1)S(1)} %collective-permute-done.9.refs_4_) | copy-start | bytes 1130500
  55.4 0.9 %copy-start.19 = (bf16[23,2,16,256]{3,2,1,0:T(8,128)(2,1)}, bf16[23,2,16,256]{3,2,1,0:T(8,128)(2,1)S(1)}, u32[]{:S(2)}) copy-start(bf16[23,2,16,256]{3,2,1,0:T(8,128)(2,1)S(1)} %collective-permute-done.10.refs_7_) | copy-start | bytes 1130500

commit v4 on v3

--- a/solution.py
+++ b/solution.py
@@ -36,9 +36,7 @@
     high = waves.astype(ml_dtypes.bfloat16).astype(np.float32)
     terms = np.concatenate([high, waves - high, high, np.zeros_like(high)], axis=-1)
     lanes = np.tile(terms, rows).astype(ml_dtypes.bfloat16)
-    across = high[:, 1, :sector_cols].transpose(0, 2, 1)
-    across = np.concatenate([across, np.zeros_like(across)], axis=1).astype(ml_dtypes.bfloat16)
-    return jnp.asarray(lanes), jnp.asarray(across)
+    return jnp.asarray(lanes)
 
 
 def band_pairs(count):
@@ -100,18 +98,24 @@
             out_ref[at : at + BLOCK] = taps.astype(jnp.bfloat16)
 
 
-def tap_matrix(psi, lon_start, lon_width, first, sent):
-    rows, basis = psi.shape[0], psi.shape[1]
-    psi = psi.reshape(rows, basis, TAPS * TAPS)
-    psi = jnp.pad(psi, ((0, 0), (0, 16 - basis), (0, 32 - TAPS * TAPS)))
-    width = 2 * (rows + TAPS - 1) * BLOCK
+def tap_matrices(psis, lon_start, lon_width, layers):
+    rows, basis = psis[0].shape[0], psis[0].shape[1]
+
+    def kernel(*refs):
+        psi_refs, (start_ref, width_ref), out_refs = refs[: len(layers)], refs[len(layers) : -len(layers)], refs[-len(layers) :]
+        for (first, sent), psi_ref, out_ref in zip(layers, psi_refs, out_refs):
+            taps_kernel(first, sent, psi_ref, start_ref, width_ref, out_ref)
+
+    psis = [psi.reshape(rows, basis, TAPS * TAPS) for psi in psis]
+    psis = [jnp.pad(psi, ((0, 0), (0, 16 - basis), (0, 32 - TAPS * TAPS))) for psi in psis]
+    shape = jax.ShapeDtypeStruct((basis * rows * BLOCK, 2 * (rows + TAPS - 1) * BLOCK), jnp.bfloat16)
     return pl.pallas_call(
-        functools.partial(taps_kernel, first, sent),
-        out_shape=jax.ShapeDtypeStruct((basis * rows * BLOCK, width), jnp.bfloat16),
-        in_specs=[VMEM, SMEM, SMEM],
+        kernel,
+        out_shape=[shape] * len(layers),
+        in_specs=[VMEM] * len(layers) + [SMEM, SMEM],
         cost_estimate=LITTLE,
         compiler_params=vmem_params(),
-    )(psi, lon_start, lon_width)
+    )(*psis, lon_start, lon_width)
 
 
 def harmonic_rows(waves, row):
@@ -119,13 +123,18 @@
     return part[:8]
 
 
-def packet_kernel(latent_ref, across_ref, out_ref, edges_ref, one_ref, two_ref, out_sems):
+def packet_kernel(count, latent_ref, out_ref, edges_ref, one_ref, two_ref, out_sems):
     rows, cols = latent_ref.shape[0], latent_ref.shape[1]
     even = lax.axis_index("lat") % 2 == 0
     first = jnp.where(first_is_south(), 2, 0)
     payload = [(latent_ref.at[pl.ds(at, 2)], ref) for at, ref in ((first, one_ref), (2 - first, two_ref))]
     sends = start_copies(payload, out_sems)
-    across = across_ref[lax.axis_index("lat")]
+    length = cols * lax.axis_size("lat")
+    column = lax.axis_index("lat") * cols + lax.broadcasted_iota(jnp.int32, (count, cols), 1)
+    phase = column * lax.broadcasted_iota(jnp.int32, (count, cols), 0) % length
+    angles = phase.astype(jnp.float32) * jnp.float32(2.0 * math.pi / length)
+    blank = jnp.zeros((16 - 2 * count, cols), jnp.float32)
+    across = jnp.concatenate([jnp.cos(angles), jnp.sin(angles), blank], axis=0).astype(jnp.bfloat16)
     for i in range(rows):
         part = jnp.dot(across, latent_ref[i], preferred_element_type=jnp.float32)
         out_ref[8 * i : 8 * i + 8] = part[:8]
@@ -170,16 +179,15 @@
     one_ref[...], two_ref[...] = payloads(upper_ref[...], lower_ref[...])
 
 
-def cycle_mix(norm_factor, lat_total, total_ref, coef_ref, counts_ref, w_ref):
-    rows, basis = coef_ref.shape[0], coef_ref.shape[1]
-    lanes, channels = total_ref.shape
+def cycle_mix(norm_factor, lat_total, layer, total, coef_ref, counts_ref, w_ref):
+    rows, basis = coef_ref.shape[1], coef_ref.shape[2]
+    lanes, channels = total.shape
     first_row = lax.axis_index("lon") * rows
     columns = []
     for i in range(rows):
         polar = (first_row + i < counts_ref[0]) | (first_row + i >= lat_total - counts_ref[1])
-        columns.append(jnp.where(polar, coef_ref[i].T * norm_factor, 0.0))
+        columns.append(jnp.where(polar, coef_ref[layer, i].T * norm_factor, 0.0))
     coefs = jnp.concatenate(columns, axis=0)
-    total = total_ref[...]
     acc = jnp.zeros((2 * lanes, w_ref.shape[1]), jnp.float32)
     for k in range(basis):
         term = total * coefs[:, k : k + 1]
@@ -240,7 +248,7 @@
     own = pl.ds(low * BLOCK, one_ref.shape[1])
     copies = start_copies([(one_hbm.at[:, own], one_ref), (two_hbm.at[:, own], two_ref)], sems)
     if not first:
-        cycle_ref[...] = mix(total_ref, coef_ref, counts_ref, w_ref)
+        cycle_ref[...] = mix(0, total_ref[...], coef_ref, counts_ref, w_ref)
 
     def half(start, t):
         b = start + t
@@ -279,11 +287,11 @@
 def second_kernel(mix, groups, *refs):
     parts = [refs[at : at + 4] for at in range(0, 4 * len(groups), 4)]
     refs = refs[4 * len(groups) :]
-    total_ref, coef_ref, counts_ref, waves_ref, w_ref, taps_ref, bias_ref, out_hbm, feat_ref, lift_ref, cycle_ref = refs[:11]
-    refs = refs[11:]
+    total_ref, rest_ref, coef_ref, counts_ref, waves_ref, w_ref, taps_ref, bias_ref, out_hbm, *refs = refs
+    feat_ref, lift_ref, cycle_ref, *refs = refs
     out_refs, out_sems = refs[:-1], refs[-1]
     channels = w_ref.shape[1]
-    cycle_ref[...] = mix(total_ref, coef_ref, counts_ref, w_ref)
+    cycle_ref[...] = mix(1, total_ref[...] + rest_ref[...], coef_ref, counts_ref, w_ref)
     place = [(part, at) for part in range(len(groups)) for at in range(parts[part][0].shape[0])]
 
     def half(start, t):
@@ -338,7 +346,7 @@
     hid_blocks = out_blocks + 1
     lanes = row_count * 2 * harm_count
     masks = [2**t - 1 for t in range(1, sectors.bit_length())]
-    tables, across = wave_tables(sectors, col_count, row_count, harm_count)
+    tables = wave_tables(sectors, col_count, row_count, harm_count)
     waves = lax.dynamic_index_in_dim(tables, lax.axis_index("lat"), 0, keepdims=False)
     f32 = lambda *shape: jax.ShapeDtypeStruct(shape, jnp.float32)
     bf16 = lambda *shape: jax.ShapeDtypeStruct(shape, jnp.bfloat16)
@@ -348,14 +356,13 @@
     edge_rows = row_count * EDGE
     rows_shape = bf16(2, col_count, channels)
     packet, edges, *rows = pl.pallas_call(
-        packet_kernel,
+        functools.partial(packet_kernel, harm_count),
         out_shape=(f32(lanes + edge_rows, channels), f32(2, edge_rows, channels), rows_shape, rows_shape),
-        in_specs=[VMEM, VMEM],
         out_specs=[VMEM, VMEM, HBM, HBM],
         scratch_shapes=[sems(2)],
         cost_estimate=LITTLE,
         compiler_params=vmem_params(),
-    )(latent, across)
+    )(latent)
     row_one, row_two = exchange(rows)
     gots = [swap(packet, masks[0])]
     for mask in masks[1:]:
@@ -377,14 +384,16 @@
 
     mix = functools.partial(cycle_mix, norm_factor, lat_total)
     mix_shape = (row_count * 32, channels)
-    coefs = lambda cycle: cycle.reshape(row_count, basis, 2 * harm_count)
+    coefs = jnp.stack([cycle_one, cycle_two]).reshape(2, row_count, basis, 2 * harm_count)
 
     def scratch(count):
         size = count * row_count * BLOCK
         return [held(size, basis * channels), held(size, mix_shape[0])]
 
-    taps_one = tap_matrix(psi_one, lon_start, lon_width, BLOCK - EDGE, False)
-    cut = hid_blocks // 2
+    taps_one, taps_two = tap_matrices(
+        (psi_one, psi_two), lon_start, lon_width, ((BLOCK - EDGE, False), (0, True))
+    )
+    cut = hid_blocks * 28 // 46
     hidden = []
     for first, count in ((0, cut), (cut, hid_blocks - cut)):
         operands = (row_one, row_two, latent, waves, w_one, side_one, side_upper, side_lower, side_two, taps_one)
@@ -396,7 +405,7 @@
             operands += (harmonics, mix_one)
             in_specs += [VMEM, VMEM]
         else:
-            operands += (total_one, coefs(cycle_one), polar_counts)
+            operands += (total_one, coefs, polar_counts)
             in_specs += [VMEM, VMEM, SMEM]
             out_shape += (bf16(*mix_shape),)
         own = (min(first + count, out_blocks) - max(first - 1, 0)) * BLOCK
@@ -412,19 +421,19 @@
         got_one, got_two = exchange((pay_one, pay_two))
         hidden += [got_one, pay_one, pay_two, got_two]
 
-    total_two = harmonics + swap(harmonics, masks[0])
+    hops = [2**t for t in range(sectors.bit_length() - 1)]
+    total_two = harmonics + swap(harmonics, hops[0])
+    for hop in hops[1:-1]:
+        total_two = total_two + swap(total_two, hop)
     for got in (hidden[0], hidden[3]):
         total_two += 0.0 * got[0, 0, :1].astype(jnp.float32)
-    for mask in masks[1:]:
-        total_two = total_two + swap(total_two, mask)
-    psi_two, _ = lax.optimization_barrier((psi_two, harmonics))
-    taps_two = tap_matrix(psi_two, lon_start, lon_width, 0, True)
+    rest_two = swap(total_two, hops[-1])
     groups = (cut, out_blocks - cut)
-    operands = (*hidden, total_two, coefs(cycle_two), polar_counts, waves, w_two, taps_two, b_two[None])
+    operands = (*hidden, total_two, rest_two, coefs, polar_counts, waves, w_two, taps_two, b_two[None])
     return pl.pallas_call(
         functools.partial(second_kernel, mix, groups),
         out_shape=bf16(row_count, col_count, channels),
-        in_specs=[VMEM] * (len(hidden) + 2) + [SMEM] + [VMEM] * 4,
+        in_specs=[VMEM] * (len(hidden) + 3) + [SMEM] + [VMEM] * 4,
         out_specs=HBM,
         scratch_shapes=scratch(max(groups))
         + [held(*mix_shape)]

time: 67.9 us -> 65 us (0.957)
  Pallas kernels: 27.4 us -> 25.5 us
  starting transfers between devices: 25.4 us -> 24.2 us
  waiting for transfers between devices: 7.6 us -> 8.48 us
    unnamed x40 -> x42, local copies, waits for them, and re-layouts: 3.92 us -> 2.01 us
    another operation x0 -> x2, local copies, waits for them, and re-layouts: none -> 1.66 us  [body(): jnp.stack([cycle_one, cycle_two])]
    ppermute x8, waiting for transfers between devices: 0.02 us -> 1.15 us  [exchange(): lax.ppermute(value, 'lon', pair)]
    pallas_call x2, Pallas kernels: 12.5 us -> 11.8 us  [body(): pl.pallas_call(functools.partial(first_kernel, mix, first, count), out_sh...]
    ppermute x6, starting transfers between devices: 7.9 us -> 7.2 us  [swap(): lax.ppermute(value, 'lat', [(i, i ^ mask) for i in range(lax.axis_size('l...]
    pallas_call x3 -> x2, Pallas kernels: 3.04 us -> 2.46 us  [the longest x1 1.28 us: tap_matrices(): pl.pallas_call(kernel, out_shape=[shape] * len(layers), in_specs=[VMEM] *...]
  transfers between devices with their start and end apart: 14 -> 14, of which waited for: 4 -> 5; matrix products, arithmetic and copies ran while one was open for 4% -> 6% of each run, Pallas kernels for 13% -> 9%
where the time goes in v4:
time: 65 us; the launch traced here: 64.5 us
  Pallas kernels  25.5 us (39%)
  starting transfers between devices  24.2 us (37%)
  waiting for transfers between devices  8.48 us (13%)
  local copies, waits for them, and re-layouts  5.68 us (9%)
    ppermute x8, starting transfers between devices, exchange(): lax.ppermute(value, 'lon', pair)  17 us
    pallas_call x2, Pallas kernels, body(): pl.pallas_call(functools.partial(first_kernel, mix, first, count), out_sh...  11.8 us
    pallas_call x1, Pallas kernels, body(): pl.pallas_call(functools.partial(second_kernel, mix, groups), out_shape=b...  11.2 us
    ppermute x6, waiting for transfers between devices, swap(): lax.ppermute(value, 'lat', [(i, i ^ mask) for i in range(lax.axis_size('l...  7.33 us
    ppermute x6, starting transfers between devices, swap(): lax.ppermute(value, 'lat', [(i, i ^ mask) for i in range(lax.axis_size('l...  7.2 us
    unnamed x42, local copies, waits for them, and re-layouts  2.01 us
    another operation x2, local copies, waits for them, and re-layouts, body(): jnp.stack([cycle_one, cycle_two])  1.66 us
  transfers between devices with their start and end apart: 14, of which 5 were waited for; matrix products, arithmetic and copies ran while one was open for 6% of the time, Pallas kernels for 9%

profile of v4, /device:TPU:0, one launch (start us, length us, event | category | flops | bytes accessed | tf_op | source)
XLA Modules:
  0.0 64.5 jit_solution(16280478456626081441)
XLA Ops:
  0.0 1.4 %copy-done = bf16[4,720,256]{2,1,0:T(8,128)(2,1)S(1)} copy-done((bf16[4,720,256]{2,1,0:T(8,128)(2,1)S(1)}, bf16[4,720,256]{2,1,0:T(8,128)(2,1)}, u32[]{:S(2)}) %copy-start) | copy-done | bytes 1474584
  1.4 0.0 copy-start.2
  1.4 0.0 copy-start.5
  1.4 0.0 copy-start.8
  1.4 1.2 %shard_map.127 = (f32[48,256]{1,0:T(8,128)S(1)}, f32[2,16,256]{2,1,0:T(8,128)S(1)}, bf16[2,720,256]{2,1,0:T(8,128)(2,1)}, bf16[2,720,256]{2,1,0:T(8,128)(2,1)}) custom-call(bf16[4,720,256]{2,1,0:T(8,128)(2,1)S(1)} %copy-done), custom_call_target="tpu_custom_call" | custom-call | flops 1 | bytes 1 | tf_op jit(solution)/shard_map/pallas_call | solution.py:358
  2.6 3.1 %collective-permute-start = (bf16[2,720,256]{2,1,0:T(8,128)(2,1)}, bf16[2,720,256]{2,1,0:T(8,128)(2,1)}, u32[]{:S(2)}, u32[]{:S(2)}) collective-permute-start(bf16[2,720,256]{2,1,0:T(8,128)(2,1)} %get-tuple-element.23), channel_id=1, source_target_pairs={{0,1},{2,3},{1,0},{3,2},{4,5},{6,7},{5,4},{7,6},{8,9},{10,11},{9,8... | collective-permute-start | bytes 2211848 | tf_op jit(solution)/shard_map/ppermute | solution.py:52
  5.7 1.5 %collective-permute-start.1 = (bf16[2,720,256]{2,1,0:T(8,128)(2,1)}, bf16[2,720,256]{2,1,0:T(8,128)(2,1)}, u32[]{:S(2)}, u32[]{:S(2)}) collective-permute-start(bf16[2,720,256]{2,1,0:T(8,128)(2,1)} %get-tuple-element.24), channel_id=1, source_target_pairs={{1,2},{2,1},{5,6},{6,5},{9,10},{10,9},{13,14},{14,13},{17,18},{18,... | collective-permute-start | bytes 2211848 | tf_op jit(solution)/shard_map/ppermute | solution.py:52
  7.2 0.0 collective-permute-start.2
  7.2 1.2 %collective-permute-done.2.got_ref.refs_1_ = f32[48,256]{1,0:T(8,128)S(1)} collective-permute-done((f32[48,256]{1,0:T(8,128)S(1)}, f32[48,256]{1,0:T(8,128)S(1)}, u32[]{:S(2)}, u32[]{:S(2)}) %collective-permute-start.2) | collective-permute-done | bytes 49184 | tf_op jit(solution)/shard_map/ppermute | solution.py:323
  8.5 1.3 %collective-permute-start.3 = (f32[48,256]{1,0:T(8,128)S(1)}, f32[48,256]{1,0:T(8,128)S(1)}, u32[]{:S(2)}, u32[]{:S(2)}) collective-permute-start(f32[48,256]{1,0:T(8,128)S(1)} %shard_map.128.packet_ref), channel_id=1, source_target_pairs={{0,12},{4,8},{8,4},{12,0},{16,28},{20,24},{24,20},{28,16},{1,13},{... | collective-permute-start | bytes 147464 | tf_op jit(solution)/shard_map/ppermute | solution.py:323
  9.8 2.5 %collective-permute-done.3.got_ref.refs_2_ = f32[48,256]{1,0:T(8,128)S(1)} collective-permute-done((f32[48,256]{1,0:T(8,128)S(1)}, f32[48,256]{1,0:T(8,128)S(1)}, u32[]{:S(2)}, u32[]{:S(2)}) %collective-permute-start.3) | collective-permute-done | bytes 49184 | tf_op jit(solution)/shard_map/ppermute | solution.py:323
  12.3 2.7 %collective-permute-start.4 = (f32[48,256]{1,0:T(8,128)S(1)}, f32[48,256]{1,0:T(8,128)S(1)}, u32[]{:S(2)}, u32[]{:S(2)}) collective-permute-start(f32[48,256]{1,0:T(8,128)S(1)} %shard_map.129.refs_0_), channel_id=1, source_target_pairs={{0,28},{4,24},{8,20},{12,16},{16,12},{20,8},{24,4},{28,0},{1,29},{... | collective-permute-start | bytes 147464 | tf_op jit(solution)/shard_map/ppermute | solution.py:323
  14.9 1.0 %dynamic-slice_bitcast_fusion.waves_ref.refs_12_ = bf16[2,736,128]{2,1,0:T(8,128)(2,1)S(1)} fusion(bf16[8,2,736,128]{3,2,1,0:T(8,128)(2,1)} %constant.19.clone, s32[]{:T(128)S(6)} %select_n.4), kind=kLoop, calls=%fused_computation | loop fusion | bytes 753668 | tf_op jit(solution)/shard_map/jit(dynamic_index_in_dim)/squeeze | solution.py:350
  15.9 0.0 copy-start.3
  16.0 0.8 %copy.20 = f32[1,4,9,8]{3,2,1,0:T(8,128)S(1)} copy(f32[1,4,9,8]{2,3,1,0:T(8,128)} %bitcast.14) | data formatting | bytes 2304 | tf_op jit(solution)/shard_map/stack | solution.py:387
  16.8 0.8 %copy.21 = f32[1,4,9,8]{3,2,1,0:T(8,128)S(1)} copy(f32[1,4,9,8]{2,3,1,0:T(8,128)} %bitcast.15) | data formatting | bytes 2304 | tf_op jit(solution)/shard_map/stack | solution.py:387
  17.6 0.0 collective-permute-done.4.refs_3_
  17.7 3.7 %collective-permute-start.5 = (bf16[2,2,16,256]{3,2,1,0:T(8,128)(2,1)S(1)}, bf16[2,2,16,256]{3,2,1,0:T(8,128)(2,1)S(1)}, u32[]{:S(2)}, u32[]{:S(2)}) collective-permute-start(bf16[2,2,16,256]{3,2,1,0:T(8,128)(2,1)S(1)} %get-tuple-element.27), channel_id=1, source_target_pairs={{0,1},{2,3},{1,0},{3,2},{4,5},{6,7},{5,4},{7,6},{8,9},{10,11},{9,8... | collective-permute-start | bytes 98312 | tf_op jit(solution)/shard_map/ppermute | solution.py:52
  21.3 0.7 %collective-permute-start.6 = (bf16[2,2,16,256]{3,2,1,0:T(8,128)(2,1)S(1)}, bf16[2,2,16,256]{3,2,1,0:T(8,128)(2,1)S(1)}, u32[]{:S(2)}, u32[]{:S(2)}) collective-permute-start(bf16[2,2,16,256]{3,2,1,0:T(8,128)(2,1)S(1)} %get-tuple-element.30), channel_id=1, source_target_pairs={{1,2},{2,1},{5,6},{6,5},{9,10},{10,9},{13,14},{14,13},{17,18},{18,... | collective-permute-start | bytes 98312 | tf_op jit(solution)/shard_map/ppermute | solution.py:52
  22.0 0.0 copy-start.4
  22.0 0.0 copy-done.15
  22.0 0.1 copy.18
  22.1 0.9 %copy.19 = bf16[4,9,25]{2,1,0:T(8,128)(2,1)S(1)} copy(bf16[4,9,25]{1,0,2:T(4,128)(2,1)} %bitcast.13) | data formatting | bytes 3600 | tf_op jit(solution)/shard_map/reshape | solution.py:109
  23.0 1.3 %shard_map.131 = (bf16[576,256]{1,0:T(8,128)(2,1)S(1)}, bf16[576,256]{1,0:T(8,128)(2,1)S(1)}) custom-call(bf16[4,16,32]{2,1,0:T(8,128)(2,1)S(1)} %pad.7.refs_0_, bf16[4,16,32]{2,1,0:T(8,128)(2,1)S(1)} %pad.8.refs_1_, s32[16]{0:T(128)S(1)} %copy-done.6, s32[16]{0:T(128)S(1)} %copy-done.7), custom_call_target="tpu_custom_call" | custom-call | flops 1 | bytes 1 | tf_op jit(solution)/shard_map/pallas_call | solution.py:112
  24.3 0.0 collective-permute-done.5.side_one_ref
  24.3 0.0 collective-permute-done.6.side_two_ref
  24.4 0.0 collective-permute-done.one_hbm
  24.4 0.0 collective-permute-done.1.two_hbm
  24.4 7.1 %shard_map.132 = (bf16[28,2,16,256]{3,2,1,0:T(8,128)(2,1)S(1)}, bf16[28,2,16,256]{3,2,1,0:T(8,128)(2,1)S(1)}, f32[32,256]{1,0:T(8,128)S(1)}, bf16[128,256]{1,0:T(8,128)(2,1)S(1)}) custom-call(bf16[2,720,256]{2,1,0:T(8,128)(2,1)} %collective-permute-done.one_hbm, bf16[2,720,256]{2,1,0:T(8,128)(2,1)} %collective-permute-done.1.two_hbm, ...), custom_call_target="tpu_custom_call" | custom-call | flops 1 | bytes 1 | tf_op jit(solution)/shard_map/pallas_call | solution.py:412
  31.6 3.5 %collective-permute-start.7 = (bf16[28,2,16,256]{3,2,1,0:T(8,128)(2,1)S(1)}, bf16[28,2,16,256]{3,2,1,0:T(8,128)(2,1)S(1)}, u32[]{:S(2)}, u32[]{:S(2)}) collective-permute-start(bf16[28,2,16,256]{3,2,1,0:T(8,128)(2,1)S(1)} %get-tuple-element.33.refs_1_), channel_id=1, source_target_pairs={{0,1},{2,3},{1,0},{3,2},{4,5},{6,7},{5,4},{7,6},{8,9},{10,11},{9,8... | collective-permute-start | bytes 1376264 | tf_op jit(solution)/shard_map/ppermute | solution.py:52
  35.1 0.7 %collective-permute-start.8 = (bf16[28,2,16,256]{3,2,1,0:T(8,128)(2,1)S(1)}, bf16[28,2,16,256]{3,2,1,0:T(8,128)(2,1)S(1)}, u32[]{:S(2)}, u32[]{:S(2)}) collective-permute-start(bf16[28,2,16,256]{3,2,1,0:T(8,128)(2,1)S(1)} %get-tuple-element.34.refs_2_), channel_id=1, source_target_pairs={{1,2},{2,1},{5,6},{6,5},{9,10},{10,9},{13,14},{14,13},{17,18},{18,... | collective-permute-start | bytes 1376264 | tf_op jit(solution)/shard_map/ppermute | solution.py:52
  35.8 0.0 copy-done.3
  35.8 4.7 %shard_map.133 = (bf16[18,2,16,256]{3,2,1,0:T(8,128)(2,1)S(1)}, bf16[18,2,16,256]{3,2,1,0:T(8,128)(2,1)S(1)}, f32[32,256]{1,0:T(8,128)S(1)}) custom-call(bf16[2,720,256]{2,1,0:T(8,128)(2,1)} %collective-permute-done.one_hbm, bf16[2,720,256]{2,1,0:T(8,128)(2,1)} %collective-permute-done.1.two_hbm, bf16[4,720,256]{2,1,0:T(8,128)(2,1)S(1)} %copy-done.1, ...), custom_call_target="tpu_custom_call" | custom-call | flops 1 | bytes 1 | tf_op jit(solution)/shard_map/pallas_call | solution.py:412
  40.5 0.1 collective-permute-start.11
  40.6 3.0 %collective-permute-start.9 = (bf16[18,2,16,256]{3,2,1,0:T(8,128)(2,1)S(1)}, bf16[18,2,16,256]{3,2,1,0:T(8,128)(2,1)S(1)}, u32[]{:S(2)}, u32[]{:S(2)}) collective-permute-start(bf16[18,2,16,256]{3,2,1,0:T(8,128)(2,1)S(1)} %get-tuple-element.37.refs_5_), channel_id=1, source_target_pairs={{0,1},{2,3},{1,0},{3,2},{4,5},{6,7},{5,4},{7,6},{8,9},{10,11},{9,8... | collective-permute-start | bytes 884744 | tf_op jit(solution)/shard_map/ppermute | solution.py:52
  43.7 0.8 %collective-permute-start.10 = (bf16[18,2,16,256]{3,2,1,0:T(8,128)(2,1)S(1)}, bf16[18,2,16,256]{3,2,1,0:T(8,128)(2,1)S(1)}, u32[]{:S(2)}, u32[]{:S(2)}) collective-permute-start(bf16[18,2,16,256]{3,2,1,0:T(8,128)(2,1)S(1)} %get-tuple-element.38.refs_6_), channel_id=1, source_target_pairs={{1,2},{2,1},{5,6},{6,5},{9,10},{10,9},{13,14},{14,13},{17,18},{18,... | collective-permute-start | bytes 884744 | tf_op jit(solution)/shard_map/ppermute | solution.py:52
  44.5 0.0 collective-permute-done.11
  44.5 1.6 %collective-permute-start.12 = (f32[32,256]{1,0:T(8,128)S(1)}, f32[32,256]{1,0:T(8,128)S(1)}, u32[]{:S(2)}, u32[]{:S(2)}) collective-permute-start(f32[32,256]{1,0:T(8,128)S(1)} %add.31), channel_id=1, source_target_pairs={{0,8},{4,12},{8,0},{12,4},{16,24},{20,28},{24,16},{28,20},{1,9},{5... | collective-permute-start | bytes 98312 | tf_op jit(solution)/shard_map/ppermute | solution.py:323
  46.1 0.0 collective-permute-done.7.refs_0_
  46.1 0.0 collective-permute-done.8.refs_3_
  46.1 2.4 %collective-permute-done.12 = f32[32,256]{1,0:T(8,128)S(1)} collective-permute-done((f32[32,256]{1,0:T(8,128)S(1)}, f32[32,256]{1,0:T(8,128)S(1)}, u32[]{:S(2)}, u32[]{:S(2)}) %collective-permute-start.12) | collective-permute-done | bytes 32800 | tf_op jit(solution)/shard_map/ppermute | solution.py:323
  48.5 1.6 %collective-permute-start.13 = (f32[32,256]{1,0:T(8,128)S(1)}, f32[32,256]{1,0:T(8,128)S(1)}, u32[]{:S(2)}, u32[]{:S(2)}) collective-permute-start(f32[32,256]{1,0:T(8,128)S(1)} %add_add_fusion.refs_8_), channel_id=1, source_target_pairs={{0,16},{4,20},{8,24},{12,28},{16,0},{20,4},{24,8},{28,12},{1,17},{... | collective-permute-start | bytes 98312 | tf_op jit(solution)/shard_map/ppermute | solution.py:323
  50.1 1.1 %collective-permute-done.9.refs_4_ = bf16[18,2,16,256]{3,2,1,0:T(8,128)(2,1)S(1)} collective-permute-done((bf16[18,2,16,256]{3,2,1,0:T(8,128)(2,1)S(1)}, bf16[18,2,16,256]{3,2,1,0:T(8,128)(2,1)S(1)}, u32[]{:S(2)}, u32[]{:S(2)}) %collective-permute-start.9) | collective-permute-done | bytes 294944 | tf_op jit(solution)/shard_map/ppermute | solution.py:52
  51.3 0.0 collective-permute-done.10.refs_7_
  51.3 1.3 %collective-permute-done.13.refs_9_ = f32[32,256]{1,0:T(8,128)S(1)} collective-permute-done((f32[32,256]{1,0:T(8,128)S(1)}, f32[32,256]{1,0:T(8,128)S(1)}, u32[]{:S(2)}, u32[]{:S(2)}) %collective-permute-start.13) | collective-permute-done | bytes 32800 | tf_op jit(solution)/shard_map/ppermute | solution.py:323
  52.5 0.0 copy-done.16
  52.6 0.6 copy-done.20
  53.1 11.2 %shard_map.134 = bf16[4,720,256]{2,1,0:T(8,128)(2,1)} custom-call(bf16[28,2,16,256]{3,2,1,0:T(8,128)(2,1)} %copy-done.16, bf16[28,2,16,256]{3,2,1,0:T(8,128)(2,1)} %copy-done.9, bf16[28,2,16,256]{3,2,1,0:T(8,128)(2,1)} %copy-done.10, bf16[28,2,16,256]{3,2,1,0:T(8,128)(2,1)} %copy-done.17, bf16[18,2,16,256]{3,2,1,0:T(8,128)(2,1)} %copy-done.18, ...), custom_call_target="tpu_custom_call" | custom-call | flops 13589544960 | bytes 8000000 | tf_op jit(solution)/shard_map/pallas_call | solution.py:433
  (42 shorter events, 0.2 us)
Async XLA Ops:
  0.0 1.4 %copy-start = (bf16[4,720,256]{2,1,0:T(8,128)(2,1)S(1)}, bf16[4,720,256]{2,1,0:T(8,128)(2,1)}, u32[]{:S(2)}) copy-start(bf16[4,720,256]{2,1,0:T(8,128)(2,1)} %mid_ref.3) | copy-start | bytes 4423684
  1.4 20.6 %copy-start.15 = (bf16[4,9,5,5]{1,0,3,2:T(4,128)(2,1)S(1)}, bf16[4,9,5,5]{1,0,3,2:T(4,128)(2,1)}, u32[]{:S(2)}) copy-start(bf16[4,9,5,5]{1,0,3,2:T(4,128)(2,1)} %param.14) | copy-start | bytes 5404
  1.4 21.6 %copy-start.6 = (s32[16]{0:T(128)S(1)}, s32[16]{0:T(128)}, u32[]{:S(2)}) copy-start(s32[16]{0:T(128)} %refs_2_.2) | copy-start | bytes 196
  1.4 21.7 %copy-start.7 = (s32[16]{0:T(128)S(1)}, s32[16]{0:T(128)}, u32[]{:S(2)}) copy-start(s32[16]{0:T(128)} %refs_3_.1) | copy-start | bytes 196
  1.4 23.0 %copy-start.1 = (bf16[4,720,256]{2,1,0:T(8,128)(2,1)S(1)}, bf16[4,720,256]{2,1,0:T(8,128)(2,1)}, u32[]{:S(2)}) copy-start(bf16[4,720,256]{2,1,0:T(8,128)(2,1)} %mid_ref.3) | copy-start | bytes 4423684
  1.4 23.0 %copy-start.2 = (bf16[2304,256]{1,0:T(8,128)(2,1)S(1)}, bf16[2304,256]{1,0:T(8,128)(2,1)}, u32[]{:S(2)}) copy-start(bf16[2304,256]{1,0:T(8,128)(2,1)} %w_ref.3) | copy-start | bytes 3538948
  1.4 23.0 %copy-start.5 = (f32[256]{0:T(256)S(1)}, f32[256]{0:T(256)}, u32[]{:S(2)}) copy-start(f32[256]{0:T(256)} %param.20) | copy-start | bytes 3076
  1.4 23.0 %copy-start.8 = (s32[2]{0:T(128)S(1)}, s32[2]{0:T(128)}, u32[]{:S(2)}) copy-start(s32[2]{0:T(128)} %refs_11_.1) | copy-start | bytes 28
  2.6 21.8 %collective-permute-start = (bf16[2,720,256]{2,1,0:T(8,128)(2,1)}, bf16[2,720,256]{2,1,0:T(8,128)(2,1)}, u32[]{:S(2)}, u32[]{:S(2)}) collective-permute-start(bf16[2,720,256]{2,1,0:T(8,128)(2,1)} %get-tuple-element.23), channel_id=1, source_target_pairs={{0,1},{2,3},{1,0},{3,2},{4,5},{6,7},{5,4},{7,6},{8,9},{10,11},{9,8... | collective-permute-start | bytes 2211848 | tf_op jit(solution)/shard_map/ppermute | solution.py:52
  5.7 18.7 %collective-permute-start.1 = (bf16[2,720,256]{2,1,0:T(8,128)(2,1)}, bf16[2,720,256]{2,1,0:T(8,128)(2,1)}, u32[]{:S(2)}, u32[]{:S(2)}) collective-permute-start(bf16[2,720,256]{2,1,0:T(8,128)(2,1)} %get-tuple-element.24), channel_id=1, source_target_pairs={{1,2},{2,1},{5,6},{6,5},{9,10},{10,9},{13,14},{14,13},{17,18},{18,... | collective-permute-start | bytes 2211848 | tf_op jit(solution)/shard_map/ppermute | solution.py:52
  7.2 1.2 %collective-permute-start.2 = (f32[48,256]{1,0:T(8,128)S(1)}, f32[48,256]{1,0:T(8,128)S(1)}, u32[]{:S(2)}, u32[]{:S(2)}) collective-permute-start(f32[48,256]{1,0:T(8,128)S(1)} %get-tuple-element.25.packet_ref), channel_id=1, source_target_pairs={{0,4},{4,0},{8,12},{12,8},{16,20},{20,16},{24,28},{28,24},{1,5},{5... | collective-permute-start | bytes 147464 | tf_op jit(solution)/shard_map/ppermute | solution.py:323
  8.5 3.8 %collective-permute-start.3 = (f32[48,256]{1,0:T(8,128)S(1)}, f32[48,256]{1,0:T(8,128)S(1)}, u32[]{:S(2)}, u32[]{:S(2)}) collective-permute-start(f32[48,256]{1,0:T(8,128)S(1)} %shard_map.128.packet_ref), channel_id=1, source_target_pairs={{0,12},{4,8},{8,4},{12,0},{16,28},{20,24},{24,20},{28,16},{1,13},{... | collective-permute-start | bytes 147464 | tf_op jit(solution)/shard_map/ppermute | solution.py:323
  12.3 5.4 %collective-permute-start.4 = (f32[48,256]{1,0:T(8,128)S(1)}, f32[48,256]{1,0:T(8,128)S(1)}, u32[]{:S(2)}, u32[]{:S(2)}) collective-permute-start(f32[48,256]{1,0:T(8,128)S(1)} %shard_map.129.refs_0_), channel_id=1, source_target_pairs={{0,28},{4,24},{8,20},{12,16},{16,12},{20,8},{24,4},{28,0},{1,29},{... | collective-permute-start | bytes 147464 | tf_op jit(solution)/shard_map/ppermute | solution.py:323
  15.9 19.8 %copy-start.3 = (bf16[2,736,128]{2,1,0:T(8,128)(2,1)}, bf16[2,736,128]{2,1,0:T(8,128)(2,1)S(1)}, u32[]{:S(2)}) copy-start(bf16[2,736,128]{2,1,0:T(8,128)(2,1)S(1)} %dynamic-slice_bitcast_fusion.waves_ref.refs_12_) | copy-start | bytes 1130500
  17.7 6.7 %collective-permute-start.5 = (bf16[2,2,16,256]{3,2,1,0:T(8,128)(2,1)S(1)}, bf16[2,2,16,256]{3,2,1,0:T(8,128)(2,1)S(1)}, u32[]{:S(2)}, u32[]{:S(2)}) collective-permute-start(bf16[2,2,16,256]{3,2,1,0:T(8,128)(2,1)S(1)} %get-tuple-element.27), channel_id=1, source_target_pairs={{0,1},{2,3},{1,0},{3,2},{4,5},{6,7},{5,4},{7,6},{8,9},{10,11},{9,8... | collective-permute-start | bytes 98312 | tf_op jit(solution)/shard_map/ppermute | solution.py:52
  21.3 3.0 %collective-permute-start.6 = (bf16[2,2,16,256]{3,2,1,0:T(8,128)(2,1)S(1)}, bf16[2,2,16,256]{3,2,1,0:T(8,128)(2,1)S(1)}, u32[]{:S(2)}, u32[]{:S(2)}) collective-permute-start(bf16[2,2,16,256]{3,2,1,0:T(8,128)(2,1)S(1)} %get-tuple-element.30), channel_id=1, source_target_pairs={{1,2},{2,1},{5,6},{6,5},{9,10},{10,9},{13,14},{14,13},{17,18},{18,... | collective-permute-start | bytes 98312 | tf_op jit(solution)/shard_map/ppermute | solution.py:52
  22.0 9.5 %copy-start.4 = (f32[2,4,9,8]{3,2,1,0:T(8,128)}, f32[2,4,9,8]{3,2,1,0:T(8,128)S(1)}, u32[]{:S(2)}) copy-start(f32[2,4,9,8]{3,2,1,0:T(8,128)S(1)} %pad_maximum_fusion.refs_1_.refs_10_) | copy-start | bytes 6916
  24.3 7.2 %copy-start.11 = (bf16[576,256]{1,0:T(8,128)(2,1)}, bf16[576,256]{1,0:T(8,128)(2,1)S(1)}, u32[]{:S(2)}) copy-start(bf16[576,256]{1,0:T(8,128)(2,1)S(1)} %get-tuple-element.40.refs_14_) | copy-start | bytes 884740
  31.5 9.0 %copy-start.9 = (bf16[28,2,16,256]{3,2,1,0:T(8,128)(2,1)}, bf16[28,2,16,256]{3,2,1,0:T(8,128)(2,1)S(1)}, u32[]{:S(2)}) copy-start(bf16[28,2,16,256]{3,2,1,0:T(8,128)(2,1)S(1)} %get-tuple-element.33.refs_1_) | copy-start | bytes 1376260
  31.5 9.0 %copy-start.10 = (bf16[28,2,16,256]{3,2,1,0:T(8,128)(2,1)}, bf16[28,2,16,256]{3,2,1,0:T(8,128)(2,1)S(1)}, u32[]{:S(2)}) copy-start(bf16[28,2,16,256]{3,2,1,0:T(8,128)(2,1)S(1)} %get-tuple-element.34.refs_2_) | copy-start | bytes 1376260
  31.6 14.5 %collective-permute-start.7 = (bf16[28,2,16,256]{3,2,1,0:T(8,128)(2,1)S(1)}, bf16[28,2,16,256]{3,2,1,0:T(8,128)(2,1)S(1)}, u32[]{:S(2)}, u32[]{:S(2)}) collective-permute-start(bf16[28,2,16,256]{3,2,1,0:T(8,128)(2,1)S(1)} %get-tuple-element.33.refs_1_), channel_id=1, source_target_pairs={{0,1},{2,3},{1,0},{3,2},{4,5},{6,7},{5,4},{7,6},{8,9},{10,11},{9,8... | collective-permute-start | bytes 1376264 | tf_op jit(solution)/shard_map/ppermute | solution.py:52
  35.1 11.0 %collective-permute-start.8 = (bf16[28,2,16,256]{3,2,1,0:T(8,128)(2,1)S(1)}, bf16[28,2,16,256]{3,2,1,0:T(8,128)(2,1)S(1)}, u32[]{:S(2)}, u32[]{:S(2)}) collective-permute-start(bf16[28,2,16,256]{3,2,1,0:T(8,128)(2,1)S(1)} %get-tuple-element.34.refs_2_), channel_id=1, source_target_pairs={{1,2},{2,1},{5,6},{6,5},{9,10},{10,9},{13,14},{14,13},{17,18},{18,... | collective-permute-start | bytes 1376264 | tf_op jit(solution)/shard_map/ppermute | solution.py:52
  40.5 12.0 %copy-start.12 = (bf16[18,2,16,256]{3,2,1,0:T(8,128)(2,1)}, bf16[18,2,16,256]{3,2,1,0:T(8,128)(2,1)S(1)}, u32[]{:S(2)}) copy-start(bf16[18,2,16,256]{3,2,1,0:T(8,128)(2,1)S(1)} %get-tuple-element.37.refs_5_) | copy-start | bytes 884740
  40.5 12.0 %copy-start.13 = (bf16[18,2,16,256]{3,2,1,0:T(8,128)(2,1)}, bf16[18,2,16,256]{3,2,1,0:T(8,128)(2,1)S(1)}, u32[]{:S(2)}) copy-start(bf16[18,2,16,256]{3,2,1,0:T(8,128)(2,1)S(1)} %get-tuple-element.38.refs_6_) | copy-start | bytes 884740
  40.5 4.0 %collective-permute-start.11 = (f32[32,256]{1,0:T(8,128)S(1)}, f32[32,256]{1,0:T(8,128)S(1)}, u32[]{:S(2)}, u32[]{:S(2)}) collective-permute-start(f32[32,256]{1,0:T(8,128)S(1)} %get-tuple-element.39), channel_id=1, source_target_pairs={{0,4},{4,0},{8,12},{12,8},{16,20},{20,16},{24,28},{28,24},{1,5},{5... | collective-permute-start | bytes 98312 | tf_op jit(solution)/shard_map/ppermute | solution.py:323
  40.6 10.6 %collective-permute-start.9 = (bf16[18,2,16,256]{3,2,1,0:T(8,128)(2,1)S(1)}, bf16[18,2,16,256]{3,2,1,0:T(8,128)(2,1)S(1)}, u32[]{:S(2)}, u32[]{:S(2)}) collective-permute-start(bf16[18,2,16,256]{3,2,1,0:T(8,128)(2,1)S(1)} %get-tuple-element.37.refs_5_), channel_id=1, source_target_pairs={{0,1},{2,3},{1,0},{3,2},{4,5},{6,7},{5,4},{7,6},{8,9},{10,11},{9,8... | collective-permute-start | bytes 884744 | tf_op jit(solution)/shard_map/ppermute | solution.py:52
  43.7 7.6 %collective-permute-start.10 = (bf16[18,2,16,256]{3,2,1,0:T(8,128)(2,1)S(1)}, bf16[18,2,16,256]{3,2,1,0:T(8,128)(2,1)S(1)}, u32[]{:S(2)}, u32[]{:S(2)}) collective-permute-start(bf16[18,2,16,256]{3,2,1,0:T(8,128)(2,1)S(1)} %get-tuple-element.38.refs_6_), channel_id=1, source_target_pairs={{1,2},{2,1},{5,6},{6,5},{9,10},{10,9},{13,14},{14,13},{17,18},{18,... | collective-permute-start | bytes 884744 | tf_op jit(solution)/shard_map/ppermute | solution.py:52
  44.5 4.0 %collective-permute-start.12 = (f32[32,256]{1,0:T(8,128)S(1)}, f32[32,256]{1,0:T(8,128)S(1)}, u32[]{:S(2)}, u32[]{:S(2)}) collective-permute-start(f32[32,256]{1,0:T(8,128)S(1)} %add.31), channel_id=1, source_target_pairs={{0,8},{4,12},{8,0},{12,4},{16,24},{20,28},{24,16},{28,20},{1,9},{5... | collective-permute-start | bytes 98312 | tf_op jit(solution)/shard_map/ppermute | solution.py:323
  46.1 6.4 %copy-start.16 = (bf16[28,2,16,256]{3,2,1,0:T(8,128)(2,1)}, bf16[28,2,16,256]{3,2,1,0:T(8,128)(2,1)S(1)}, u32[]{:S(2)}) copy-start(bf16[28,2,16,256]{3,2,1,0:T(8,128)(2,1)S(1)} %collective-permute-done.7.refs_0_) | copy-start | bytes 1376260
  46.1 6.4 %copy-start.17 = (bf16[28,2,16,256]{3,2,1,0:T(8,128)(2,1)}, bf16[28,2,16,256]{3,2,1,0:T(8,128)(2,1)S(1)}, u32[]{:S(2)}) copy-start(bf16[28,2,16,256]{3,2,1,0:T(8,128)(2,1)S(1)} %collective-permute-done.8.refs_3_) | copy-start | bytes 1376260
  48.5 4.0 %copy-start.14 = (f32[32,256]{1,0:T(8,128)}, f32[32,256]{1,0:T(8,128)S(1)}, u32[]{:S(2)}) copy-start(f32[32,256]{1,0:T(8,128)S(1)} %add_add_fusion.refs_8_) | copy-start | bytes 98308
  48.5 4.0 %collective-permute-start.13 = (f32[32,256]{1,0:T(8,128)S(1)}, f32[32,256]{1,0:T(8,128)S(1)}, u32[]{:S(2)}, u32[]{:S(2)}) collective-permute-start(f32[32,256]{1,0:T(8,128)S(1)} %add_add_fusion.refs_8_), channel_id=1, source_target_pairs={{0,16},{4,20},{8,24},{12,28},{16,0},{20,4},{24,8},{28,12},{1,17},{... | collective-permute-start | bytes 98312 | tf_op jit(solution)/shard_map/ppermute | solution.py:323
  51.3 1.3 %copy-start.18 = (bf16[18,2,16,256]{3,2,1,0:T(8,128)(2,1)}, bf16[18,2,16,256]{3,2,1,0:T(8,128)(2,1)S(1)}, u32[]{:S(2)}) copy-start(bf16[18,2,16,256]{3,2,1,0:T(8,128)(2,1)S(1)} %collective-permute-done.9.refs_4_) | copy-start | bytes 884740
  51.3 1.3 %copy-start.19 = (bf16[18,2,16,256]{3,2,1,0:T(8,128)(2,1)}, bf16[18,2,16,256]{3,2,1,0:T(8,128)(2,1)S(1)}, u32[]{:S(2)}) copy-start(bf16[18,2,16,256]{3,2,1,0:T(8,128)(2,1)S(1)} %collective-permute-done.10.refs_7_) | copy-start | bytes 884740
  52.5 0.6 copy-start.20

commit v5 on v4

--- a/solution.py
+++ b/solution.py
@@ -235,7 +235,7 @@
     return pl.ds(at if isinstance(at, int) else pl.multiple_of(at, BLOCK), BLOCK)
 
 
-def first_kernel(mix, first, count, one_hbm, two_hbm, mid_ref, waves_ref, w_ref, side_one_ref, side_upper_ref,
+def first_kernel(mix, first, count, pieces, one_hbm, two_hbm, mid_ref, waves_ref, w_ref, side_one_ref, side_upper_ref,
                  side_lower_ref, side_two_ref, taps_ref, bias_ref, *refs):
     feat_ref, lift_ref, one_ref, two_ref, sems = refs[-5:]
     if first:
@@ -262,12 +262,15 @@
 
     for copy in copies:
         copy.wait()
-    mixed = group_values(first, count, half, taps_ref, w_ref, bias_ref,
-                         lambda b: waves_ref[0, aligned(b)], cycle_ref, feat_ref, lift_ref)
-    value = (0.5 * mixed * (1.0 + lax.erf(mixed * math.sqrt(0.5)))).astype(jnp.bfloat16)
-    for t in range(count):
-        piece = value[t * 4 * BLOCK : (t + 1) * 4 * BLOCK].reshape(4, BLOCK, channels)
-        pay_one_ref[t], pay_two_ref[t] = payloads(piece[:2], piece[2:])
+    start = 0
+    for size in split(count, pieces):
+        mixed = group_values(first + start, size, half, taps_ref, w_ref, bias_ref,
+                             lambda b: waves_ref[0, aligned(b)], cycle_ref, feat_ref, lift_ref)
+        value = (0.5 * mixed * (1.0 + lax.erf(mixed * math.sqrt(0.5)))).astype(jnp.bfloat16)
+        for t in range(size):
+            piece = value[t * 4 * BLOCK : (t + 1) * 4 * BLOCK].reshape(4, BLOCK, channels)
+            pay_one_ref[start + t], pay_two_ref[start + t] = payloads(piece[:2], piece[2:])
+        start += size
 
     size = count * BLOCK
     place = lax.broadcasted_iota(jnp.int32, (size, waves_ref.shape[2]), 0) + first * BLOCK
@@ -285,14 +288,14 @@
 
 
 def second_kernel(mix, groups, *refs):
-    parts = [refs[at : at + 4] for at in range(0, 4 * len(groups), 4)]
-    refs = refs[4 * len(groups) :]
+    parts = [refs[:4], refs[4:8]]
+    refs = refs[8:]
     total_ref, rest_ref, coef_ref, counts_ref, waves_ref, w_ref, taps_ref, bias_ref, out_hbm, *refs = refs
     feat_ref, lift_ref, cycle_ref, *refs = refs
     out_refs, out_sems = refs[:-1], refs[-1]
     channels = w_ref.shape[1]
     cycle_ref[...] = mix(1, total_ref[...] + rest_ref[...], coef_ref, counts_ref, w_ref)
-    place = [(part, at) for part in range(len(groups)) for at in range(parts[part][0].shape[0])]
+    place = [(part, at) for part in range(len(parts)) for at in range(parts[part][0].shape[0])]
 
     def half(start, t):
         part, at = place[start + t]
@@ -317,6 +320,10 @@
 def conv_cost(blocks, channels):
     macs = blocks * BLOCK * 4 * 18 * channels * channels
     return pl.CostEstimate(flops=4 * macs, bytes_accessed=8_000_000, transcendentals=0)
+
+
+def split(count, pieces):
+    return [count * (n + 1) // pieces - count * n // pieces for n in range(pieces)]
 
 
 def swap(value, mask):
@@ -393,9 +400,9 @@
     taps_one, taps_two = tap_matrices(
         (psi_one, psi_two), lon_start, lon_width, ((BLOCK - EDGE, False), (0, True))
     )
-    cut = hid_blocks * 28 // 46
+    cut = hid_blocks * 30 // 46
     hidden = []
-    for first, count in ((0, cut), (cut, hid_blocks - cut)):
+    for first, count, pieces in ((0, cut, 2), (cut, hid_blocks - cut, 1)):
         operands = (row_one, row_two, latent, waves, w_one, side_one, side_upper, side_lower, side_two, taps_one)
         operands += (b_one[None],)
         half = bf16(count, 2, BLOCK, channels)
@@ -410,7 +417,7 @@
             out_shape += (bf16(*mix_shape),)
         own = (min(first + count, out_blocks) - max(first - 1, 0)) * BLOCK
         pay_one, pay_two, harmonics, *made = pl.pallas_call(
-            functools.partial(first_kernel, mix, first, count),
+            functools.partial(first_kernel, mix, first, count, pieces),
             out_shape=out_shape,
             in_specs=in_specs,
             scratch_shapes=scratch(count) + [held(2, own, channels), held(2, own, channels), sems(2)],
@@ -428,7 +435,7 @@
     for got in (hidden[0], hidden[3]):
         total_two += 0.0 * got[0, 0, :1].astype(jnp.float32)
     rest_two = swap(total_two, hops[-1])
-    groups = (cut, out_blocks - cut)
+    groups = split(out_blocks, 3)
     operands = (*hidden, total_two, rest_two, coefs, polar_counts, waves, w_two, taps_two, b_two[None])
     return pl.pallas_call(
         functools.partial(second_kernel, mix, groups),

time: 65 us -> 64.8 us (level)
    ppermute x8, waiting for transfers between devices: 1.15 us -> 2.65 us  [exchange(): lax.ppermute(value, 'lon', pair)]
    ppermute x6, waiting for transfers between devices: 7.33 us -> 5.84 us  [swap(): lax.ppermute(value, 'lat', [(i, i ^ mask) for i in range(lax.axis_size('l...]
  transfers between devices with their start and end apart: 14 -> 14, of which waited for: 5 -> 6; matrix products, arithmetic and copies ran while one was open for 6% -> 6% of each run, Pallas kernels for 9% -> 9%
where the time goes in v5:
time: 64.8 us; the launch traced here: 64.2 us
  Pallas kernels  25.2 us (39%)
  starting transfers between devices  24.2 us (37%)
  waiting for transfers between devices  8.48 us (13%)
  local copies, waits for them, and re-layouts  5.68 us (9%)
    ppermute x8, starting transfers between devices, exchange(): lax.ppermute(value, 'lon', pair)  17 us
    pallas_call x2, Pallas kernels, body(): pl.pallas_call(functools.partial(first_kernel, mix, first, count, pieces)...  11.5 us
    pallas_call x1, Pallas kernels, body(): pl.pallas_call(functools.partial(second_kernel, mix, groups), out_shape=b...  11.3 us
    ppermute x6, starting transfers between devices, swap(): lax.ppermute(value, 'lat', [(i, i ^ mask) for i in range(lax.axis_size('l...  7.2 us
    ppermute x6, waiting for transfers between devices, swap(): lax.ppermute(value, 'lat', [(i, i ^ mask) for i in range(lax.axis_size('l...  5.84 us
    ppermute x8, waiting for transfers between devices, exchange(): lax.ppermute(value, 'lon', pair)  2.65 us
    unnamed x42, local copies, waits for them, and re-layouts  2.01 us
    another operation x2, local copies, waits for them, and re-layouts, body(): jnp.stack([cycle_one, cycle_two])  1.66 us
  transfers between devices with their start and end apart: 14, of which 6 were waited for; matrix products, arithmetic and copies ran while one was open for 6% of the time, Pallas kernels for 9%

profile of v5, /device:TPU:0, one launch (start us, length us, event | category | flops | bytes accessed | tf_op | source)
XLA Modules:
  0.0 64.2 jit_solution(309833362074949894)
XLA Ops:
  0.0 1.4 %copy-done = bf16[4,720,256]{2,1,0:T(8,128)(2,1)S(1)} copy-done((bf16[4,720,256]{2,1,0:T(8,128)(2,1)S(1)}, bf16[4,720,256]{2,1,0:T(8,128)(2,1)}, u32[]{:S(2)}) %copy-start) | copy-done | bytes 1474584
  1.4 0.0 copy-start.2
  1.4 0.0 copy-start.5
  1.4 0.0 copy-start.8
  1.4 1.2 %shard_map.127 = (f32[48,256]{1,0:T(8,128)S(1)}, f32[2,16,256]{2,1,0:T(8,128)S(1)}, bf16[2,720,256]{2,1,0:T(8,128)(2,1)}, bf16[2,720,256]{2,1,0:T(8,128)(2,1)}) custom-call(bf16[4,720,256]{2,1,0:T(8,128)(2,1)S(1)} %copy-done), custom_call_target="tpu_custom_call" | custom-call | flops 1 | bytes 1 | tf_op jit(solution)/shard_map/pallas_call | solution.py:365
  2.6 3.1 %collective-permute-start = (bf16[2,720,256]{2,1,0:T(8,128)(2,1)}, bf16[2,720,256]{2,1,0:T(8,128)(2,1)}, u32[]{:S(2)}, u32[]{:S(2)}) collective-permute-start(bf16[2,720,256]{2,1,0:T(8,128)(2,1)} %get-tuple-element.23), channel_id=1, source_target_pairs={{0,1},{2,3},{1,0},{3,2},{4,5},{6,7},{5,4},{7,6},{8,9},{10,11},{9,8... | collective-permute-start | bytes 2211848 | tf_op jit(solution)/shard_map/ppermute | solution.py:52
  5.7 1.5 %collective-permute-start.1 = (bf16[2,720,256]{2,1,0:T(8,128)(2,1)}, bf16[2,720,256]{2,1,0:T(8,128)(2,1)}, u32[]{:S(2)}, u32[]{:S(2)}) collective-permute-start(bf16[2,720,256]{2,1,0:T(8,128)(2,1)} %get-tuple-element.24), channel_id=1, source_target_pairs={{1,2},{2,1},{5,6},{6,5},{9,10},{10,9},{13,14},{14,13},{17,18},{18,... | collective-permute-start | bytes 2211848 | tf_op jit(solution)/shard_map/ppermute | solution.py:52
  7.2 0.0 collective-permute-start.2
  7.2 1.2 %collective-permute-done.2.got_ref.refs_1_ = f32[48,256]{1,0:T(8,128)S(1)} collective-permute-done((f32[48,256]{1,0:T(8,128)S(1)}, f32[48,256]{1,0:T(8,128)S(1)}, u32[]{:S(2)}, u32[]{:S(2)}) %collective-permute-start.2) | collective-permute-done | bytes 49184 | tf_op jit(solution)/shard_map/ppermute | solution.py:330
  8.5 1.3 %collective-permute-start.3 = (f32[48,256]{1,0:T(8,128)S(1)}, f32[48,256]{1,0:T(8,128)S(1)}, u32[]{:S(2)}, u32[]{:S(2)}) collective-permute-start(f32[48,256]{1,0:T(8,128)S(1)} %shard_map.128.packet_ref), channel_id=1, source_target_pairs={{0,12},{4,8},{8,4},{12,0},{16,28},{20,24},{24,20},{28,16},{1,13},{... | collective-permute-start | bytes 147464 | tf_op jit(solution)/shard_map/ppermute | solution.py:330
  9.8 2.5 %collective-permute-done.3.got_ref.refs_2_ = f32[48,256]{1,0:T(8,128)S(1)} collective-permute-done((f32[48,256]{1,0:T(8,128)S(1)}, f32[48,256]{1,0:T(8,128)S(1)}, u32[]{:S(2)}, u32[]{:S(2)}) %collective-permute-start.3) | collective-permute-done | bytes 49184 | tf_op jit(solution)/shard_map/ppermute | solution.py:330
  12.3 2.7 %collective-permute-start.4 = (f32[48,256]{1,0:T(8,128)S(1)}, f32[48,256]{1,0:T(8,128)S(1)}, u32[]{:S(2)}, u32[]{:S(2)}) collective-permute-start(f32[48,256]{1,0:T(8,128)S(1)} %shard_map.129.refs_0_), channel_id=1, source_target_pairs={{0,28},{4,24},{8,20},{12,16},{16,12},{20,8},{24,4},{28,0},{1,29},{... | collective-permute-start | bytes 147464 | tf_op jit(solution)/shard_map/ppermute | solution.py:330
  14.9 1.0 %dynamic-slice_bitcast_fusion.waves_ref.refs_12_ = bf16[2,736,128]{2,1,0:T(8,128)(2,1)S(1)} fusion(bf16[8,2,736,128]{3,2,1,0:T(8,128)(2,1)} %constant.19.clone, s32[]{:T(128)S(6)} %select_n.4), kind=kLoop, calls=%fused_computation | loop fusion | bytes 753668 | tf_op jit(solution)/shard_map/jit(dynamic_index_in_dim)/squeeze | solution.py:357
  15.9 0.0 copy-start.3
  16.0 0.8 %copy.20 = f32[1,4,9,8]{3,2,1,0:T(8,128)S(1)} copy(f32[1,4,9,8]{2,3,1,0:T(8,128)} %bitcast.14) | data formatting | bytes 2304 | tf_op jit(solution)/shard_map/stack | solution.py:394
  16.8 0.8 %copy.21 = f32[1,4,9,8]{3,2,1,0:T(8,128)S(1)} copy(f32[1,4,9,8]{2,3,1,0:T(8,128)} %bitcast.15) | data formatting | bytes 2304 | tf_op jit(solution)/shard_map/stack | solution.py:394
  17.6 0.0 collective-permute-done.4.refs_3_
  17.7 3.7 %collective-permute-start.5 = (bf16[2,2,16,256]{3,2,1,0:T(8,128)(2,1)S(1)}, bf16[2,2,16,256]{3,2,1,0:T(8,128)(2,1)S(1)}, u32[]{:S(2)}, u32[]{:S(2)}) collective-permute-start(bf16[2,2,16,256]{3,2,1,0:T(8,128)(2,1)S(1)} %get-tuple-element.27), channel_id=1, source_target_pairs={{0,1},{2,3},{1,0},{3,2},{4,5},{6,7},{5,4},{7,6},{8,9},{10,11},{9,8... | collective-permute-start | bytes 98312 | tf_op jit(solution)/shard_map/ppermute | solution.py:52
  21.3 0.7 %collective-permute-start.6 = (bf16[2,2,16,256]{3,2,1,0:T(8,128)(2,1)S(1)}, bf16[2,2,16,256]{3,2,1,0:T(8,128)(2,1)S(1)}, u32[]{:S(2)}, u32[]{:S(2)}) collective-permute-start(bf16[2,2,16,256]{3,2,1,0:T(8,128)(2,1)S(1)} %get-tuple-element.30), channel_id=1, source_target_pairs={{1,2},{2,1},{5,6},{6,5},{9,10},{10,9},{13,14},{14,13},{17,18},{18,... | collective-permute-start | bytes 98312 | tf_op jit(solution)/shard_map/ppermute | solution.py:52
  22.0 0.0 copy-start.4
  22.0 0.1 copy.18
  22.1 0.9 %copy.19 = bf16[4,9,25]{2,1,0:T(8,128)(2,1)S(1)} copy(bf16[4,9,25]{1,0,2:T(4,128)(2,1)} %bitcast.13) | data formatting | bytes 3600 | tf_op jit(solution)/shard_map/reshape | solution.py:109
  23.0 1.3 %shard_map.131 = (bf16[576,256]{1,0:T(8,128)(2,1)S(1)}, bf16[576,256]{1,0:T(8,128)(2,1)S(1)}) custom-call(bf16[4,16,32]{2,1,0:T(8,128)(2,1)S(1)} %pad.7.refs_0_, bf16[4,16,32]{2,1,0:T(8,128)(2,1)S(1)} %pad.8.refs_1_, s32[16]{0:T(128)S(1)} %copy-done.6, s32[16]{0:T(128)S(1)} %copy-done.7), custom_call_target="tpu_custom_call" | custom-call | flops 1 | bytes 1 | tf_op jit(solution)/shard_map/pallas_call | solution.py:112
  24.3 0.0 copy-start.11
  24.3 0.0 collective-permute-done.5.side_one_ref
  24.3 0.0 collective-permute-done.6.side_two_ref
  24.4 0.0 collective-permute-done.one_hbm
  24.4 0.0 collective-permute-done.1.two_hbm
  24.4 7.3 %shard_map.132 = (bf16[30,2,16,256]{3,2,1,0:T(8,128)(2,1)S(1)}, bf16[30,2,16,256]{3,2,1,0:T(8,128)(2,1)S(1)}, f32[32,256]{1,0:T(8,128)S(1)}, bf16[128,256]{1,0:T(8,128)(2,1)S(1)}) custom-call(bf16[2,720,256]{2,1,0:T(8,128)(2,1)} %collective-permute-done.one_hbm, bf16[2,720,256]{2,1,0:T(8,128)(2,1)} %collective-permute-done.1.two_hbm, ...), custom_call_target="tpu_custom_call" | custom-call | flops 1 | bytes 1 | tf_op jit(solution)/shard_map/pallas_call | solution.py:419
  31.8 3.5 %collective-permute-start.7 = (bf16[30,2,16,256]{3,2,1,0:T(8,128)(2,1)S(1)}, bf16[30,2,16,256]{3,2,1,0:T(8,128)(2,1)S(1)}, u32[]{:S(2)}, u32[]{:S(2)}) collective-permute-start(bf16[30,2,16,256]{3,2,1,0:T(8,128)(2,1)S(1)} %get-tuple-element.33.refs_1_), channel_id=1, source_target_pairs={{0,1},{2,3},{1,0},{3,2},{4,5},{6,7},{5,4},{7,6},{8,9},{10,11},{9,8... | collective-permute-start | bytes 1474568 | tf_op jit(solution)/shard_map/ppermute | solution.py:52
  35.3 0.7 %collective-permute-start.8 = (bf16[30,2,16,256]{3,2,1,0:T(8,128)(2,1)S(1)}, bf16[30,2,16,256]{3,2,1,0:T(8,128)(2,1)S(1)}, u32[]{:S(2)}, u32[]{:S(2)}) collective-permute-start(bf16[30,2,16,256]{3,2,1,0:T(8,128)(2,1)S(1)} %get-tuple-element.34.refs_2_), channel_id=1, source_target_pairs={{1,2},{2,1},{5,6},{6,5},{9,10},{10,9},{13,14},{14,13},{17,18},{18,... | collective-permute-start | bytes 1474568 | tf_op jit(solution)/shard_map/ppermute | solution.py:52
  36.0 0.0 copy-done.3
  36.0 4.2 %shard_map.133 = (bf16[16,2,16,256]{3,2,1,0:T(8,128)(2,1)S(1)}, bf16[16,2,16,256]{3,2,1,0:T(8,128)(2,1)S(1)}, f32[32,256]{1,0:T(8,128)S(1)}) custom-call(bf16[2,720,256]{2,1,0:T(8,128)(2,1)} %collective-permute-done.one_hbm, bf16[2,720,256]{2,1,0:T(8,128)(2,1)} %collective-permute-done.1.two_hbm, bf16[4,720,256]{2,1,0:T(8,128)(2,1)S(1)} %copy-done.1, ...), custom_call_target="tpu_custom_call" | custom-call | flops 1 | bytes 1 | tf_op jit(solution)/shard_map/pallas_call | solution.py:419
  40.2 0.1 collective-permute-start.11
  40.3 3.0 %collective-permute-start.9 = (bf16[16,2,16,256]{3,2,1,0:T(8,128)(2,1)S(1)}, bf16[16,2,16,256]{3,2,1,0:T(8,128)(2,1)S(1)}, u32[]{:S(2)}, u32[]{:S(2)}) collective-permute-start(bf16[16,2,16,256]{3,2,1,0:T(8,128)(2,1)S(1)} %get-tuple-element.37.refs_5_), channel_id=1, source_target_pairs={{0,1},{2,3},{1,0},{3,2},{4,5},{6,7},{5,4},{7,6},{8,9},{10,11},{9,8... | collective-permute-start | bytes 786440 | tf_op jit(solution)/shard_map/ppermute | solution.py:52
  43.3 0.8 %collective-permute-start.10 = (bf16[16,2,16,256]{3,2,1,0:T(8,128)(2,1)S(1)}, bf16[16,2,16,256]{3,2,1,0:T(8,128)(2,1)S(1)}, u32[]{:S(2)}, u32[]{:S(2)}) collective-permute-start(bf16[16,2,16,256]{3,2,1,0:T(8,128)(2,1)S(1)} %get-tuple-element.38.refs_6_), channel_id=1, source_target_pairs={{1,2},{2,1},{5,6},{6,5},{9,10},{10,9},{13,14},{14,13},{17,18},{18,... | collective-permute-start | bytes 786440 | tf_op jit(solution)/shard_map/ppermute | solution.py:52
  44.2 0.0 collective-permute-done.11
  44.2 1.6 %collective-permute-start.12 = (f32[32,256]{1,0:T(8,128)S(1)}, f32[32,256]{1,0:T(8,128)S(1)}, u32[]{:S(2)}, u32[]{:S(2)}) collective-permute-start(f32[32,256]{1,0:T(8,128)S(1)} %add.31), channel_id=1, source_target_pairs={{0,8},{4,12},{8,0},{12,4},{16,24},{20,28},{24,16},{28,20},{1,9},{5... | collective-permute-start | bytes 98312 | tf_op jit(solution)/shard_map/ppermute | solution.py:330
  45.8 1.1 %collective-permute-done.7.refs_0_ = bf16[30,2,16,256]{3,2,1,0:T(8,128)(2,1)S(1)} collective-permute-done((bf16[30,2,16,256]{3,2,1,0:T(8,128)(2,1)S(1)}, bf16[30,2,16,256]{3,2,1,0:T(8,128)(2,1)S(1)}, u32[]{:S(2)}, u32[]{:S(2)}) %collective-permute-start.7) | collective-permute-done | bytes 491552 | tf_op jit(solution)/shard_map/ppermute | solution.py:52
  46.8 0.0 collective-permute-done.8.refs_3_
  46.9 1.3 %collective-permute-done.12 = f32[32,256]{1,0:T(8,128)S(1)} collective-permute-done((f32[32,256]{1,0:T(8,128)S(1)}, f32[32,256]{1,0:T(8,128)S(1)}, u32[]{:S(2)}, u32[]{:S(2)}) %collective-permute-start.12) | collective-permute-done | bytes 32800 | tf_op jit(solution)/shard_map/ppermute | solution.py:330
  48.2 1.6 %collective-permute-start.13 = (f32[32,256]{1,0:T(8,128)S(1)}, f32[32,256]{1,0:T(8,128)S(1)}, u32[]{:S(2)}, u32[]{:S(2)}) collective-permute-start(f32[32,256]{1,0:T(8,128)S(1)} %add_add_fusion.refs_8_), channel_id=1, source_target_pairs={{0,16},{4,20},{8,24},{12,28},{16,0},{20,4},{24,8},{28,12},{1,17},{... | collective-permute-start | bytes 98312 | tf_op jit(solution)/shard_map/ppermute | solution.py:330
  49.8 1.6 %collective-permute-done.9.refs_4_ = bf16[16,2,16,256]{3,2,1,0:T(8,128)(2,1)S(1)} collective-permute-done((bf16[16,2,16,256]{3,2,1,0:T(8,128)(2,1)S(1)}, bf16[16,2,16,256]{3,2,1,0:T(8,128)(2,1)S(1)}, u32[]{:S(2)}, u32[]{:S(2)}) %collective-permute-start.9) | collective-permute-done | bytes 262176 | tf_op jit(solution)/shard_map/ppermute | solution.py:52
  51.4 0.0 collective-permute-done.10.refs_7_
  51.4 0.8 %collective-permute-done.13.refs_9_ = f32[32,256]{1,0:T(8,128)S(1)} collective-permute-done((f32[32,256]{1,0:T(8,128)S(1)}, f32[32,256]{1,0:T(8,128)S(1)}, u32[]{:S(2)}, u32[]{:S(2)}) %collective-permute-start.13) | collective-permute-done | bytes 32800 | tf_op jit(solution)/shard_map/ppermute | solution.py:330
  52.2 0.0 copy-done.12
  52.3 0.6 copy-done.20
  52.8 11.3 %shard_map.134 = bf16[4,720,256]{2,1,0:T(8,128)(2,1)} custom-call(bf16[30,2,16,256]{3,2,1,0:T(8,128)(2,1)} %copy-done.16, bf16[30,2,16,256]{3,2,1,0:T(8,128)(2,1)} %copy-done.9, bf16[30,2,16,256]{3,2,1,0:T(8,128)(2,1)} %copy-done.10, bf16[30,2,16,256]{3,2,1,0:T(8,128)(2,1)} %copy-done.17, bf16[16,2,16,256]{3,2,1,0:T(8,128)(2,1)} %copy-done.18, ...), custom_call_target="tpu_custom_call" | custom-call | flops 13589544960 | bytes 8000000 | tf_op jit(solution)/shard_map/pallas_call | solution.py:440
  (42 shorter events, 0.2 us)
Async XLA Ops:
  0.0 1.4 %copy-start = (bf16[4,720,256]{2,1,0:T(8,128)(2,1)S(1)}, bf16[4,720,256]{2,1,0:T(8,128)(2,1)}, u32[]{:S(2)}) copy-start(bf16[4,720,256]{2,1,0:T(8,128)(2,1)} %mid_ref.3) | copy-start | bytes 4423684
  1.4 20.6 %copy-start.15 = (bf16[4,9,5,5]{1,0,3,2:T(4,128)(2,1)S(1)}, bf16[4,9,5,5]{1,0,3,2:T(4,128)(2,1)}, u32[]{:S(2)}) copy-start(bf16[4,9,5,5]{1,0,3,2:T(4,128)(2,1)} %param.14) | copy-start | bytes 5404
  1.4 21.6 %copy-start.6 = (s32[16]{0:T(128)S(1)}, s32[16]{0:T(128)}, u32[]{:S(2)}) copy-start(s32[16]{0:T(128)} %refs_2_.2) | copy-start | bytes 196
  1.4 21.7 %copy-start.7 = (s32[16]{0:T(128)S(1)}, s32[16]{0:T(128)}, u32[]{:S(2)}) copy-start(s32[16]{0:T(128)} %refs_3_.1) | copy-start | bytes 196
  1.4 23.0 %copy-start.1 = (bf16[4,720,256]{2,1,0:T(8,128)(2,1)S(1)}, bf16[4,720,256]{2,1,0:T(8,128)(2,1)}, u32[]{:S(2)}) copy-start(bf16[4,720,256]{2,1,0:T(8,128)(2,1)} %mid_ref.3) | copy-start | bytes 4423684
  1.4 23.0 %copy-start.2 = (bf16[2304,256]{1,0:T(8,128)(2,1)S(1)}, bf16[2304,256]{1,0:T(8,128)(2,1)}, u32[]{:S(2)}) copy-start(bf16[2304,256]{1,0:T(8,128)(2,1)} %w_ref.3) | copy-start | bytes 3538948
  1.4 23.0 %copy-start.5 = (f32[256]{0:T(256)S(1)}, f32[256]{0:T(256)}, u32[]{:S(2)}) copy-start(f32[256]{0:T(256)} %param.20) | copy-start | bytes 3076
  1.4 23.0 %copy-start.8 = (s32[2]{0:T(128)S(1)}, s32[2]{0:T(128)}, u32[]{:S(2)}) copy-start(s32[2]{0:T(128)} %refs_11_.1) | copy-start | bytes 28
  2.6 21.8 %collective-permute-start = (bf16[2,720,256]{2,1,0:T(8,128)(2,1)}, bf16[2,720,256]{2,1,0:T(8,128)(2,1)}, u32[]{:S(2)}, u32[]{:S(2)}) collective-permute-start(bf16[2,720,256]{2,1,0:T(8,128)(2,1)} %get-tuple-element.23), channel_id=1, source_target_pairs={{0,1},{2,3},{1,0},{3,2},{4,5},{6,7},{5,4},{7,6},{8,9},{10,11},{9,8... | collective-permute-start | bytes 2211848 | tf_op jit(solution)/shard_map/ppermute | solution.py:52
  5.7 18.7 %collective-permute-start.1 = (bf16[2,720,256]{2,1,0:T(8,128)(2,1)}, bf16[2,720,256]{2,1,0:T(8,128)(2,1)}, u32[]{:S(2)}, u32[]{:S(2)}) collective-permute-start(bf16[2,720,256]{2,1,0:T(8,128)(2,1)} %get-tuple-element.24), channel_id=1, source_target_pairs={{1,2},{2,1},{5,6},{6,5},{9,10},{10,9},{13,14},{14,13},{17,18},{18,... | collective-permute-start | bytes 2211848 | tf_op jit(solution)/shard_map/ppermute | solution.py:52
  7.2 1.2 %collective-permute-start.2 = (f32[48,256]{1,0:T(8,128)S(1)}, f32[48,256]{1,0:T(8,128)S(1)}, u32[]{:S(2)}, u32[]{:S(2)}) collective-permute-start(f32[48,256]{1,0:T(8,128)S(1)} %get-tuple-element.25.packet_ref), channel_id=1, source_target_pairs={{0,4},{4,0},{8,12},{12,8},{16,20},{20,16},{24,28},{28,24},{1,5},{5... | collective-permute-start | bytes 147464 | tf_op jit(solution)/shard_map/ppermute | solution.py:330
  8.5 3.8 %collective-permute-start.3 = (f32[48,256]{1,0:T(8,128)S(1)}, f32[48,256]{1,0:T(8,128)S(1)}, u32[]{:S(2)}, u32[]{:S(2)}) collective-permute-start(f32[48,256]{1,0:T(8,128)S(1)} %shard_map.128.packet_ref), channel_id=1, source_target_pairs={{0,12},{4,8},{8,4},{12,0},{16,28},{20,24},{24,20},{28,16},{1,13},{... | collective-permute-start | bytes 147464 | tf_op jit(solution)/shard_map/ppermute | solution.py:330
  12.3 5.4 %collective-permute-start.4 = (f32[48,256]{1,0:T(8,128)S(1)}, f32[48,256]{1,0:T(8,128)S(1)}, u32[]{:S(2)}, u32[]{:S(2)}) collective-permute-start(f32[48,256]{1,0:T(8,128)S(1)} %shard_map.129.refs_0_), channel_id=1, source_target_pairs={{0,28},{4,24},{8,20},{12,16},{16,12},{20,8},{24,4},{28,0},{1,29},{... | collective-permute-start | bytes 147464 | tf_op jit(solution)/shard_map/ppermute | solution.py:330
  15.9 20.1 %copy-start.3 = (bf16[2,736,128]{2,1,0:T(8,128)(2,1)}, bf16[2,736,128]{2,1,0:T(8,128)(2,1)S(1)}, u32[]{:S(2)}) copy-start(bf16[2,736,128]{2,1,0:T(8,128)(2,1)S(1)} %dynamic-slice_bitcast_fusion.waves_ref.refs_12_) | copy-start | bytes 1130500
  17.7 6.7 %collective-permute-start.5 = (bf16[2,2,16,256]{3,2,1,0:T(8,128)(2,1)S(1)}, bf16[2,2,16,256]{3,2,1,0:T(8,128)(2,1)S(1)}, u32[]{:S(2)}, u32[]{:S(2)}) collective-permute-start(bf16[2,2,16,256]{3,2,1,0:T(8,128)(2,1)S(1)} %get-tuple-element.27), channel_id=1, source_target_pairs={{0,1},{2,3},{1,0},{3,2},{4,5},{6,7},{5,4},{7,6},{8,9},{10,11},{9,8... | collective-permute-start | bytes 98312 | tf_op jit(solution)/shard_map/ppermute | solution.py:52
  21.3 3.0 %collective-permute-start.6 = (bf16[2,2,16,256]{3,2,1,0:T(8,128)(2,1)S(1)}, bf16[2,2,16,256]{3,2,1,0:T(8,128)(2,1)S(1)}, u32[]{:S(2)}, u32[]{:S(2)}) collective-permute-start(bf16[2,2,16,256]{3,2,1,0:T(8,128)(2,1)S(1)} %get-tuple-element.30), channel_id=1, source_target_pairs={{1,2},{2,1},{5,6},{6,5},{9,10},{10,9},{13,14},{14,13},{17,18},{18,... | collective-permute-start | bytes 98312 | tf_op jit(solution)/shard_map/ppermute | solution.py:52
  22.0 9.7 %copy-start.4 = (f32[2,4,9,8]{3,2,1,0:T(8,128)}, f32[2,4,9,8]{3,2,1,0:T(8,128)S(1)}, u32[]{:S(2)}) copy-start(f32[2,4,9,8]{3,2,1,0:T(8,128)S(1)} %pad_maximum_fusion.refs_1_.refs_10_) | copy-start | bytes 6916
  24.3 7.4 %copy-start.11 = (bf16[576,256]{1,0:T(8,128)(2,1)}, bf16[576,256]{1,0:T(8,128)(2,1)S(1)}, u32[]{:S(2)}) copy-start(bf16[576,256]{1,0:T(8,128)(2,1)S(1)} %get-tuple-element.40.refs_14_) | copy-start | bytes 884740
  31.7 8.4 %copy-start.9 = (bf16[30,2,16,256]{3,2,1,0:T(8,128)(2,1)}, bf16[30,2,16,256]{3,2,1,0:T(8,128)(2,1)S(1)}, u32[]{:S(2)}) copy-start(bf16[30,2,16,256]{3,2,1,0:T(8,128)(2,1)S(1)} %get-tuple-element.33.refs_1_) | copy-start | bytes 1474564
  31.8 8.4 %copy-start.10 = (bf16[30,2,16,256]{3,2,1,0:T(8,128)(2,1)}, bf16[30,2,16,256]{3,2,1,0:T(8,128)(2,1)S(1)}, u32[]{:S(2)}) copy-start(bf16[30,2,16,256]{3,2,1,0:T(8,128)(2,1)S(1)} %get-tuple-element.34.refs_2_) | copy-start | bytes 1474564
  31.8 15.1 %collective-permute-start.7 = (bf16[30,2,16,256]{3,2,1,0:T(8,128)(2,1)S(1)}, bf16[30,2,16,256]{3,2,1,0:T(8,128)(2,1)S(1)}, u32[]{:S(2)}, u32[]{:S(2)}) collective-permute-start(bf16[30,2,16,256]{3,2,1,0:T(8,128)(2,1)S(1)} %get-tuple-element.33.refs_1_), channel_id=1, source_target_pairs={{0,1},{2,3},{1,0},{3,2},{4,5},{6,7},{5,4},{7,6},{8,9},{10,11},{9,8... | collective-permute-start | bytes 1474568 | tf_op jit(solution)/shard_map/ppermute | solution.py:52
  35.3 11.5 %collective-permute-start.8 = (bf16[30,2,16,256]{3,2,1,0:T(8,128)(2,1)S(1)}, bf16[30,2,16,256]{3,2,1,0:T(8,128)(2,1)S(1)}, u32[]{:S(2)}, u32[]{:S(2)}) collective-permute-start(bf16[30,2,16,256]{3,2,1,0:T(8,128)(2,1)S(1)} %get-tuple-element.34.refs_2_), channel_id=1, source_target_pairs={{1,2},{2,1},{5,6},{6,5},{9,10},{10,9},{13,14},{14,13},{17,18},{18,... | collective-permute-start | bytes 1474568 | tf_op jit(solution)/shard_map/ppermute | solution.py:52
  40.2 12.0 %copy-start.12 = (bf16[16,2,16,256]{3,2,1,0:T(8,128)(2,1)}, bf16[16,2,16,256]{3,2,1,0:T(8,128)(2,1)S(1)}, u32[]{:S(2)}) copy-start(bf16[16,2,16,256]{3,2,1,0:T(8,128)(2,1)S(1)} %get-tuple-element.37.refs_5_) | copy-start | bytes 786436
  40.2 12.0 %copy-start.13 = (bf16[16,2,16,256]{3,2,1,0:T(8,128)(2,1)}, bf16[16,2,16,256]{3,2,1,0:T(8,128)(2,1)S(1)}, u32[]{:S(2)}) copy-start(bf16[16,2,16,256]{3,2,1,0:T(8,128)(2,1)S(1)} %get-tuple-element.38.refs_6_) | copy-start | bytes 786436
  40.2 4.0 %collective-permute-start.11 = (f32[32,256]{1,0:T(8,128)S(1)}, f32[32,256]{1,0:T(8,128)S(1)}, u32[]{:S(2)}, u32[]{:S(2)}) collective-permute-start(f32[32,256]{1,0:T(8,128)S(1)} %get-tuple-element.39), channel_id=1, source_target_pairs={{0,4},{4,0},{8,12},{12,8},{16,20},{20,16},{24,28},{28,24},{1,5},{5... | collective-permute-start | bytes 98312 | tf_op jit(solution)/shard_map/ppermute | solution.py:330
  40.3 11.1 %collective-permute-start.9 = (bf16[16,2,16,256]{3,2,1,0:T(8,128)(2,1)S(1)}, bf16[16,2,16,256]{3,2,1,0:T(8,128)(2,1)S(1)}, u32[]{:S(2)}, u32[]{:S(2)}) collective-permute-start(bf16[16,2,16,256]{3,2,1,0:T(8,128)(2,1)S(1)} %get-tuple-element.37.refs_5_), channel_id=1, source_target_pairs={{0,1},{2,3},{1,0},{3,2},{4,5},{6,7},{5,4},{7,6},{8,9},{10,11},{9,8... | collective-permute-start | bytes 786440 | tf_op jit(solution)/shard_map/ppermute | solution.py:52
  43.3 8.0 %collective-permute-start.10 = (bf16[16,2,16,256]{3,2,1,0:T(8,128)(2,1)S(1)}, bf16[16,2,16,256]{3,2,1,0:T(8,128)(2,1)S(1)}, u32[]{:S(2)}, u32[]{:S(2)}) collective-permute-start(bf16[16,2,16,256]{3,2,1,0:T(8,128)(2,1)S(1)} %get-tuple-element.38.refs_6_), channel_id=1, source_target_pairs={{1,2},{2,1},{5,6},{6,5},{9,10},{10,9},{13,14},{14,13},{17,18},{18,... | collective-permute-start | bytes 786440 | tf_op jit(solution)/shard_map/ppermute | solution.py:52
  44.2 4.0 %collective-permute-start.12 = (f32[32,256]{1,0:T(8,128)S(1)}, f32[32,256]{1,0:T(8,128)S(1)}, u32[]{:S(2)}, u32[]{:S(2)}) collective-permute-start(f32[32,256]{1,0:T(8,128)S(1)} %add.31), channel_id=1, source_target_pairs={{0,8},{4,12},{8,0},{12,4},{16,24},{20,28},{24,16},{28,20},{1,9},{5... | collective-permute-start | bytes 98312 | tf_op jit(solution)/shard_map/ppermute | solution.py:330
  46.8 5.4 %copy-start.16 = (bf16[30,2,16,256]{3,2,1,0:T(8,128)(2,1)}, bf16[30,2,16,256]{3,2,1,0:T(8,128)(2,1)S(1)}, u32[]{:S(2)}) copy-start(bf16[30,2,16,256]{3,2,1,0:T(8,128)(2,1)S(1)} %collective-permute-done.7.refs_0_) | copy-start | bytes 1474564
  46.8 5.4 %copy-start.17 = (bf16[30,2,16,256]{3,2,1,0:T(8,128)(2,1)}, bf16[30,2,16,256]{3,2,1,0:T(8,128)(2,1)S(1)}, u32[]{:S(2)}) copy-start(bf16[30,2,16,256]{3,2,1,0:T(8,128)(2,1)S(1)} %collective-permute-done.8.refs_3_) | copy-start | bytes 1474564
  48.2 4.0 %copy-start.14 = (f32[32,256]{1,0:T(8,128)}, f32[32,256]{1,0:T(8,128)S(1)}, u32[]{:S(2)}) copy-start(f32[32,256]{1,0:T(8,128)S(1)} %add_add_fusion.refs_8_) | copy-start | bytes 98308
  48.2 4.0 %collective-permute-start.13 = (f32[32,256]{1,0:T(8,128)S(1)}, f32[32,256]{1,0:T(8,128)S(1)}, u32[]{:S(2)}, u32[]{:S(2)}) collective-permute-start(f32[32,256]{1,0:T(8,128)S(1)} %add_add_fusion.refs_8_), channel_id=1, source_target_pairs={{0,16},{4,20},{8,24},{12,28},{16,0},{20,4},{24,8},{28,12},{1,17},{... | collective-permute-start | bytes 98312 | tf_op jit(solution)/shard_map/ppermute | solution.py:330
  51.4 0.9 %copy-start.18 = (bf16[16,2,16,256]{3,2,1,0:T(8,128)(2,1)}, bf16[16,2,16,256]{3,2,1,0:T(8,128)(2,1)S(1)}, u32[]{:S(2)}) copy-start(bf16[16,2,16,256]{3,2,1,0:T(8,128)(2,1)S(1)} %collective-permute-done.9.refs_4_) | copy-start | bytes 786436
  51.4 0.9 %copy-start.19 = (bf16[16,2,16,256]{3,2,1,0:T(8,128)(2,1)}, bf16[16,2,16,256]{3,2,1,0:T(8,128)(2,1)S(1)}, u32[]{:S(2)}) copy-start(bf16[16,2,16,256]{3,2,1,0:T(8,128)(2,1)S(1)} %collective-permute-done.10.refs_7_) | copy-start | bytes 786436
  52.2 0.6 copy-start.20
